TPU v7x, 256 devices: a whole 4x4x8 slice. The times are simulated.
256 devices in a mesh: section: 2 (over core), tensor: 32 (over z, y), dp: 4 (over x).
Axes of the slice: x: 4, y: 4, z: 8, core: 2. Of those that a mesh axis runs over, the one named last changes fastest.
Arguments:
- hidden: bfloat16 [1024, 4096], P(('section', 'dp'), 'tensor'), may hold values from -500 to 500
- norm_gain: float32 [4096], P('tensor'), may hold values from 0.5 to 1.5
- head_weight: bfloat16 [131072, 4096], P(('section', 'tensor', 'dp')), may hold values from -1 to 1
- targets: int32 [1024], P(('section', 'dp')), may hold values from 0 to 131071
- span_starts: int32 [1024], P(('section', 'dp')), may hold values from 0 to 1
- live_rows: int32 [1024], P(('section', 'dp')), may hold values from 0 to 1, as said below
Outputs:
- hidden_grad: bfloat16 [1024, 4096], P(('section', 'dp'), 'tensor')
- gain_grad: float32 [4096], P('tensor')
- weight_grad: bfloat16 [131072, 4096], P(('section', 'tensor', 'dp'))
- mean_loss: float32 [], replicated
Inputs may be any that keep to these rules, and one draw needn't show every extreme that they name: `live_rows`: in the rows of one device the live rows come first; each device has 1 to 112 of them, and some device exactly 112.
All inputs are finite; a program needn't handle non-finite values.
Results may differ from a plain program's by a relative error of at most 0.0077.
Values may be sent and summed in bfloat16 or wider, within the bound.
No kernel may reach another device: no remote copies, remote signals or barrier semaphores. Data moves between devices by JAX's collectives and lax.ppermute only.
A program may use at most 128 MiB of HBM per device.

v0:
```python
import functools
import jax
import jax.numpy as jnp
from jax import lax
from jax.experimental import pallas as pl
from jax.experimental.pallas import tpu as pltpu
from jax.sharding import Mesh, PartitionSpec as P

NSENT = 100
LIVE = 112
loss_scale = 8192.0
epsilon = 1e-06
f32, bf16 = jnp.float32, jnp.bfloat16
VMEM = pl.BlockSpec(memory_space=pltpu.VMEM)
SMEM = pl.BlockSpec(memory_space=pltpu.SMEM)
HBM = pl.BlockSpec(memory_space=pltpu.HBM)
R = 4
ORDER = (0, 1, 3, 2)
SCOPED = 16 << 20


def shift(x, axis, k):
    n = lax.axis_size(axis)
    return lax.ppermute(x, axis, [(i, (i + k) % n) for i in range(n)])


def ring_gather(block, axis):
    half = block.shape[0] // 2
    one, three = shift(block, axis, 1), shift(block, axis, -1)
    two = shift(one[:half], axis, 1), shift(three[half:], axis, -1)
    return block, one, three, *two


def pick(refs, outer, inner, z, Zh):
    if outer == 2:
        ref = refs[3 + inner // 2]
        inner = inner % 2
    else:
        ref = refs[(0, 1, None, 2)[outer]]
    at = pl.multiple_of((inner * Zh + z) * LIVE, 16)
    return ref[pl.ds(at, LIVE), :].astype(f32)


def same():
    return lax.broadcasted_iota(jnp.int32, (LIVE, 128), 0) == lax.broadcasted_iota(
        jnp.int32, (LIVE, 128), 1
    )


def to_row(column):
    return jnp.sum(jnp.where(same(), column, 0.0), axis=0, keepdims=True)


def to_column(row):
    return jnp.sum(jnp.where(same(), row, 0.0), axis=1, keepdims=True)


def place_of(x, p):
    return lax.rem(x - ORDER[p] + R, R)


def forward_kernel(Zh, place_ref, w0_ref, w1_ref, *refs):
    gains, a_refs, b_refs = refs[:R], refs[R : R + 5], refs[R + 5 : R + 10]
    n_ref, inv_ref, l_ref, share_ref, w_ref, w_sems = refs[R + 10 :]
    Z = 2 * Zh
    V = w0_ref.shape[0]
    tile = 2 * V // 2
    copies = [
        pltpu.make_async_copy(w, w_ref.at[i], w_sems.at[i]) for i, w in enumerate((w0_ref, w1_ref))
    ]
    for copy in copies:
        copy.start()
    for p, j in enumerate(ORDER):
        rows = slice(p * LIVE, (p + 1) * LIVE)

        def square(z, total):
            for k in range(R):
                for refs, outer, at in ((a_refs, j, k), (b_refs, k, j)):
                    block = pick(refs, outer, at, z, Zh)
                    total = total + block * block
            return total

        total = lax.fori_loop(0, Zh, square, jnp.zeros((LIVE, 128), f32))
        mean_square = jnp.sum(total, axis=1, keepdims=True) / (Z * R * 128)
        inv = lax.rsqrt(mean_square + epsilon)
        if j == 0:
            inv_ref[...] = inv
        wide = jnp.broadcast_to(inv, (LIVE, 128))

        def scale(z, _):
            for k in range(R):
                y = lax.rem(place_ref[0] - k + R, R)
                for half, refs, outer, at in ((0, a_refs, j, k), (1, b_refs, k, j)):
                    t = half * Zh + z
                    line = pl.multiple_of(Zh * LIVE + t * 16, 16)
                    pieces = gains[k][pl.ds(line, 16), :].astype(f32)
                    gain = pieces[0:1] + pieces[1:2] + pieces[2:3]
                    column = pl.multiple_of((t * R + y) * 128, 128)
                    n_ref[rows, pl.ds(column, 128)] = (
                        pick(refs, outer, at, z, Zh) * wide * gain
                    ).astype(bf16)
            return 0

        lax.fori_loop(0, Zh, scale, 0)

    def logits_of(q, _):
        pltpu.make_async_copy(w0_ref, w_ref.at[q], w_sems.at[q]).wait()
        l_ref[:, pl.ds(pl.multiple_of(q * tile, tile), tile)] = lax.dot_general(
            n_ref[...], w_ref[q], (((1,), (1,)), ((), ())), preferred_element_type=f32
        )
        return 0

    lax.fori_loop(0, 2, logits_of, 0)
    place = lax.broadcasted_iota(jnp.int32, (R, 128), 0)
    share = jnp.zeros((R, 128), f32)
    for p in range(R):
        logits = l_ref[p * LIVE : (p + 1) * LIVE, :]
        top = jnp.max(logits, axis=1, keepdims=True)
        here = top + jnp.log(jnp.sum(jnp.exp(logits - top), axis=1, keepdims=True))
        share = jnp.where(place == place_of(place_ref[1], p), to_row(here), share)
    share_ref[...] = jnp.broadcast_to(share[None], share_ref.shape)


def forward(place, Zh, w0, w1, gains, a, b):
    V, D = w0.shape
    rows = R * LIVE
    return pl.pallas_call(
        functools.partial(forward_kernel, Zh),
        out_shape=(
            jax.ShapeDtypeStruct((rows, D), bf16),
            jax.ShapeDtypeStruct((LIVE, 1), f32),
            jax.ShapeDtypeStruct((rows, 2 * V), f32),
            jax.ShapeDtypeStruct((2 * Zh * R * R, R, 128), f32),
        ),
        in_specs=[SMEM, HBM, HBM] + [VMEM] * (R + 10),
        out_specs=(VMEM,) * 4,
        scratch_shapes=[
            pltpu.VMEM((2, V, D), bf16),
            pltpu.SemaphoreType.DMA((2,)),
        ],
        compiler_params=pltpu.CompilerParams(vmem_limit_bytes=28 << 20),
        cost_estimate=pl.CostEstimate(
            flops=4 * rows * V * D, bytes_accessed=4 * V * D, transcendentals=2 * rows * V
        ),
        name="forward",
    )(place, w0, w1, *gains, *a, *b)


def split_tile(rows):
    place = lax.broadcasted_iota(jnp.int32, (16, 128), 0)
    tile = jnp.zeros((16, 128), f32)
    for i, row in enumerate(rows):
        for n in range(3):
            piece = row.astype(bf16).astype(f32)
            tile = jnp.where(place == 3 * i + n, piece, tile)
            row = row - piece
    return tile.astype(bf16)


def read_tile(tile, n):
    tile = tile.astype(f32)
    return [tile[3 * i : 3 * i + 1] + tile[3 * i + 1 : 3 * i + 2] + tile[3 * i + 2 : 3 * i + 3] for i in range(n)]


def soft_kernel(Zh, place_ref, w0_ref, w1_ref, every_ref, l_ref, n_ref, label_ref, live_ref, factor_ref, *refs):
    g_ref, g1_ref, side_ref, loss_ref, gain_ref, a_low, a_high, b_low, b_high = refs[:9]
    wa_ref, wb_ref, sems = refs[9:]
    V = w0_ref.shape[0]
    far = lax.rem(place_ref[0] + 2, R)
    copies = []
    for i, w in enumerate((w0_ref, w1_ref)):
        rows = pl.ds(i * V, V)
        copies.append(
            [pltpu.make_async_copy(w.at[:, pl.ds(0, Zh * R * 128)], wa_ref.at[rows], sems.at[0, i])]
        )
        for z in range(Zh):
            column = pl.multiple_of(((Zh + z) * R + far) * 128, 128)
            copies[-1].append(
                pltpu.make_async_copy(
                    w.at[:, pl.ds(column, 128)],
                    wb_ref.at[rows, pl.ds(z * 128, 128)],
                    sems.at[1 + z, i],
                )
            )
    for pair in copies:
        for copy in pair:
            copy.start()
    every = every_ref[...]
    best = jnp.max(every, axis=0)
    log_total = best + jnp.log(jnp.sum(jnp.exp(every - best[None]), axis=0))
    place = lax.broadcasted_iota(jnp.int32, (R, 128), 0)
    lane = lax.broadcasted_iota(jnp.int32, (1, 2 * V), 1)
    entry = jnp.where(lane < V, place_ref[2] + lane, place_ref[3] + lane - V).astype(f32)

    def block(p, sums):
        inner, target, loss = sums
        rows = pl.ds(pl.multiple_of(p * LIVE, 16), LIVE)
        distance = jnp.where(p < 2, p, 5 - p)
        here = lax.rem(place_ref[1] - distance + R, R)
        total = jnp.sum(jnp.where(place == here, log_total, 0.0), axis=0, keepdims=True)
        pick_row = lambda ref: jnp.sum(jnp.where(place == p, ref[...], 0.0), axis=0, keepdims=True)
        live = pick_row(live_ref)
        logits = l_ref[rows, :]
        match = to_column(pick_row(label_ref)) == entry
        grad = jnp.exp(logits - to_column(total)) - jnp.where(match, 1.0, 0.0)
        grad = grad * to_column(pick_row(factor_ref))
        g_ref[rows, :] = grad.astype(bf16)
        g1_ref[rows, :] = grad[:, V:].astype(bf16)
        line = to_row(jnp.sum(grad * logits, axis=1, keepdims=True))
        inner = jnp.where(place == p, line, inner)
        own = jnp.sum(jnp.where(match, logits, 0.0), axis=1, keepdims=True) * to_column(live)
        target = target + jnp.sum(own, axis=0, keepdims=True)
        loss = loss + jnp.sum(live * total, axis=1, keepdims=True)
        return inner, target, loss

    zero = jnp.zeros((1, 1), f32)
    inner, target, loss = lax.fori_loop(0, R, block, (jnp.zeros((R, 128), f32), zero, zero))
    for p in range(R):
        side_ref[p] = split_tile([inner[p : p + 1], jnp.broadcast_to(target, (1, 128))])
    loss_ref[...] = jnp.broadcast_to(loss, (1, 128))
    for pair in copies:
        for copy in pair:
            copy.wait()
    half = Zh // 2
    gain_ref[...] = jnp.zeros_like(gain_ref)
    part = jnp.dot(g_ref[(R - 1) * LIVE :, :], wa_ref[...], preferred_element_type=f32)
    gain = part * n_ref[(R - 1) * LIVE :, 0 : Zh * R * 128].astype(f32)
    gain = jnp.sum(gain, axis=0, keepdims=True)
    for t in range(Zh * R):
        at = t % (half * R) * LIVE
        gain_ref[t : t + 1, :] = gain[:, t * 128 : (t + 1) * 128]
        (a_low if t < half * R else a_high)[at : at + LIVE, :] = part[
            :, t * 128 : (t + 1) * 128
        ].astype(bf16)
    part = jnp.dot(g_ref[...], wb_ref[...], preferred_element_type=f32)
    for z in range(Zh):
        at = z % half * R * LIVE
        t = (Zh + z) * R + far
        block = part[:, z * 128 : (z + 1) * 128]
        (b_low if z < half else b_high)[at : at + R * LIVE, :] = block.astype(bf16)
        gain = block * n_ref[:, pl.ds(pl.multiple_of(t * 128, 128), 128)].astype(f32)
        gain_ref[pl.ds(t, 1), :] = jnp.sum(gain, axis=0, keepdims=True)
    a_low[Zh // 2 * R * LIVE :, :] = side_ref[R - 1]


def soft_rows(place, Zh, w0, w1, every, logits, normed, labels, live, factor):
    V = w0.shape[0]
    rows = logits.shape[0]
    half = Zh // 2 * R * LIVE
    shapes = [((rows, 2 * V), bf16), ((rows, V), bf16), ((R, 16, 128), bf16), ((1, 128), f32)]
    shapes += [((2 * Zh * R, 128), f32)]
    shapes += [((half + 16, 128), bf16)] + [((half, 128), bf16)] * 3
    return pl.pallas_call(
        functools.partial(soft_kernel, Zh),
        out_shape=tuple(jax.ShapeDtypeStruct(*shape) for shape in shapes),
        in_specs=[SMEM, HBM, HBM] + [VMEM] * 6,
        out_specs=(VMEM,) * len(shapes),
        scratch_shapes=[
            pltpu.VMEM((2 * V, Zh * R * 128), bf16),
            pltpu.VMEM((2 * V, Zh * 128), bf16),
            pltpu.SemaphoreType.DMA((1 + Zh, 2)),
        ],
        compiler_params=pltpu.CompilerParams(vmem_limit_bytes=20 << 20),
        name="soft_rows",
    )(place, w0, w1, every, logits, normed, labels, live, factor)


def near_kernel(Zh, place_ref, w0_ref, w1_ref, side_ref, g_ref, n_ref, *refs):
    a0, a1, a3, b0, b1, b3, gain_ref, w_ref, scratch, sems = refs
    V = w0_ref.shape[0]
    copies = []
    wide = 2 * R * 128
    for q in range(4):
        for i, w in enumerate((w0_ref, w1_ref)):
            copies.append(
                pltpu.make_async_copy(
                    w.at[:, pl.ds(q * wide, wide)], w_ref.at[q, pl.ds(i * V, V)], sems.at[q, i]
                )
            )
    for copy in copies:
        copy.start()

    def arrived(q):
        for i in range(2):
            pltpu.make_async_copy(
                w0_ref.at[:, pl.ds(0, wide)], w_ref.at[q, pl.ds(i * V, V)], sems.at[q, i]
            ).wait()
        return w_ref[q]

    gain_ref[...] = jnp.zeros_like(gain_ref)

    def first(q, _):
        part = jnp.dot(g_ref[0 : 3 * LIVE, :], arrived(q), preferred_element_type=f32)
        gain = n_ref[0 : 3 * LIVE, pl.ds(pl.multiple_of(q * wide, 128), wide)].astype(f32)
        gain = jnp.sum(part * gain, axis=0, keepdims=True)
        for t in range(2 * R):
            at = pl.multiple_of((q * 2 * R + t) * LIVE, 16)
            gain_ref[pl.ds(q * 2 * R + t, 1), :] = gain[:, t * 128 : (t + 1) * 128]
            for p, ref in enumerate((a0, a1, a3)):
                ref[pl.ds(at, LIVE), :] = part[
                    p * LIVE : (p + 1) * LIVE, t * 128 : (t + 1) * 128
                ].astype(ref.dtype)
        return 0

    def second(q, _):
        scratch[...] = jnp.dot(g_ref[...], arrived(2 + q), preferred_element_type=f32)
        for z in range(2):
            at = pl.multiple_of((q * 2 + z) * (R * LIVE), 16)
            for k, ref in ((0, b0), (1, b1), (3, b3)):
                t = z * R + lax.rem(place_ref[0] + k, R)
                part = scratch[:, pl.ds(pl.multiple_of(t * 128, 128), 128)]
                ref[pl.ds(at, R * LIVE), :] = part.astype(ref.dtype)
                t = (Zh + q * 2) * R + t
                gain = n_ref[:, pl.ds(pl.multiple_of(t * 128, 128), 128)].astype(f32)
                gain_ref[pl.ds(t, 1), :] = jnp.sum(part * gain, axis=0, keepdims=True)
        return 0

    lax.fori_loop(0, 2, first, 0)
    lax.fori_loop(0, 2, second, 0)
    a1[Zh * R * LIVE :, :] = side_ref[1]
    a3[Zh * R * LIVE :, :] = side_ref[2]


def near_rows(place, Zh, w0, w1, side, g, normed):
    V = w0.shape[0]
    rows, block = g.shape[0], Zh * R * LIVE
    shapes = [(block, 128), (block + 16, 128), (block + 16, 128)] + [(block, 128)] * 3
    return pl.pallas_call(
        functools.partial(near_kernel, Zh),
        out_shape=(
            *(jax.ShapeDtypeStruct(shape, bf16) for shape in shapes),
            jax.ShapeDtypeStruct((2 * Zh * R, 128), f32),
        ),
        in_specs=[SMEM, HBM, HBM, VMEM, VMEM, VMEM],
        out_specs=(VMEM,) * 7,
        scratch_shapes=[
            pltpu.VMEM((4, 2 * V, 2 * R * 128), bf16),
            pltpu.VMEM((rows, 2 * R * 128), f32),
            pltpu.SemaphoreType.DMA((4, 2)),
        ],
        compiler_params=pltpu.CompilerParams(vmem_limit_bytes=28 << 20),
        name="near_rows",
    )(place, w0, w1, side, g, normed)


def two(value):
    high = value.astype(bf16)
    return high, (value - high.astype(f32)).astype(bf16)


def relay_kernel(up, down, low, high, *refs):
    half, block = high.shape[0], 2 * high.shape[0]
    up_out, down_out = refs[-2:] if len(refs) == 2 else refs[2:4]
    add = lambda a, b: (a.astype(f32) + b.astype(f32)).astype(bf16)
    up_out[0:half, :] = add(up[0:half, :], low[0:half, :])
    up_out[half:block, :] = up[half:block, :]
    down_out[0:half, :] = down[0:half, :]
    down_out[half:block, :] = add(down[half:block, :], high[...])
    if len(refs) > 2:
        mine, came = read_tile(up[block:, :], 2), read_tile(low[half:, :], 2)
        up_out[block : block + 16, :] = split_tile([a + b for a, b in zip(mine, came)])
        down_out[block : block + 16, :] = down[block:, :]
        gain = refs[0][...] + refs[1][...]
        refs[4][...] = gain
        lines = gain.shape[0]
        for i, piece in enumerate(two(gain)):
            for out in (up_out, down_out):
                at = block + 16 + i * lines
                out[at : at + lines, :] = piece


def relay(up, down, low, high, *gains):
    lines = gains[0].shape[0] if gains else 0
    shape = jax.ShapeDtypeStruct((up.shape[0] + 2 * lines, 128), bf16)
    shapes = (shape, shape) + ((jax.ShapeDtypeStruct((lines, 128), f32),) if gains else ())
    return pl.pallas_call(
        relay_kernel,
        out_shape=shapes,
        in_specs=[VMEM] * (4 + len(gains)),
        out_specs=(VMEM,) * len(shapes),
        compiler_params=pltpu.CompilerParams(vmem_limit_bytes=SCOPED),
        name="relay",
    )(up, down, low, high, *gains)


def turn_kernel(Zh, y_ref, side_ref, mine, far, a0, a1, a2, b0, b1, b2, *outs):
    block, part = Zh * R * LIVE, Zh * LIVE

    def one(z, _):
        to = pl.ds(pl.multiple_of(z * LIVE, 16), LIVE)
        for k in range(R):
            row = pl.multiple_of((z * R + lax.rem(y_ref[0] + k, R)) * LIVE, 16)
            rows = pl.ds(row, LIVE)
            total = a0[rows, :].astype(f32) + a1[rows, :].astype(f32) + a2[rows, :].astype(f32)
            outs[k][to, :] = total.astype(outs[k].dtype)
        for j in range(R):
            rows = pl.ds(pl.multiple_of((z * R + ORDER.index(j)) * LIVE, 16), LIVE)
            total = b0[rows, :].astype(f32) + b1[rows, :].astype(f32) + b2[rows, :].astype(f32)
            outs[R + j][to, :] = total.astype(outs[R + j].dtype)
        return 0

    lax.fori_loop(0, Zh, one, 0)
    tiles = [read_tile(t, 2) for t in (side_ref[0], a1[block : block + 16, :], a2[block : block + 16, :])]
    tile = split_tile([sum(rows) for rows in zip(*tiles)])
    outs[2 * R][...] = tile
    lines, gain_ref = mine.shape[0], outs[2 * R + 2]
    gain = mine[...] + far[...]
    for ref in (a1, a2):
        for i in range(2):
            at = block + 16 + i * lines
            gain = gain + ref[at : at + lines, :].astype(f32)
    gain_ref[...] = gain
    Z = 2 * Zh
    place = lax.broadcasted_iota(jnp.int32, (Z, 128), 0)
    for k in range(R):
        gain = jnp.zeros((Z, 128), f32)
        for z in range(Z):
            line = gain_ref[pl.ds(z * R + lax.rem(y_ref[0] + k, R), 1), :]
            gain = jnp.where(place == z, line, gain)
        if k == 0:
            outs[2 * R + 1][...] = gain
        else:
            outs[k][part : part + 16, :] = tile
            outs[k][part + 16 : part + 32, :] = jnp.concatenate(
                [piece.astype(f32) for piece in two(gain)]
            ).astype(bf16)


def turn_rows(y, Zh, side, mine, far, a, b):
    part = Zh * LIVE
    shapes = [((part, 128), f32)] + [((part + 32, 128), bf16)] * (R - 1)
    shapes += [((part, 128), f32)] + [((part, 128), bf16)] * (R - 1) + [((16, 128), bf16)]
    shapes += [((2 * Zh, 128), f32)]
    return pl.pallas_call(
        functools.partial(turn_kernel, Zh),
        out_shape=tuple(jax.ShapeDtypeStruct(*shape) for shape in shapes),
        in_specs=[SMEM] + [VMEM] * 9,
        out_specs=(VMEM,) * (2 * R + 2),
        scratch_shapes=[pltpu.VMEM(mine.shape, f32)],
        compiler_params=pltpu.CompilerParams(vmem_limit_bytes=SCOPED),
        name="turn_rows",
    )(y, side, mine, far, *a, *b)


def gather_kernel(Zh, side_ref, gain_ref, *refs):
    a, b, out = refs[:R], refs[R : 2 * R], refs[2 * R]
    at, Z = Zh * LIVE, 2 * Zh
    tiles = [read_tile(side_ref[...], 2)] + [read_tile(ref[at : at + 16, :], 2) for ref in a[1:]]
    lines = [sum(rows) for rows in zip(*tiles)]
    gain = gain_ref[...]
    for ref in a[1:]:
        pieces = ref[at + 16 : at + 32, :].astype(f32)
        gain = gain + pieces[0:Z] + pieces[Z : 2 * Z]
    for z in range(Z):
        out[z, LIVE:128, :] = split_tile(lines + [gain[z : z + 1]])
    for half, refs in enumerate((a, b)):

        def one(z, _):
            rows = pl.ds(pl.multiple_of(z * LIVE, 16), LIVE)
            total = refs[0][rows, :]
            for ref in refs[1:]:
                total = total + ref[rows, :].astype(f32)
            out[half * Zh + z, 0:LIVE, :] = total.astype(bf16)
            return 0

        lax.fori_loop(0, Zh, one, 0)


def gather_rows(Zh, side, gain, a, b):
    return pl.pallas_call(
        functools.partial(gather_kernel, Zh),
        out_shape=jax.ShapeDtypeStruct((2 * Zh, 128, 128), bf16),
        in_specs=[VMEM] * (2 * R + 2),
        out_specs=VMEM,
        compiler_params=pltpu.CompilerParams(vmem_limit_bytes=SCOPED),
        name="gather_rows",
    )(side, gain, *a, *b)


def prepare_kernel(vocab, hidden_ref, gain_ref, target_ref, start_ref, live_ref, out_ref, meta_ref):
    gain = gain_ref[...]
    high = gain.astype(bf16).astype(f32)
    middle = (gain - high).astype(bf16).astype(f32)
    low = gain - high - middle
    row = lax.broadcasted_iota(jnp.int32, (16, 128), 0)
    tile = jnp.where(row == 0, high, jnp.where(row == 1, middle, jnp.where(row == 2, low, 0.0)))
    for z in range(out_ref.shape[0]):
        out_ref[z, 0:LIVE, :] = hidden_ref[0:LIVE, :]
        out_ref[z, LIVE:128, :] = tile.astype(bf16)
    starts = start_ref[...]
    upto = lax.broadcasted_iota(jnp.int32, (128, 128), 0) <= lax.broadcasted_iota(
        jnp.int32, (128, 128), 1
    )
    flags = jnp.broadcast_to(starts.astype(f32), (16, 128)).astype(bf16)
    order = jnp.dot(flags, upto.astype(f32).astype(bf16), preferred_element_type=f32)
    order = order[0:1].astype(jnp.int32) - 1
    sentinel = vocab - 1 - jnp.clip(order, 0, NSENT - 1)
    label = jnp.where(starts > 0, sentinel, target_ref[...])
    pieces = (label >> 16, (label >> 8) & 255, label & 255, live_ref[...])
    tile = jnp.zeros((16, 128), f32)
    for i, piece in enumerate(pieces):
        tile = jnp.where(row == i, piece.astype(f32), tile)
    meta_ref[...] = tile.astype(bf16)


def prepare(Z, vocab, hidden, norm_gain, targets, span_starts, live_rows):
    line = lambda a: a.reshape(1, 128)
    return pl.pallas_call(
        functools.partial(prepare_kernel, vocab),
        out_shape=(
            jax.ShapeDtypeStruct((Z, 128, 128), bf16),
            jax.ShapeDtypeStruct((16, 128), bf16),
        ),
        in_specs=[VMEM] * 5,
        out_specs=(VMEM, VMEM),
        name="prepare",
    )(hidden, line(norm_gain), line(targets), line(span_starts), line(live_rows))


def meta_kernel(at, w_ref, *refs):
    label_ref, live_ref, factor_ref, total_ref = refs[R:]
    place = lax.broadcasted_iota(jnp.int32, (R, 128), 0)
    labels, live, total = jnp.zeros((R, 128), f32), jnp.zeros((R, 128), f32), jnp.zeros((1, 1), f32)
    for p, j in enumerate(ORDER):
        tile = refs[j][at : at + 16, :].astype(f32)
        label = tile[0:1] * 65536 + tile[1:2] * 256 + tile[2:3]
        labels = jnp.where(place == p, label, labels)
        live = jnp.where(place == p, tile[3:4], live)
        total = total + jnp.sum(tile[3:4] + tile[4:5], axis=1, keepdims=True)
    label_ref[...] = labels
    live_ref[...] = live
    factor_ref[...] = live * (loss_scale / total)
    total_ref[...] = jnp.broadcast_to(total, (1, 128))


def read_meta(at, weight, blocks):
    line = jax.ShapeDtypeStruct((R, 128), f32)
    return pl.pallas_call(
        functools.partial(meta_kernel, at),
        out_shape=(line, line, line, jax.ShapeDtypeStruct((1, 128), f32)),
        in_specs=[VMEM] * (1 + R),
        out_specs=(VMEM,) * 4,
        compiler_params=pltpu.CompilerParams(vmem_limit_bytes=SCOPED),
        name="read_meta",
    )(weight, *blocks)


def outer_kernel(g_ref, h_ref, n_ref, m_ref, out_ref, g_turned, h_turned):
    V = h_ref.shape[1]

    @pl.when(pl.program_id(0) == 0)
    def _():
        g_turned[...] = g_ref[:, 0:V].astype(f32).T.astype(bf16)
        h_turned[...] = h_ref[...].astype(f32).T.astype(bf16)

    total = jnp.dot(g_turned[...], n_ref[...], preferred_element_type=f32)
    total = total + jnp.dot(h_turned[...], m_ref[...], preferred_element_type=f32)
    out_ref[...] = total.astype(bf16)


def outer(g, h, n, m):
    rows, V = h.shape
    D, wide = n.shape[1], 512
    whole = lambda a: pl.BlockSpec(a.shape, lambda i: (0, 0))
    part = pl.BlockSpec((rows, wide), lambda i: (0, i))
    return pl.pallas_call(
        outer_kernel,
        grid=(D // wide,),
        out_shape=jax.ShapeDtypeStruct((V, D), bf16),
        in_specs=[whole(g), whole(h), part, part],
        out_specs=pl.BlockSpec((V, wide), lambda i: (0, i)),
        scratch_shapes=[pltpu.VMEM((V, rows), bf16)] * 2,
        compiler_params=pltpu.CompilerParams(vmem_limit_bytes=SCOPED),
        cost_estimate=pl.CostEstimate(
            flops=4 * rows * V * D, bytes_accessed=8 * V * D, transcendentals=0
        ),
        name="outer",
    )(g, h, n, m)


def finish_kernel(D, loss_ref, total_ref, hidden_ref, gain_ref, inv_ref, out_ref, sums_ref):
    total = total_ref[0].astype(f32)
    for z in range(1, total_ref.shape[0]):
        total = total + total_ref[z].astype(f32)
    inner, target, gain = read_tile(total[LIVE:128], 3)
    total = total[0:LIVE]
    inner = to_column(inner)
    inv = inv_ref[...]
    activation = hidden_ref[0:LIVE, :].astype(f32)
    grad = inv * (total * gain_ref[...]) - activation * (inv * inv * (inner / D))
    out_ref[0:LIVE, :] = grad.astype(bf16)
    out_ref[LIVE:128, :] = jnp.zeros((128 - LIVE, 128), bf16)
    sums_ref[0:1, :] = gain / gain_ref[...]
    sums_ref[1:2, :] = loss_ref[...] - target


def finish(D, loss, total, hidden, norm_gain, inv_rms):
    return pl.pallas_call(
        functools.partial(finish_kernel, D),
        out_shape=(jax.ShapeDtypeStruct((128, 128), bf16), jax.ShapeDtypeStruct((2, 128), f32)),
        in_specs=[VMEM] * 5,
        out_specs=(VMEM, VMEM),
        name="finish",
    )(loss, total, hidden, norm_gain.reshape(1, 128), inv_rms)


def body(hidden, norm_gain, head_weight, targets, span_starts, live_rows):
    Z, Y, X = (lax.axis_size(a) for a in "zyx")
    Zh = Z // 2
    V, D = head_weight.shape
    vocab = V * 2 * Z * Y * X
    c, z, y, x = (lax.axis_index(a) for a in "czyx")
    spot = (z * Y + y) * X + x
    first, second = (c * (Z * Y * X) + spot) * V, ((1 - c) * (Z * Y * X) + spot) * V
    place = jnp.stack([y, x, first, second]).astype(jnp.int32)

    live_other = shift(live_rows, "c", 1)
    weight_other = shift(head_weight, "c", 1)

    block, meta = prepare(Z, vocab, hidden, norm_gain, targets, span_starts, live_rows)
    block = lax.all_to_all(block, "z", 0, 0)
    meta = meta + jnp.pad(live_other[None].astype(bf16), ((4, 11), (0, 0)))
    block, weight_other, meta = lax.optimization_barrier((block, weight_other, meta))

    a_block = jnp.concatenate(
        [block[:Zh, :LIVE].reshape(-1, 128), block[:, LIVE:].reshape(-1, 128)]
    )
    b_block = jnp.concatenate([block[Zh:, :LIVE].reshape(-1, 128), meta])
    a_blocks = [a_block] + [shift(a_block, "y", k) for k in range(1, R)]
    b_blocks = [b_block] + [shift(b_block, "x", k) for k in range(1, R)]
    a_all = ring_gather(jnp.concatenate([a[: Zh * LIVE] for a in a_blocks]), "x")
    b_all = ring_gather(jnp.concatenate([b[: Zh * LIVE] for b in b_blocks]), "y")
    labels, live, factor, live_total = read_meta(Zh * LIVE, head_weight, b_blocks)
    a_all, b_all, labels, live, factor = lax.optimization_barrier(
        (a_all, b_all, labels, live, factor)
    )

    weights = (head_weight, weight_other)
    normed_all, inv_rms, logits, share = forward(place, Zh, *weights, a_blocks, a_all, b_all)
    normed_other = shift(normed_all, "c", 1)
    every = lax.all_to_all(share, ("z", "y", "x"), 0, 0)
    every, normed_other = lax.optimization_barrier((every, normed_other))
    g, g1, side, loss, gain_far, a_low, a_high, b_low, b_high = soft_rows(
        place, Zh, *weights, every, logits, normed_all, labels, live, factor
    )

    a_low, a_high = shift(a_low, "x", 1), shift(a_high, "x", -1)
    b_low, b_high = shift(b_low, "y", 1), shift(b_high, "y", -1)
    near = near_rows(place, Zh, *weights, side, g, normed_all)
    g_other = shift(g1, "c", 1)
    near, a_low, a_high, b_low, b_high, g, g_other = lax.optimization_barrier(
        (near, a_low, a_high, b_low, b_high, g, g_other)
    )
    a0, a1, a3, b0, b1, b3, gain_near = near
    a_up, a_down, gain = relay(a3, a1, a_low, a_high, gain_far, gain_near)
    b_up, b_down = relay(b1, b3, b_low, b_high)
    a_in = shift(a_up, "x", 1), shift(a_down, "x", -1)
    b_in = shift(b_up, "y", 1), shift(b_down, "y", -1)
    gain_in = shift(gain, "x", 2)
    weight_grad = outer(g, g_other, normed_all, normed_other)
    a_in, b_in, weight_grad = lax.optimization_barrier((a_in, b_in, weight_grad))
    outs = turn_rows(place, Zh, side, gain, gain_in, (a0, *a_in), (b0, *b_in))
    a_sums = [outs[0]] + [shift(outs[k], "y", k) for k in range(1, R)]
    b_sums = [outs[R]] + [shift(outs[R + k], "x", -k) for k in range(1, R)]
    total = gather_rows(Zh, outs[2 * R], outs[2 * R + 1], a_sums, b_sums)
    total = lax.all_to_all(total, "z", 0, 0)
    hidden_grad, sums = finish(D, loss, total, hidden, norm_gain, inv_rms)

    sums = sums + shift(sums, "c", 1)
    gain_grad = sums[0]
    mean_loss = sums[1, 0] / live_total[0, 0]
    return (hidden_grad, gain_grad, weight_grad, mean_loss)


def solution(mesh):
    S, T, X = mesh.devices.shape
    split = Mesh(mesh.devices.reshape(S, T // R, R, X), ("c", "z", "y", "x"))
    rows, features, entries = ("c", "x"), ("z", "y"), ("c", "z", "y", "x")
    return jax.shard_map(
        body,
        mesh=split,
        in_specs=(P(rows, features), P(features), P(entries, None), P(rows), P(rows), P(rows)),
        out_specs=(P(rows, features), P(features), P(entries, None), P()),
        check_vma=False,
    )
```

profile of v0, /device:TPU:1, one launch (start us, length us, event | category | flops | bytes accessed | tf_op | source)
XLA Modules:
  0.0 165.4 jit_solution(15892781196245955360)
XLA Ops:
  0.6 3.3 %collective-permute-start = (bf16[512,4096]{1,0:T(8,128)(2,1)}, bf16[512,4096]{1,0:T(8,128)(2,1)}, u32[]{:S(2)}, u32[]{:S(2)}) collective-permute-start(bf16[512,4096]{1,0:T(8,128)(2,1)} %w0_ref.5), channel_id=1, source_target_pairs={{0,128},{128,0},{1,129},{129,1},{2,130},{130,2},{3,131},{131,3},{4... | collective-permute-start | bytes 12582920 | tf_op jit(solution)/shard_map/ppermute | solution.py:24
  4.0 1.5 prepare.1
  5.5 6.5 %all-to-all-start = ((bf16[8,128,128]{2,1,0:T(8,128)(2,1)}), bf16[8,128,128]{2,1,0:T(8,128)(2,1)S(1)}, u32[]{:S(2)}, u32[]{:S(2)}) async-start(bf16[8,128,128]{2,1,0:T(8,128)(2,1)} %get-tuple-element.83), calls=%async_computation | async-start | bytes 524288 | tf_op jit(solution)/shard_map/all_to_all | solution.py:621
  11.9 0.3 collective-permute-start.1
  12.2 1.0 collective-permute-done.1
  13.2 0.7 pad_add_fusion
  13.9 10.4 %all-to-all-done = bf16[8,128,128]{2,1,0:T(8,128)(2,1)S(1)} async-done(((bf16[8,128,128]{2,1,0:T(8,128)(2,1)}), bf16[8,128,128]{2,1,0:T(8,128)(2,1)S(1)}, u32[]{:S(2)}, u32[]{:S(2)}) %all-to-all-start) | async-done | bytes 262176 | tf_op jit(solution)/shard_map/all_to_all | solution.py:621
  24.4 2.6 %collective-permute-start.11 = (bf16[464,128]{1,0:T(8,128)(2,1)S(1)}, bf16[464,128]{1,0:T(8,128)(2,1)S(1)}, u32[]{:S(2)}, u32[]{:S(2)}) collective-permute-start(bf16[464,128]{1,0:T(8,128)(2,1)S(1)} %pad_maximum_fusion.3.refs_0_), channel_id=1, source_target_pairs={{0,3},{1,0},{2,1},{3,2},{4,7},{5,4},{6,5},{7,6},{8,11},{9,8},{10,9... | collective-permute-start | bytes 356360 | tf_op jit(solution)/shard_map/ppermute | solution.py:24
  26.9 0.5 collective-permute-start.10
  27.4 0.6 collective-permute-start.9
  28.1 2.8 %collective-permute-start.4 = (bf16[576,128]{1,0:T(8,128)(2,1)S(1)}, bf16[576,128]{1,0:T(8,128)(2,1)S(1)}, u32[]{:S(2)}, u32[]{:S(2)}) collective-permute-start(bf16[576,128]{1,0:T(8,128)(2,1)S(1)} %pad_maximum_fusion.2.refs_0_), channel_id=1, source_target_pairs={{0,12},{4,0},{8,4},{12,8},{1,13},{5,1},{9,5},{13,9},{2,14},{6,2},{... | collective-permute-start | bytes 442376 | tf_op jit(solution)/shard_map/ppermute | solution.py:24
  30.9 0.3 collective-permute-start.3
  31.2 0.7 collective-permute-start.2
  31.9 0.5 collective-permute-done.10.refs_2_
  32.4 3.6 %collective-permute-done.9.refs_1_ = bf16[464,128]{1,0:T(8,128)(2,1)S(1)} collective-permute-done((bf16[464,128]{1,0:T(8,128)(2,1)S(1)}, bf16[464,128]{1,0:T(8,128)(2,1)S(1)}, u32[]{:S(2)}, u32[]{:S(2)}) %collective-permute-start.9) | collective-permute-done | bytes 118816 | tf_op jit(solution)/shard_map/ppermute | solution.py:24
  36.1 2.8 %collective-permute-start.13 = (bf16[1792,128]{1,0:T(8,128)(2,1)S(1)}, bf16[1792,128]{1,0:T(8,128)(2,1)S(1)}, u32[]{:S(2)}, u32[]{:S(2)}) collective-permute-start(bf16[1792,128]{1,0:T(8,128)(2,1)S(1)} %pad_maximum_fusion.1.refs_9_), channel_id=1, source_target_pairs={{0,12},{4,0},{8,4},{12,8},{1,13},{5,1},{9,5},{13,9},{2,14},{6,2},{... | collective-permute-start | bytes 1376264 | tf_op jit(solution)/shard_map/ppermute | solution.py:24
  38.9 1.7 %collective-permute-done.2.refs_1_ = bf16[576,128]{1,0:T(8,128)(2,1)S(1)} collective-permute-done((bf16[576,128]{1,0:T(8,128)(2,1)S(1)}, bf16[576,128]{1,0:T(8,128)(2,1)S(1)}, u32[]{:S(2)}, u32[]{:S(2)}) %collective-permute-start.2) | collective-permute-done | bytes 147488 | tf_op jit(solution)/shard_map/ppermute | solution.py:24
  40.7 0.7 copy-done.4
  41.4 2.6 %collective-permute-start.6 = (bf16[1792,128]{1,0:T(8,128)(2,1)S(1)}, bf16[1792,128]{1,0:T(8,128)(2,1)S(1)}, u32[]{:S(2)}, u32[]{:S(2)}) collective-permute-start(bf16[1792,128]{1,0:T(8,128)(2,1)S(1)} %pad_maximum_fusion.refs_4_), channel_id=1, source_target_pairs={{0,3},{1,0},{2,1},{3,2},{4,7},{5,4},{6,5},{7,6},{8,11},{9,8},{10,9... | collective-permute-start | bytes 1376264 | tf_op jit(solution)/shard_map/ppermute | solution.py:24
  44.0 4.1 %collective-permute-done.13.refs_11_ = bf16[1792,128]{1,0:T(8,128)(2,1)S(1)} collective-permute-done((bf16[1792,128]{1,0:T(8,128)(2,1)S(1)}, bf16[1792,128]{1,0:T(8,128)(2,1)S(1)}, u32[]{:S(2)}, u32[]{:S(2)}) %collective-permute-start.13) | collective-permute-done | bytes 458784 | tf_op jit(solution)/shard_map/ppermute | solution.py:24
  48.2 0.7 slice.73
  48.9 3.4 %collective-permute-start.15 = (bf16[896,128]{1,0:T(8,128)(2,1)}, bf16[896,128]{1,0:T(8,128)(2,1)}, u32[]{:S(2)}, u32[]{:S(2)}) collective-permute-start(bf16[896,128]{1,0:T(8,128)(2,1)} %slice.73), channel_id=1, source_target_pairs={{0,12},{4,0},{8,4},{12,8},{1,13},{5,1},{9,5},{13,9},{2,14},{6,2},{... | collective-permute-start | bytes 688136 | tf_op jit(solution)/shard_map/ppermute | solution.py:24
  52.3 0.7 slice.72
  53.0 0.7 slice.68
  53.7 2.8 %collective-permute-start.8 = (bf16[896,128]{1,0:T(8,128)(2,1)}, bf16[896,128]{1,0:T(8,128)(2,1)}, u32[]{:S(2)}, u32[]{:S(2)}) collective-permute-start(bf16[896,128]{1,0:T(8,128)(2,1)} %slice.68), channel_id=1, source_target_pairs={{0,3},{1,0},{2,1},{3,2},{4,7},{5,4},{6,5},{7,6},{8,11},{9,8},{10,9... | collective-permute-start | bytes 688136 | tf_op jit(solution)/shard_map/ppermute | solution.py:24
  56.5 0.7 slice.67
  57.2 0.1 pad_add_fusion.1.place_ref.y_ref
  57.3 2.2 %copy-done = bf16[512,4096]{1,0:T(8,128)(2,1)S(1)} copy-done((bf16[512,4096]{1,0:T(8,128)(2,1)S(1)}, bf16[512,4096]{1,0:T(8,128)(2,1)}, u32[]{:S(2)}) %copy-start) | copy-done | bytes 4194328
  59.4 0.1 read_meta.1
  59.5 0.3 collective-permute-done.14.refs_12_
  59.9 3.7 %collective-permute-done.7.refs_7_ = bf16[896,128]{1,0:T(8,128)(2,1)} collective-permute-done((bf16[896,128]{1,0:T(8,128)(2,1)}, bf16[896,128]{1,0:T(8,128)(2,1)}, u32[]{:S(2)}, u32[]{:S(2)}) %collective-permute-start.7) | collective-permute-done | bytes 229408 | tf_op jit(solution)/shard_map/ppermute | solution.py:24
  63.6 9.2 %forward.1 = (bf16[448,4096]{1,0:T(8,128)(2,1)S(1)}, f32[112,1]{1,0:T(8,128)S(1)}, f32[448,1024]{1,0:T(8,128)S(1)}, f32[128,4,128]{2,1,0:T(4,128)S(1)}) custom-call(s32[4]{0:T(128)S(1)} %pad_add_fusion.1.place_ref.y_ref, bf16[512,4096]{1,0:T(8,128)(2,1)S(1)} %copy-done.1, bf16[512,4096]{1,0:T(8,128)(2,1)} %collective-permute-done.w1_ref, ...), custom_call_target="tpu_custom_call" | custom-call | flops 3758096384 | bytes 8388608 | tf_op jit(solution)/shard_map/forward/pallas_call | solution.py:127
  72.8 3.9 %collective-permute-start.16 = (bf16[448,4096]{1,0:T(8,128)(2,1)S(1)}, bf16[448,4096]{1,0:T(8,128)(2,1)S(1)}, u32[]{:S(2)}, u32[]{:S(2)}) collective-permute-start(bf16[448,4096]{1,0:T(8,128)(2,1)S(1)} %get-tuple-element.102.n_ref), channel_id=1, source_target_pairs={{0,128},{128,0},{1,129},{129,1},{2,130},{130,2},{3,131},{131,3},{4... | collective-permute-start | bytes 11010056 | tf_op jit(solution)/shard_map/ppermute | solution.py:24
  76.7 19.8 %all_to_all.15.every_ref = f32[128,4,128]{2,1,0:T(4,128)S(1)} all-to-all(f32[128,4,128]{2,1,0:T(4,128)S(1)} %get-tuple-element.101), channel_id=1, replica_groups=mesh['c'=2,'z'=8,'y'=4,'x'=4] {'z','y','x'}, dimensions={0} | all-to-all | bytes 524288 | tf_op jit(solution)/shard_map/all_to_all | solution.py:641
  96.5 4.0 %soft_rows.1 = (bf16[448,1024]{1,0:T(8,128)(2,1)S(1)}, bf16[448,512]{1,0:T(8,128)(2,1)S(1)}, bf16[4,16,128]{2,1,0:T(8,128)(2,1)S(1)}, f32[1,128]{1,0:T(1,128)S(1...) custom-call(s32[4]{0:T(128)S(1)} %pad_add_fusion.1.place_ref.y_ref, ...), custom_call_target="tpu_custom_call" | custom-call | tf_op jit(solution)/shard_map/soft_rows/pallas_call | solution.py:253
  100.6 1.9 %collective-permute-start.21 = (bf16[448,512]{1,0:T(8,128)(2,1)S(1)}, bf16[448,512]{1,0:T(8,128)(2,1)S(1)}, u32[]{:S(2)}, u32[]{:S(2)}) collective-permute-start(bf16[448,512]{1,0:T(8,128)(2,1)S(1)} %get-tuple-element.122), channel_id=1, source_target_pairs={{0,128},{128,0},{1,129},{129,1},{2,130},{130,2},{3,131},{131,3},{4... | collective-permute-start | bytes 1376264 | tf_op jit(solution)/shard_map/ppermute | solution.py:24
  102.5 0.3 collective-permute-start.17
  102.7 2.4 %collective-permute-start.18 = (bf16[896,128]{1,0:T(8,128)(2,1)S(1)}, bf16[896,128]{1,0:T(8,128)(2,1)S(1)}, u32[]{:S(2)}, u32[]{:S(2)}) collective-permute-start(bf16[896,128]{1,0:T(8,128)(2,1)S(1)} %get-tuple-element.119), channel_id=1, source_target_pairs={{0,3},{1,0},{2,1},{3,2},{4,7},{5,4},{6,5},{7,6},{8,11},{9,8},{10,9... | collective-permute-start | bytes 688136 | tf_op jit(solution)/shard_map/ppermute | solution.py:24
  105.2 0.3 collective-permute-start.19
  105.5 2.4 %collective-permute-start.20 = (bf16[896,128]{1,0:T(8,128)(2,1)S(1)}, bf16[896,128]{1,0:T(8,128)(2,1)S(1)}, u32[]{:S(2)}, u32[]{:S(2)}) collective-permute-start(bf16[896,128]{1,0:T(8,128)(2,1)S(1)} %get-tuple-element.121), channel_id=1, source_target_pairs={{0,12},{4,0},{8,4},{12,8},{1,13},{5,1},{9,5},{13,9},{2,14},{6,2},{... | collective-permute-start | bytes 688136 | tf_op jit(solution)/shard_map/ppermute | solution.py:24
  107.8 6.9 %near_rows.1 = (bf16[1792,128]{1,0:T(8,128)(2,1)S(1)}, bf16[1808,128]{1,0:T(8,128)(2,1)S(1)}, bf16[1808,128]{1,0:T(8,128)(2,1)S(1)}, bf16[1792,128]{1,0:T(8,128)...) custom-call(s32[4]{0:T(128)S(1)} %pad_add_fusion.1.place_ref.y_ref, ...), custom_call_target="tpu_custom_call" | custom-call | tf_op jit(solution)/shard_map/near_rows/pallas_call | solution.py:328
  114.8 0.1 relay.2
  115.0 0.1 collective-permute-start.23
  115.1 2.7 %collective-permute-start.24 = (bf16[1872,128]{1,0:T(8,128)(2,1)S(1)}, bf16[1872,128]{1,0:T(8,128)(2,1)S(1)}, u32[]{:S(2)}, u32[]{:S(2)}) collective-permute-start(bf16[1872,128]{1,0:T(8,128)(2,1)S(1)} %get-tuple-element.132), channel_id=1, source_target_pairs={{0,3},{1,0},{2,1},{3,2},{4,7},{5,4},{6,5},{7,6},{8,11},{9,8},{10,9... | collective-permute-start | bytes 1437704 | tf_op jit(solution)/shard_map/ppermute | solution.py:24
  117.7 0.1 relay.3
  117.9 0.1 collective-permute-start.25
  118.0 2.7 %collective-permute-start.26 = (bf16[1792,128]{1,0:T(8,128)(2,1)S(1)}, bf16[1792,128]{1,0:T(8,128)(2,1)S(1)}, u32[]{:S(2)}, u32[]{:S(2)}) collective-permute-start(bf16[1792,128]{1,0:T(8,128)(2,1)S(1)} %get-tuple-element.138), channel_id=1, source_target_pairs={{0,12},{4,0},{8,4},{12,8},{1,13},{5,1},{9,5},{13,9},{2,14},{6,2},{... | collective-permute-start | bytes 1376264 | tf_op jit(solution)/shard_map/ppermute | solution.py:24
  120.6 7.4 %outer.1 = bf16[512,4096]{1,0:T(8,128)(2,1)} custom-call(bf16[448,1024]{1,0:T(8,128)(2,1)S(1)} %get-tuple-element.139.g_ref, bf16[448,512]{1,0:T(8,128)(2,1)S(1)} %collective-permute-done.21.h_ref, bf16[448,4096]{1,0:T(8,128)(2,1)S(1)} %get-tuple-element.102.n_ref, bf16[448,4096]{1,0:T(8,128)(2,1)S(1)} %collective-permute-done.16.m_ref), custom_call_target="tpu_custom_call" | custom-call | flops 3758096384 | bytes 16777216 | tf_op jit(solution)/shard_map/outer/pallas_call | solution.py:566
  128.0 1.4 collective-permute-done.25.b1
  129.4 0.9 turn_rows.1
  130.4 0.7 collective-permute-start.30
  131.1 3.2 %collective-permute-start.28 = (bf16[480,128]{1,0:T(8,128)(2,1)S(1)}, bf16[480,128]{1,0:T(8,128)(2,1)S(1)}, u32[]{:S(2)}, u32[]{:S(2)}) collective-permute-start(bf16[480,128]{1,0:T(8,128)(2,1)S(1)} %get-tuple-element.151), channel_id=1, source_target_pairs={{0,8},{4,12},{8,0},{12,4},{1,9},{5,13},{9,1},{13,5},{2,10},{6,14},... | collective-permute-start | bytes 368648 | tf_op jit(solution)/shard_map/ppermute | solution.py:24
  134.3 0.7 collective-permute-start.31
  135.0 0.6 collective-permute-start.32
  135.6 3.9 %collective-permute-done.31.refs_6_ = bf16[448,128]{1,0:T(8,128)(2,1)S(1)} collective-permute-done((bf16[448,128]{1,0:T(8,128)(2,1)S(1)}, bf16[448,128]{1,0:T(8,128)(2,1)S(1)}, u32[]{:S(2)}, u32[]{:S(2)}) %collective-permute-start.31) | collective-permute-done | bytes 114720 | tf_op jit(solution)/shard_map/ppermute | solution.py:24
  139.5 1.5 collective-permute-done.32.refs_7_
  141.0 0.2 gather_rows.1
  141.2 12.4 %all_to_all.16.total_ref = bf16[8,128,128]{2,1,0:T(8,128)(2,1)} all-to-all(bf16[8,128,128]{2,1,0:T(8,128)(2,1)S(1)} %gather_rows.1), channel_id=1, replica_groups=mesh['c'=2,'z'=8,'y'=4,'x'=4] {'z'}, dimensions={0} | all-to-all | bytes 524288 | tf_op jit(solution)/shard_map/all_to_all | solution.py:666
  153.6 1.8 %finish.1 = (bf16[128,128]{1,0:T(8,128)(2,1)}, f32[2,128]{1,0:T(2,128)}) custom-call(f32[1,128]{1,0:T(1,128)} %copy-done.7, bf16[8,128,128]{2,1,0:T(8,128)(2,1)} %all_to_all.16.total_ref, bf16[128,128]{1,0:T(8,128)(2,1)} %hidden_ref.3, f32[1,128]{1,0:T(1,128)} %bitcast.24, f32[112,1]{1,0:T(8,128)} %copy-done.6), custom_call_target="tpu_custom_call" | custom-call | tf_op jit(solution)/shard_map/finish/pallas_call | solution.py:598
  155.3 5.5 %collective-permute-start.33 = (f32[2,128]{1,0:T(2,128)}, f32[2,128]{1,0:T(2,128)S(1)}, u32[]{:S(2)}, u32[]{:S(2)}) collective-permute-start(f32[2,128]{1,0:T(2,128)} %get-tuple-element.159), channel_id=1, source_target_pairs={{0,128},{128,0},{1,129},{129,1},{2,130},{130,2},{3,131},{131,3},{4... | collective-permute-start | bytes 3080 | tf_op jit(solution)/shard_map/ppermute | solution.py:24
  160.8 1.0 collective-permute-done.33
  161.9 0.7 add.25
  162.5 0.5 slice.62
  163.1 0.5 slice_bitcast_fusion
  (57 shorter events, 0.3 us)
Async XLA Ops:
  0.6 23.7 %collective-permute-start = (bf16[512,4096]{1,0:T(8,128)(2,1)}, bf16[512,4096]{1,0:T(8,128)(2,1)}, u32[]{:S(2)}, u32[]{:S(2)}) collective-permute-start(bf16[512,4096]{1,0:T(8,128)(2,1)} %w0_ref.5), channel_id=1, source_target_pairs={{0,128},{128,0},{1,129},{129,1},{2,130},{130,2},{3,131},{131,3},{4... | collective-permute-start | bytes 12582920 | tf_op jit(solution)/shard_map/ppermute | solution.py:24
  5.5 18.8 %all-to-all-start = ((bf16[8,128,128]{2,1,0:T(8,128)(2,1)}), bf16[8,128,128]{2,1,0:T(8,128)(2,1)S(1)}, u32[]{:S(2)}, u32[]{:S(2)}) async-start(bf16[8,128,128]{2,1,0:T(8,128)(2,1)} %get-tuple-element.83), calls=%async_computation | async-start | bytes 524288 | tf_op jit(solution)/shard_map/all_to_all | solution.py:621
  11.9 1.3 collective-permute-start.1
  24.4 6.9 %collective-permute-start.11 = (bf16[464,128]{1,0:T(8,128)(2,1)S(1)}, bf16[464,128]{1,0:T(8,128)(2,1)S(1)}, u32[]{:S(2)}, u32[]{:S(2)}) collective-permute-start(bf16[464,128]{1,0:T(8,128)(2,1)S(1)} %pad_maximum_fusion.3.refs_0_), channel_id=1, source_target_pairs={{0,3},{1,0},{2,1},{3,2},{4,7},{5,4},{6,5},{7,6},{8,11},{9,8},{10,9... | collective-permute-start | bytes 356360 | tf_op jit(solution)/shard_map/ppermute | solution.py:24
  26.9 5.5 %collective-permute-start.10 = (bf16[464,128]{1,0:T(8,128)(2,1)S(1)}, bf16[464,128]{1,0:T(8,128)(2,1)S(1)}, u32[]{:S(2)}, u32[]{:S(2)}) collective-permute-start(bf16[464,128]{1,0:T(8,128)(2,1)S(1)} %pad_maximum_fusion.3.refs_0_), channel_id=1, source_target_pairs={{0,2},{1,3},{2,0},{3,1},{4,6},{5,7},{6,4},{7,5},{8,10},{9,11},{10,... | collective-permute-start | bytes 356360 | tf_op jit(solution)/shard_map/ppermute | solution.py:24
  27.4 8.6 %collective-permute-start.9 = (bf16[464,128]{1,0:T(8,128)(2,1)S(1)}, bf16[464,128]{1,0:T(8,128)(2,1)S(1)}, u32[]{:S(2)}, u32[]{:S(2)}) collective-permute-start(bf16[464,128]{1,0:T(8,128)(2,1)S(1)} %pad_maximum_fusion.3.refs_0_), channel_id=1, source_target_pairs={{0,1},{1,2},{2,3},{3,0},{4,5},{5,6},{6,7},{7,4},{8,9},{9,10},{10,1... | collective-permute-start | bytes 356360 | tf_op jit(solution)/shard_map/ppermute | solution.py:24
  28.1 10.8 %collective-permute-start.4 = (bf16[576,128]{1,0:T(8,128)(2,1)S(1)}, bf16[576,128]{1,0:T(8,128)(2,1)S(1)}, u32[]{:S(2)}, u32[]{:S(2)}) collective-permute-start(bf16[576,128]{1,0:T(8,128)(2,1)S(1)} %pad_maximum_fusion.2.refs_0_), channel_id=1, source_target_pairs={{0,12},{4,0},{8,4},{12,8},{1,13},{5,1},{9,5},{13,9},{2,14},{6,2},{... | collective-permute-start | bytes 442376 | tf_op jit(solution)/shard_map/ppermute | solution.py:24
  30.9 8.0 %collective-permute-start.3 = (bf16[576,128]{1,0:T(8,128)(2,1)S(1)}, bf16[576,128]{1,0:T(8,128)(2,1)S(1)}, u32[]{:S(2)}, u32[]{:S(2)}) collective-permute-start(bf16[576,128]{1,0:T(8,128)(2,1)S(1)} %pad_maximum_fusion.2.refs_0_), channel_id=1, source_target_pairs={{0,8},{4,12},{8,0},{12,4},{1,9},{5,13},{9,1},{13,5},{2,10},{6,14},... | collective-permute-start | bytes 442376 | tf_op jit(solution)/shard_map/ppermute | solution.py:24
  31.2 9.4 %collective-permute-start.2 = (bf16[576,128]{1,0:T(8,128)(2,1)S(1)}, bf16[576,128]{1,0:T(8,128)(2,1)S(1)}, u32[]{:S(2)}, u32[]{:S(2)}) collective-permute-start(bf16[576,128]{1,0:T(8,128)(2,1)S(1)} %pad_maximum_fusion.2.refs_0_), channel_id=1, source_target_pairs={{0,4},{4,8},{8,12},{12,0},{1,5},{5,9},{9,13},{13,1},{2,6},{6,10},{... | collective-permute-start | bytes 442376 | tf_op jit(solution)/shard_map/ppermute | solution.py:24
  36.1 12.1 %collective-permute-start.13 = (bf16[1792,128]{1,0:T(8,128)(2,1)S(1)}, bf16[1792,128]{1,0:T(8,128)(2,1)S(1)}, u32[]{:S(2)}, u32[]{:S(2)}) collective-permute-start(bf16[1792,128]{1,0:T(8,128)(2,1)S(1)} %pad_maximum_fusion.1.refs_9_), channel_id=1, source_target_pairs={{0,12},{4,0},{8,4},{12,8},{1,13},{5,1},{9,5},{13,9},{2,14},{6,2},{... | collective-permute-start | bytes 1376264 | tf_op jit(solution)/shard_map/ppermute | solution.py:24
  38.9 13.4 %collective-permute-start.12 = (bf16[1792,128]{1,0:T(8,128)(2,1)S(1)}, bf16[1792,128]{1,0:T(8,128)(2,1)S(1)}, u32[]{:S(2)}, u32[]{:S(2)}) collective-permute-start(bf16[1792,128]{1,0:T(8,128)(2,1)S(1)} %pad_maximum_fusion.1.refs_9_), channel_id=1, source_target_pairs={{0,4},{4,8},{8,12},{12,0},{1,5},{5,9},{9,13},{13,1},{2,6},{6,10},{... | collective-permute-start | bytes 1376264 | tf_op jit(solution)/shard_map/ppermute | solution.py:24
  38.9 1.8 %copy-start.2 = (bf16[576,128]{1,0:T(8,128)(2,1)}, bf16[576,128]{1,0:T(8,128)(2,1)S(1)}, u32[]{:S(2)}) copy-start(bf16[576,128]{1,0:T(8,128)(2,1)S(1)} %collective-permute-done.3.refs_2_) | copy-start | bytes 442372
  40.7 0.7 copy-start.4
  41.4 11.6 %collective-permute-start.6 = (bf16[1792,128]{1,0:T(8,128)(2,1)S(1)}, bf16[1792,128]{1,0:T(8,128)(2,1)S(1)}, u32[]{:S(2)}, u32[]{:S(2)}) collective-permute-start(bf16[1792,128]{1,0:T(8,128)(2,1)S(1)} %pad_maximum_fusion.refs_4_), channel_id=1, source_target_pairs={{0,3},{1,0},{2,1},{3,2},{4,7},{5,4},{6,5},{7,6},{8,11},{9,8},{10,9... | collective-permute-start | bytes 1376264 | tf_op jit(solution)/shard_map/ppermute | solution.py:24
  44.0 12.5 %collective-permute-start.5 = (bf16[1792,128]{1,0:T(8,128)(2,1)S(1)}, bf16[1792,128]{1,0:T(8,128)(2,1)S(1)}, u32[]{:S(2)}, u32[]{:S(2)}) collective-permute-start(bf16[1792,128]{1,0:T(8,128)(2,1)S(1)} %pad_maximum_fusion.refs_4_), channel_id=1, source_target_pairs={{0,1},{1,2},{2,3},{3,0},{4,5},{5,6},{6,7},{7,4},{8,9},{9,10},{10,1... | collective-permute-start | bytes 1376264 | tf_op jit(solution)/shard_map/ppermute | solution.py:24
  48.9 10.7 %collective-permute-start.15 = (bf16[896,128]{1,0:T(8,128)(2,1)}, bf16[896,128]{1,0:T(8,128)(2,1)}, u32[]{:S(2)}, u32[]{:S(2)}) collective-permute-start(bf16[896,128]{1,0:T(8,128)(2,1)} %slice.73), channel_id=1, source_target_pairs={{0,12},{4,0},{8,4},{12,8},{1,13},{5,1},{9,5},{13,9},{2,14},{6,2},{... | collective-permute-start | bytes 688136 | tf_op jit(solution)/shard_map/ppermute | solution.py:24
  53.0 6.9 %collective-permute-start.14 = (bf16[896,128]{1,0:T(8,128)(2,1)}, bf16[896,128]{1,0:T(8,128)(2,1)}, u32[]{:S(2)}, u32[]{:S(2)}) collective-permute-start(bf16[896,128]{1,0:T(8,128)(2,1)} %slice.72), channel_id=1, source_target_pairs={{0,4},{4,8},{8,12},{12,0},{1,5},{5,9},{9,13},{13,1},{2,6},{6,10},{... | collective-permute-start | bytes 688136 | tf_op jit(solution)/shard_map/ppermute | solution.py:24
  53.7 6.2 %collective-permute-start.8 = (bf16[896,128]{1,0:T(8,128)(2,1)}, bf16[896,128]{1,0:T(8,128)(2,1)}, u32[]{:S(2)}, u32[]{:S(2)}) collective-permute-start(bf16[896,128]{1,0:T(8,128)(2,1)} %slice.68), channel_id=1, source_target_pairs={{0,3},{1,0},{2,1},{3,2},{4,7},{5,4},{6,5},{7,6},{8,11},{9,8},{10,9... | collective-permute-start | bytes 688136 | tf_op jit(solution)/shard_map/ppermute | solution.py:24
  57.2 6.4 %collective-permute-start.7 = (bf16[896,128]{1,0:T(8,128)(2,1)}, bf16[896,128]{1,0:T(8,128)(2,1)}, u32[]{:S(2)}, u32[]{:S(2)}) collective-permute-start(bf16[896,128]{1,0:T(8,128)(2,1)} %slice.67), channel_id=1, source_target_pairs={{0,1},{1,2},{2,3},{3,0},{4,5},{5,6},{6,7},{7,4},{8,9},{9,10},{10,1... | collective-permute-start | bytes 688136 | tf_op jit(solution)/shard_map/ppermute | solution.py:24
  57.2 2.2 %copy-start = (bf16[512,4096]{1,0:T(8,128)(2,1)S(1)}, bf16[512,4096]{1,0:T(8,128)(2,1)}, u32[]{:S(2)}) copy-start(bf16[512,4096]{1,0:T(8,128)(2,1)} %w0_ref.5) | copy-start | bytes 12582916
  59.4 4.1 %copy-start.1 = (bf16[512,4096]{1,0:T(8,128)(2,1)S(1)}, bf16[512,4096]{1,0:T(8,128)(2,1)}, u32[]{:S(2)}) copy-start(bf16[512,4096]{1,0:T(8,128)(2,1)} %w0_ref.5) | copy-start | bytes 12582916
  59.4 4.1 %copy-start.3 = (bf16[576,128]{1,0:T(8,128)(2,1)S(1)}, bf16[576,128]{1,0:T(8,128)(2,1)}, u32[]{:S(2)}) copy-start(bf16[576,128]{1,0:T(8,128)(2,1)} %copy-done.2) | copy-start | bytes 442372
  59.4 4.1 %copy-start.5 = (bf16[576,128]{1,0:T(8,128)(2,1)S(1)}, bf16[576,128]{1,0:T(8,128)(2,1)}, u32[]{:S(2)}) copy-start(bf16[576,128]{1,0:T(8,128)(2,1)} %copy-done.4) | copy-start | bytes 442372
  72.8 27.7 %copy-start.6 = (f32[112,1]{1,0:T(8,128)}, f32[112,1]{1,0:T(8,128)S(1)}, u32[]{:S(2)}) copy-start(f32[112,1]{1,0:T(8,128)S(1)} %get-tuple-element.157.inv_ref) | copy-start | bytes 1348
  72.8 23.7 %collective-permute-start.16 = (bf16[448,4096]{1,0:T(8,128)(2,1)S(1)}, bf16[448,4096]{1,0:T(8,128)(2,1)S(1)}, u32[]{:S(2)}, u32[]{:S(2)}) collective-permute-start(bf16[448,4096]{1,0:T(8,128)(2,1)S(1)} %get-tuple-element.102.n_ref), channel_id=1, source_target_pairs={{0,128},{128,0},{1,129},{129,1},{2,130},{130,2},{3,131},{131,3},{4... | collective-permute-start | bytes 11010056 | tf_op jit(solution)/shard_map/ppermute | solution.py:24
  100.6 7.3 %copy-start.7 = (f32[1,128]{1,0:T(1,128)}, f32[1,128]{1,0:T(1,128)S(1)}, u32[]{:S(2)}) copy-start(f32[1,128]{1,0:T(1,128)S(1)} %get-tuple-element.108.loss_ref) | copy-start | bytes 1540
  100.6 14.2 %collective-permute-start.21 = (bf16[448,512]{1,0:T(8,128)(2,1)S(1)}, bf16[448,512]{1,0:T(8,128)(2,1)S(1)}, u32[]{:S(2)}, u32[]{:S(2)}) collective-permute-start(bf16[448,512]{1,0:T(8,128)(2,1)S(1)} %get-tuple-element.122), channel_id=1, source_target_pairs={{0,128},{128,0},{1,129},{129,1},{2,130},{130,2},{3,131},{131,3},{4... | collective-permute-start | bytes 1376264 | tf_op jit(solution)/shard_map/ppermute | solution.py:24
  102.5 12.3 %collective-permute-start.17 = (bf16[912,128]{1,0:T(8,128)(2,1)S(1)}, bf16[912,128]{1,0:T(8,128)(2,1)S(1)}, u32[]{:S(2)}, u32[]{:S(2)}) collective-permute-start(bf16[912,128]{1,0:T(8,128)(2,1)S(1)} %get-tuple-element.118), channel_id=1, source_target_pairs={{0,1},{1,2},{2,3},{3,0},{4,5},{5,6},{6,7},{7,4},{8,9},{9,10},{10,1... | collective-permute-start | bytes 700424 | tf_op jit(solution)/shard_map/ppermute | solution.py:24
  102.7 12.0 %collective-permute-start.18 = (bf16[896,128]{1,0:T(8,128)(2,1)S(1)}, bf16[896,128]{1,0:T(8,128)(2,1)S(1)}, u32[]{:S(2)}, u32[]{:S(2)}) collective-permute-start(bf16[896,128]{1,0:T(8,128)(2,1)S(1)} %get-tuple-element.119), channel_id=1, source_target_pairs={{0,3},{1,0},{2,1},{3,2},{4,7},{5,4},{6,5},{7,6},{8,11},{9,8},{10,9... | collective-permute-start | bytes 688136 | tf_op jit(solution)/shard_map/ppermute | solution.py:24
  105.2 9.6 %collective-permute-start.19 = (bf16[896,128]{1,0:T(8,128)(2,1)S(1)}, bf16[896,128]{1,0:T(8,128)(2,1)S(1)}, u32[]{:S(2)}, u32[]{:S(2)}) collective-permute-start(bf16[896,128]{1,0:T(8,128)(2,1)S(1)} %get-tuple-element.120), channel_id=1, source_target_pairs={{0,4},{4,8},{8,12},{12,0},{1,5},{5,9},{9,13},{13,1},{2,6},{6,10},{... | collective-permute-start | bytes 688136 | tf_op jit(solution)/shard_map/ppermute | solution.py:24
  105.5 9.3 %collective-permute-start.20 = (bf16[896,128]{1,0:T(8,128)(2,1)S(1)}, bf16[896,128]{1,0:T(8,128)(2,1)S(1)}, u32[]{:S(2)}, u32[]{:S(2)}) collective-permute-start(bf16[896,128]{1,0:T(8,128)(2,1)S(1)} %get-tuple-element.121), channel_id=1, source_target_pairs={{0,12},{4,0},{8,4},{12,8},{1,13},{5,1},{9,5},{13,9},{2,14},{6,2},{... | collective-permute-start | bytes 688136 | tf_op jit(solution)/shard_map/ppermute | solution.py:24
  115.0 14.4 %collective-permute-start.23 = (bf16[1872,128]{1,0:T(8,128)(2,1)S(1)}, bf16[1872,128]{1,0:T(8,128)(2,1)S(1)}, u32[]{:S(2)}, u32[]{:S(2)}) collective-permute-start(bf16[1872,128]{1,0:T(8,128)(2,1)S(1)} %get-tuple-element.131), channel_id=1, source_target_pairs={{0,1},{1,2},{2,3},{3,0},{4,5},{5,6},{6,7},{7,4},{8,9},{9,10},{10,1... | collective-permute-start | bytes 1437704 | tf_op jit(solution)/shard_map/ppermute | solution.py:24
  115.1 14.3 %collective-permute-start.24 = (bf16[1872,128]{1,0:T(8,128)(2,1)S(1)}, bf16[1872,128]{1,0:T(8,128)(2,1)S(1)}, u32[]{:S(2)}, u32[]{:S(2)}) collective-permute-start(bf16[1872,128]{1,0:T(8,128)(2,1)S(1)} %get-tuple-element.132), channel_id=1, source_target_pairs={{0,3},{1,0},{2,1},{3,2},{4,7},{5,4},{6,5},{7,6},{8,11},{9,8},{10,9... | collective-permute-start | bytes 1437704 | tf_op jit(solution)/shard_map/ppermute | solution.py:24
  117.9 11.5 %collective-permute-start.25 = (bf16[1792,128]{1,0:T(8,128)(2,1)S(1)}, bf16[1792,128]{1,0:T(8,128)(2,1)S(1)}, u32[]{:S(2)}, u32[]{:S(2)}) collective-permute-start(bf16[1792,128]{1,0:T(8,128)(2,1)S(1)} %get-tuple-element.137), channel_id=1, source_target_pairs={{0,4},{4,8},{8,12},{12,0},{1,5},{5,9},{9,13},{13,1},{2,6},{6,10},{... | collective-permute-start | bytes 1376264 | tf_op jit(solution)/shard_map/ppermute | solution.py:24
  118.0 11.5 %collective-permute-start.26 = (bf16[1792,128]{1,0:T(8,128)(2,1)S(1)}, bf16[1792,128]{1,0:T(8,128)(2,1)S(1)}, u32[]{:S(2)}, u32[]{:S(2)}) collective-permute-start(bf16[1792,128]{1,0:T(8,128)(2,1)S(1)} %get-tuple-element.138), channel_id=1, source_target_pairs={{0,12},{4,0},{8,4},{12,8},{1,13},{5,1},{9,5},{13,9},{2,14},{6,2},{... | collective-permute-start | bytes 1376264 | tf_op jit(solution)/shard_map/ppermute | solution.py:24
  120.6 8.8 %collective-permute-start.22 = (f32[32,128]{1,0:T(8,128)S(1)}, f32[32,128]{1,0:T(8,128)S(1)}, u32[]{:S(2)}, u32[]{:S(2)}) collective-permute-start(f32[32,128]{1,0:T(8,128)S(1)} %get-tuple-element.129.mine), channel_id=1, source_target_pairs={{0,2},{1,3},{2,0},{3,1},{4,6},{5,7},{6,4},{7,5},{8,10},{9,11},{10,... | collective-permute-start | bytes 49160 | tf_op jit(solution)/shard_map/ppermute | solution.py:24
  130.4 4.6 %collective-permute-start.30 = (bf16[448,128]{1,0:T(8,128)(2,1)S(1)}, bf16[448,128]{1,0:T(8,128)(2,1)S(1)}, u32[]{:S(2)}, u32[]{:S(2)}) collective-permute-start(bf16[448,128]{1,0:T(8,128)(2,1)S(1)} %get-tuple-element.154), channel_id=1, source_target_pairs={{0,3},{1,0},{2,1},{3,2},{4,7},{5,4},{6,5},{7,6},{8,11},{9,8},{10,9... | collective-permute-start | bytes 344072 | tf_op jit(solution)/shard_map/ppermute | solution.py:24
  131.1 9.9 %collective-permute-start.27 = (bf16[480,128]{1,0:T(8,128)(2,1)S(1)}, bf16[480,128]{1,0:T(8,128)(2,1)S(1)}, u32[]{:S(2)}, u32[]{:S(2)}) collective-permute-start(bf16[480,128]{1,0:T(8,128)(2,1)S(1)} %get-tuple-element.150), channel_id=1, source_target_pairs={{0,4},{4,8},{8,12},{12,0},{1,5},{5,9},{9,13},{13,1},{2,6},{6,10},{... | collective-permute-start | bytes 368648 | tf_op jit(solution)/shard_map/ppermute | solution.py:24
  131.1 9.9 %collective-permute-start.28 = (bf16[480,128]{1,0:T(8,128)(2,1)S(1)}, bf16[480,128]{1,0:T(8,128)(2,1)S(1)}, u32[]{:S(2)}, u32[]{:S(2)}) collective-permute-start(bf16[480,128]{1,0:T(8,128)(2,1)S(1)} %get-tuple-element.151), channel_id=1, source_target_pairs={{0,8},{4,12},{8,0},{12,4},{1,9},{5,13},{9,1},{13,5},{2,10},{6,14},... | collective-permute-start | bytes 368648 | tf_op jit(solution)/shard_map/ppermute | solution.py:24
  134.3 6.7 %collective-permute-start.29 = (bf16[480,128]{1,0:T(8,128)(2,1)S(1)}, bf16[480,128]{1,0:T(8,128)(2,1)S(1)}, u32[]{:S(2)}, u32[]{:S(2)}) collective-permute-start(bf16[480,128]{1,0:T(8,128)(2,1)S(1)} %get-tuple-element.152), channel_id=1, source_target_pairs={{0,12},{4,0},{8,4},{12,8},{1,13},{5,1},{9,5},{13,9},{2,14},{6,2},{... | collective-permute-start | bytes 368648 | tf_op jit(solution)/shard_map/ppermute | solution.py:24
  134.3 5.2 %collective-permute-start.31 = (bf16[448,128]{1,0:T(8,128)(2,1)S(1)}, bf16[448,128]{1,0:T(8,128)(2,1)S(1)}, u32[]{:S(2)}, u32[]{:S(2)}) collective-permute-start(bf16[448,128]{1,0:T(8,128)(2,1)S(1)} %get-tuple-element.155), channel_id=1, source_target_pairs={{0,2},{1,3},{2,0},{3,1},{4,6},{5,7},{6,4},{7,5},{8,10},{9,11},{10,... | collective-permute-start | bytes 344072 | tf_op jit(solution)/shard_map/ppermute | solution.py:24
  135.0 6.0 %collective-permute-start.32 = (bf16[448,128]{1,0:T(8,128)(2,1)S(1)}, bf16[448,128]{1,0:T(8,128)(2,1)S(1)}, u32[]{:S(2)}, u32[]{:S(2)}) collective-permute-start(bf16[448,128]{1,0:T(8,128)(2,1)S(1)} %get-tuple-element.156), channel_id=1, source_target_pairs={{0,1},{1,2},{2,3},{3,0},{4,5},{5,6},{6,7},{7,4},{8,9},{9,10},{10,1... | collective-permute-start | bytes 344072 | tf_op jit(solution)/shard_map/ppermute | solution.py:24
  155.3 6.6 %collective-permute-start.33 = (f32[2,128]{1,0:T(2,128)}, f32[2,128]{1,0:T(2,128)S(1)}, u32[]{:S(2)}, u32[]{:S(2)}) collective-permute-start(f32[2,128]{1,0:T(2,128)} %get-tuple-element.159), channel_id=1, source_target_pairs={{0,128},{128,0},{1,129},{129,1},{2,130},{130,2},{3,131},{131,3},{4... | collective-permute-start | bytes 3080 | tf_op jit(solution)/shard_map/ppermute | solution.py:24
where the time goes:
time: 166 us; the launch traced here: 165 us
  starting transfers between devices  56.6 us (34%)
  waiting for transfers between devices  33.2 us (20%)
  Pallas kernels  32.4 us (20%)
  blocking collectives  32.2 us (19%)
  local copies, waits for them, and re-layouts  6.79 us (4%)
  between operations  2.7 us (2%)
    ppermute x34, starting transfers between devices, shift(): return lax.ppermute(x, axis, [(i, (i + k) % n) for i in range(n)])  50.2 us
    ppermute x34, waiting for transfers between devices, shift(): return lax.ppermute(x, axis, [(i, (i + k) % n) for i in range(n)])  22.7 us
    all_to_all x1, blocking collectives, body(): every = lax.all_to_all(share, ('z', 'y', 'x'), 0, 0)  19.8 us
    all_to_all x1, blocking collectives, body(): total = lax.all_to_all(total, 'z', 0, 0)  12.4 us
    all_to_all x1, waiting for transfers between devices, body(): block = lax.all_to_all(block, 'z', 0, 0)  10.4 us
    pallas_call x1, Pallas kernels, forward(): pl.pallas_call(functools.partial(forward_kernel, Zh), out_shape=(jax.Shap...  9.22 us
    pallas_call x1, Pallas kernels, outer(): pl.pallas_call(outer_kernel, grid=(D // wide,), out_shape=jax.ShapeDtypeS...  7.42 us
    pallas_call x1, Pallas kernels, near_rows(): pl.pallas_call(functools.partial(near_kernel, Zh), out_shape=(*(jax.Shape...  6.93 us
  transfers between devices with their start and end apart: 35, of which 12 were waited for; matrix products, arithmetic and copies ran while one was open for 2% of the time, Pallas kernels for 10%

commit v1 on v0

--- a/solution.py
+++ b/solution.py
@@ -31,14 +31,11 @@
     return block, one, three, *two
 
 
-def pick(refs, outer, inner, z, Zh):
-    if outer == 2:
-        ref = refs[3 + inner // 2]
-        inner = inner % 2
-    else:
-        ref = refs[(0, 1, None, 2)[outer]]
-    at = pl.multiple_of((inner * Zh + z) * LIVE, 16)
-    return ref[pl.ds(at, LIVE), :].astype(f32)
+PARTS = ((0, 0, 4), (1, 0, 4), (3, 0, 4), (2, 0, 2), (2, 2, 4))
+
+
+def spot_of(j):
+    return jnp.where(j < 2, j, 5 - j)
 
 
 def same():
@@ -59,54 +56,82 @@
     return lax.rem(x - ORDER[p] + R, R)
 
 
-def forward_kernel(Zh, place_ref, w0_ref, w1_ref, *refs):
-    gains, a_refs, b_refs = refs[:R], refs[R : R + 5], refs[R + 5 : R + 10]
-    n_ref, inv_ref, l_ref, share_ref, w_ref, w_sems = refs[R + 10 :]
+def forward_kernel(Zh, place_ref, w0_ref, w1_ref, gain_ref, *refs):
+    a_refs, b_refs = refs[:5], refs[5:10]
+    n_ref, inv_ref, l_ref, share_ref, w_ref, total_ref, w_sems = refs[10:]
     Z = 2 * Zh
     V = w0_ref.shape[0]
-    tile = 2 * V // 2
     copies = [
         pltpu.make_async_copy(w, w_ref.at[i], w_sems.at[i]) for i, w in enumerate((w0_ref, w1_ref))
     ]
     for copy in copies:
         copy.start()
-    for p, j in enumerate(ORDER):
-        rows = slice(p * LIVE, (p + 1) * LIVE)
-
-        def square(z, total):
-            for k in range(R):
-                for refs, outer, at in ((a_refs, j, k), (b_refs, k, j)):
-                    block = pick(refs, outer, at, z, Zh)
-                    total = total + block * block
-            return total
-
-        total = lax.fori_loop(0, Zh, square, jnp.zeros((LIVE, 128), f32))
-        mean_square = jnp.sum(total, axis=1, keepdims=True) / (Z * R * 128)
+
+    def load(ref, i, z):
+        at = pl.multiple_of((i * Zh + z) * LIVE, 16)
+        return ref[pl.ds(at, LIVE), :].astype(f32)
+
+    def squares(ref, i):
+        def add(z, total):
+            block = load(ref, i, z)
+            return total + block * block
+
+        return lax.fori_loop(0, Zh, add, jnp.zeros((LIVE, 128), f32), unroll=True)
+
+    total_ref[...] = jnp.zeros_like(total_ref)
+    for ref, (j, first, last) in zip(a_refs, PARTS):
+        add = lambda i, total, ref=ref: total + squares(ref, i)
+        p = ORDER.index(j)
+        total_ref[p] = lax.fori_loop(0, last - first, add, total_ref[p])
+    for ref, (_, first, last) in zip(b_refs, PARTS):
+
+        def add(i, _, ref=ref, first=first):
+            p = spot_of(first + i)
+            total_ref[p] = total_ref[p] + squares(ref, i)
+            return 0
+
+        lax.fori_loop(0, last - first, add, 0)
+    for p in range(R):
+        mean_square = jnp.sum(total_ref[p], axis=1, keepdims=True) / (Z * R * 128)
         inv = lax.rsqrt(mean_square + epsilon)
-        if j == 0:
+        if p == 0:
             inv_ref[...] = inv
-        wide = jnp.broadcast_to(inv, (LIVE, 128))
-
-        def scale(z, _):
-            for k in range(R):
-                y = lax.rem(place_ref[0] - k + R, R)
-                for half, refs, outer, at in ((0, a_refs, j, k), (1, b_refs, k, j)):
-                    t = half * Zh + z
-                    line = pl.multiple_of(Zh * LIVE + t * 16, 16)
-                    pieces = gains[k][pl.ds(line, 16), :].astype(f32)
-                    gain = pieces[0:1] + pieces[1:2] + pieces[2:3]
-                    column = pl.multiple_of((t * R + y) * 128, 128)
-                    n_ref[rows, pl.ds(column, 128)] = (
-                        pick(refs, outer, at, z, Zh) * wide * gain
-                    ).astype(bf16)
+        total_ref[p] = jnp.broadcast_to(inv, (LIVE, 128))
+
+    def scale(ref, i, k, p, half):
+        inv = total_ref[p]
+        y = lax.rem(place_ref[0] - k + R, R)
+        rows = pl.ds(pl.multiple_of(p * LIVE, 16), LIVE)
+
+        def one(z, _):
+            t = half * Zh + z
+            column = pl.multiple_of((t * R + y) * 128, 128)
+            n_ref[rows, pl.ds(column, 128)] = (
+                load(ref, i, z) * inv * gain_ref[pl.ds(k * Z + t, 1), :]
+            ).astype(bf16)
             return 0
 
-        lax.fori_loop(0, Zh, scale, 0)
+        lax.fori_loop(0, Zh, one, 0, unroll=True)
+
+    for ref, (j, first, last) in zip(a_refs, PARTS):
+
+        def one(i, _, ref=ref, j=j, first=first):
+            scale(ref, i, first + i, ORDER.index(j), 0)
+            return 0
+
+        lax.fori_loop(0, last - first, one, 0)
+    for ref, (k, first, last) in zip(b_refs, PARTS):
+
+        def one(i, _, ref=ref, k=k, first=first):
+            scale(ref, i, k, spot_of(first + i), 1)
+            return 0
+
+        lax.fori_loop(0, last - first, one, 0)
 
     def logits_of(q, _):
         pltpu.make_async_copy(w0_ref, w_ref.at[q], w_sems.at[q]).wait()
-        l_ref[:, pl.ds(pl.multiple_of(q * tile, tile), tile)] = lax.dot_general(
-            n_ref[...], w_ref[q], (((1,), (1,)), ((), ())), preferred_element_type=f32
+        l_ref[:, pl.ds(pl.multiple_of(q * V, V), V)] = lax.dot_general(
+            n_ref[:, 0 : w_ref.shape[2]], w_ref[q], (((1,), (1,)), ((), ())), preferred_element_type=f32
         )
         return 0
 
@@ -121,21 +146,22 @@
     share_ref[...] = jnp.broadcast_to(share[None], share_ref.shape)
 
 
-def forward(place, Zh, w0, w1, gains, a, b):
+def forward(place, Zh, w0, w1, gain, a, b):
     V, D = w0.shape
     rows = R * LIVE
     return pl.pallas_call(
         functools.partial(forward_kernel, Zh),
         out_shape=(
-            jax.ShapeDtypeStruct((rows, D), bf16),
+            jax.ShapeDtypeStruct((rows, D + V), bf16),
             jax.ShapeDtypeStruct((LIVE, 1), f32),
             jax.ShapeDtypeStruct((rows, 2 * V), f32),
             jax.ShapeDtypeStruct((2 * Zh * R * R, R, 128), f32),
         ),
-        in_specs=[SMEM, HBM, HBM] + [VMEM] * (R + 10),
+        in_specs=[SMEM, HBM, HBM] + [VMEM] * 11,
         out_specs=(VMEM,) * 4,
         scratch_shapes=[
             pltpu.VMEM((2, V, D), bf16),
+            pltpu.VMEM((R, LIVE, 128), f32),
             pltpu.SemaphoreType.DMA((2,)),
         ],
         compiler_params=pltpu.CompilerParams(vmem_limit_bytes=28 << 20),
@@ -143,7 +169,7 @@
             flops=4 * rows * V * D, bytes_accessed=4 * V * D, transcendentals=2 * rows * V
         ),
         name="forward",
-    )(place, w0, w1, *gains, *a, *b)
+    )(place, w0, w1, gain, *a, *b)
 
 
 def split_tile(rows):
@@ -163,7 +189,7 @@
 
 
 def soft_kernel(Zh, place_ref, w0_ref, w1_ref, every_ref, l_ref, n_ref, label_ref, live_ref, factor_ref, *refs):
-    g_ref, g1_ref, side_ref, loss_ref, gain_ref, a_low, a_high, b_low, b_high = refs[:9]
+    g_ref, ng_ref, side_ref, loss_ref, gain_ref, a_low, a_high, b_low, b_high = refs[:9]
     wa_ref, wb_ref, sems = refs[9:]
     V = w0_ref.shape[0]
     far = lax.rem(place_ref[0] + 2, R)
@@ -205,7 +231,7 @@
         grad = jnp.exp(logits - to_column(total)) - jnp.where(match, 1.0, 0.0)
         grad = grad * to_column(pick_row(factor_ref))
         g_ref[rows, :] = grad.astype(bf16)
-        g1_ref[rows, :] = grad[:, V:].astype(bf16)
+        ng_ref[rows, pl.ds(w0_ref.shape[1], V)] = grad[:, V:].astype(bf16)
         line = to_row(jnp.sum(grad * logits, axis=1, keepdims=True))
         inner = jnp.where(place == p, line, inner)
         own = jnp.sum(jnp.where(match, logits, 0.0), axis=1, keepdims=True) * to_column(live)
@@ -247,7 +273,7 @@
     V = w0.shape[0]
     rows = logits.shape[0]
     half = Zh // 2 * R * LIVE
-    shapes = [((rows, 2 * V), bf16), ((rows, V), bf16), ((R, 16, 128), bf16), ((1, 128), f32)]
+    shapes = [((rows, 2 * V), bf16), (normed.shape, bf16), ((R, 16, 128), bf16), ((1, 128), f32)]
     shapes += [((2 * Zh * R, 128), f32)]
     shapes += [((half + 16, 128), bf16)] + [((half, 128), bf16)] * 3
     return pl.pallas_call(
@@ -260,6 +286,7 @@
             pltpu.VMEM((2 * V, Zh * 128), bf16),
             pltpu.SemaphoreType.DMA((1 + Zh, 2)),
         ],
+        input_output_aliases={5: 1},
         compiler_params=pltpu.CompilerParams(vmem_limit_bytes=20 << 20),
         name="soft_rows",
     )(place, w0, w1, every, logits, normed, labels, live, factor)
@@ -518,11 +545,17 @@
 
 
 def meta_kernel(at, w_ref, *refs):
-    label_ref, live_ref, factor_ref, total_ref = refs[R:]
+    tiles, a_refs = refs[:R], refs[R : 2 * R]
+    label_ref, live_ref, factor_ref, total_ref, gain_ref = refs[2 * R :]
+    Z = gain_ref.shape[0] // R
+    for k, ref in enumerate(a_refs):
+        for z in range(Z):
+            pieces = ref[at + z * 16 : at + (z + 1) * 16, :].astype(f32)
+            gain_ref[k * Z + z : k * Z + z + 1, :] = pieces[0:1] + pieces[1:2] + pieces[2:3]
     place = lax.broadcasted_iota(jnp.int32, (R, 128), 0)
     labels, live, total = jnp.zeros((R, 128), f32), jnp.zeros((R, 128), f32), jnp.zeros((1, 1), f32)
     for p, j in enumerate(ORDER):
-        tile = refs[j][at : at + 16, :].astype(f32)
+        tile = tiles[j][at : at + 16, :].astype(f32)
         label = tile[0:1] * 65536 + tile[1:2] * 256 + tile[2:3]
         labels = jnp.where(place == p, label, labels)
         live = jnp.where(place == p, tile[3:4], live)
@@ -533,16 +566,22 @@
     total_ref[...] = jnp.broadcast_to(total, (1, 128))
 
 
-def read_meta(at, weight, blocks):
+def read_meta(at, weight, Z, blocks, a_blocks):
     line = jax.ShapeDtypeStruct((R, 128), f32)
     return pl.pallas_call(
         functools.partial(meta_kernel, at),
-        out_shape=(line, line, line, jax.ShapeDtypeStruct((1, 128), f32)),
-        in_specs=[VMEM] * (1 + R),
-        out_specs=(VMEM,) * 4,
+        out_shape=(
+            line,
+            line,
+            line,
+            jax.ShapeDtypeStruct((1, 128), f32),
+            jax.ShapeDtypeStruct((R * Z, 128), f32),
+        ),
+        in_specs=[VMEM] * (1 + 2 * R),
+        out_specs=(VMEM,) * 5,
         compiler_params=pltpu.CompilerParams(vmem_limit_bytes=SCOPED),
         name="read_meta",
-    )(weight, *blocks)
+    )(weight, *blocks, *a_blocks)
 
 
 def outer_kernel(g_ref, h_ref, n_ref, m_ref, out_ref, g_turned, h_turned):
@@ -558,24 +597,43 @@
     out_ref[...] = total.astype(bf16)
 
 
-def outer(g, h, n, m):
-    rows, V = h.shape
-    D, wide = n.shape[1], 512
-    whole = lambda a: pl.BlockSpec(a.shape, lambda i: (0, 0))
-    part = pl.BlockSpec((rows, wide), lambda i: (0, i))
+def outer(g, ours, theirs, D):
+    rows, V = g.shape[0], g.shape[1] // 2
+    part = pl.BlockSpec((rows, V), lambda i: (0, i))
     return pl.pallas_call(
         outer_kernel,
-        grid=(D // wide,),
+        grid=(D // V,),
         out_shape=jax.ShapeDtypeStruct((V, D), bf16),
-        in_specs=[whole(g), whole(h), part, part],
-        out_specs=pl.BlockSpec((V, wide), lambda i: (0, i)),
+        in_specs=[
+            pl.BlockSpec(g.shape, lambda i: (0, 0)),
+            pl.BlockSpec((rows, V), lambda i: (0, D // V)),
+            part,
+            part,
+        ],
+        out_specs=pl.BlockSpec((V, V), lambda i: (0, i)),
         scratch_shapes=[pltpu.VMEM((V, rows), bf16)] * 2,
         compiler_params=pltpu.CompilerParams(vmem_limit_bytes=SCOPED),
         cost_estimate=pl.CostEstimate(
             flops=4 * rows * V * D, bytes_accessed=8 * V * D, transcendentals=0
         ),
         name="outer",
-    )(g, h, n, m)
+    )(g, theirs, ours, theirs)
+
+
+def last_kernel(sums_ref, came_ref, total_ref, gain_ref, loss_ref):
+    sums = sums_ref[...] + came_ref[...]
+    gain_ref[...] = sums[0:1]
+    loss_ref[...] = sums[1:2, 0:1] / total_ref[:, 0:1]
+
+
+def last(sums, came, total):
+    return pl.pallas_call(
+        last_kernel,
+        out_shape=(jax.ShapeDtypeStruct((1, 128), f32), jax.ShapeDtypeStruct((1, 1), f32)),
+        in_specs=[VMEM] * 3,
+        out_specs=(VMEM, VMEM),
+        name="last",
+    )(sums, came, total)
 
 
 def finish_kernel(D, loss_ref, total_ref, hidden_ref, gain_ref, inv_ref, out_ref, sums_ref):
@@ -630,34 +688,34 @@
     b_blocks = [b_block] + [shift(b_block, "x", k) for k in range(1, R)]
     a_all = ring_gather(jnp.concatenate([a[: Zh * LIVE] for a in a_blocks]), "x")
     b_all = ring_gather(jnp.concatenate([b[: Zh * LIVE] for b in b_blocks]), "y")
-    labels, live, factor, live_total = read_meta(Zh * LIVE, head_weight, b_blocks)
-    a_all, b_all, labels, live, factor = lax.optimization_barrier(
-        (a_all, b_all, labels, live, factor)
+    labels, live, factor, live_total, gain = read_meta(
+        Zh * LIVE, head_weight, Z, b_blocks, a_blocks
     )
+    a_all, b_all, labels, live, factor, gain = lax.optimization_barrier(
+        (a_all, b_all, labels, live, factor, gain)
+    )
 
     weights = (head_weight, weight_other)
-    normed_all, inv_rms, logits, share = forward(place, Zh, *weights, a_blocks, a_all, b_all)
-    normed_other = shift(normed_all, "c", 1)
+    normed, inv_rms, logits, share = forward(place, Zh, *weights, gain, a_all, b_all)
     every = lax.all_to_all(share, ("z", "y", "x"), 0, 0)
-    every, normed_other = lax.optimization_barrier((every, normed_other))
-    g, g1, side, loss, gain_far, a_low, a_high, b_low, b_high = soft_rows(
-        place, Zh, *weights, every, logits, normed_all, labels, live, factor
+    g, normed, side, loss, gain_far, a_low, a_high, b_low, b_high = soft_rows(
+        place, Zh, *weights, every, logits, normed, labels, live, factor
     )
 
     a_low, a_high = shift(a_low, "x", 1), shift(a_high, "x", -1)
     b_low, b_high = shift(b_low, "y", 1), shift(b_high, "y", -1)
-    near = near_rows(place, Zh, *weights, side, g, normed_all)
-    g_other = shift(g1, "c", 1)
-    near, a_low, a_high, b_low, b_high, g, g_other = lax.optimization_barrier(
-        (near, a_low, a_high, b_low, b_high, g, g_other)
+    near = near_rows(place, Zh, *weights, side, g, normed)
+    near, a_low, a_high, b_low, b_high, g, normed = lax.optimization_barrier(
+        (near, a_low, a_high, b_low, b_high, g, normed)
     )
+    theirs = shift(normed, "c", 1)
     a0, a1, a3, b0, b1, b3, gain_near = near
     a_up, a_down, gain = relay(a3, a1, a_low, a_high, gain_far, gain_near)
     b_up, b_down = relay(b1, b3, b_low, b_high)
     a_in = shift(a_up, "x", 1), shift(a_down, "x", -1)
     b_in = shift(b_up, "y", 1), shift(b_down, "y", -1)
     gain_in = shift(gain, "x", 2)
-    weight_grad = outer(g, g_other, normed_all, normed_other)
+    weight_grad = outer(g, normed, theirs, D)
     a_in, b_in, weight_grad = lax.optimization_barrier((a_in, b_in, weight_grad))
     outs = turn_rows(place, Zh, side, gain, gain_in, (a0, *a_in), (b0, *b_in))
     a_sums = [outs[0]] + [shift(outs[k], "y", k) for k in range(1, R)]
@@ -666,9 +724,8 @@
     total = lax.all_to_all(total, "z", 0, 0)
     hidden_grad, sums = finish(D, loss, total, hidden, norm_gain, inv_rms)
 
-    sums = sums + shift(sums, "c", 1)
-    gain_grad = sums[0]
-    mean_loss = sums[1, 0] / live_total[0, 0]
+    gain_grad, mean_loss = last(sums, shift(sums, "c", 1), live_total)
+    gain_grad, mean_loss = gain_grad.reshape(128), mean_loss.reshape(())
     return (hidden_grad, gain_grad, weight_grad, mean_loss)
 
 

time: 166 us -> 162 us (0.976)
  between operations: 2.7 us -> 0.88 us
  waiting for transfers between devices: 33.2 us -> 34.9 us
    ppermute x34 -> x33, waiting for transfers between devices: 22.7 us -> 24.5 us  [shift(): return lax.ppermute(x, axis, [(i, (i + k) % n) for i in range(n)])]
    all_to_all x1, blocking collectives: 19.8 us -> 18.1 us  [body(): every = lax.all_to_all(share, ('z', 'y', 'x'), 0, 0)]
    pallas_call x1 -> x2, Pallas kernels: 7.42 us -> 8.67 us  [the longest x1 7.47 us: outer(): pl.pallas_call(outer_kernel, grid=(D // V,), out_shape=jax.ShapeDtypeStru...]
    ppermute x34 -> x33, starting transfers between devices: 50.2 us -> 49 us  [shift(): return lax.ppermute(x, axis, [(i, (i + k) % n) for i in range(n)])]
  transfers between devices with their start and end apart: 35 -> 34, of which waited for: 12 -> 13; matrix products, arithmetic and copies ran while one was open for 2% -> 2% of each run, Pallas kernels for 10% -> 10%
where the time goes in v1:
time: 162 us
  starting transfers between devices  55.5 us (34%)
  waiting for transfers between devices  34.9 us (22%)
  Pallas kernels  32.7 us (20%)
  blocking collectives  30.7 us (19%)
  local copies, waits for them, and re-layouts  6.45 us (4%)
    ppermute x33, starting transfers between devices, shift(): return lax.ppermute(x, axis, [(i, (i + k) % n) for i in range(n)])  49 us
    ppermute x33, waiting for transfers between devices, shift(): return lax.ppermute(x, axis, [(i, (i + k) % n) for i in range(n)])  24.5 us
    all_to_all x1, blocking collectives, body(): every = lax.all_to_all(share, ('z', 'y', 'x'), 0, 0)  18.1 us
    all_to_all x1, blocking collectives, body(): total = lax.all_to_all(total, 'z', 0, 0)  12.6 us
    all_to_all x1, waiting for transfers between devices, body(): block = lax.all_to_all(block, 'z', 0, 0)  10.4 us
    pallas_call x1, Pallas kernels, forward(): pl.pallas_call(functools.partial(forward_kernel, Zh), out_shape=(jax.Shap...  8.36 us
    pallas_call x1, Pallas kernels, outer(): pl.pallas_call(outer_kernel, grid=(D // V,), out_shape=jax.ShapeDtypeStru...  7.47 us
    pallas_call x1, Pallas kernels, near_rows(): pl.pallas_call(functools.partial(near_kernel, Zh), out_shape=(*(jax.Shape...  6.86 us
  transfers between devices with their start and end apart: 34, of which 13 were waited for; matrix products, arithmetic and copies ran while one was open for 2% of the time, Pallas kernels for 10%

profile of v1, /device:TPU:1, one launch (start us, length us, event | category | flops | bytes accessed | tf_op | source)
XLA Modules:
  0.0 162.0 jit_solution(11661191005802038481)
XLA Ops:
  0.6 3.3 %collective-permute-start = (bf16[512,4096]{1,0:T(8,128)(2,1)}, bf16[512,4096]{1,0:T(8,128)(2,1)}, u32[]{:S(2)}, u32[]{:S(2)}) collective-permute-start(bf16[512,4096]{1,0:T(8,128)(2,1)} %w0_ref.5), channel_id=1, source_target_pairs={{0,128},{128,0},{1,129},{129,1},{2,130},{130,2},{3,131},{131,3},{4... | collective-permute-start | bytes 12582920 | tf_op jit(solution)/shard_map/ppermute | solution.py:24
  4.0 1.5 prepare.1
  5.5 6.5 %all-to-all-start = ((bf16[8,128,128]{2,1,0:T(8,128)(2,1)}), bf16[8,128,128]{2,1,0:T(8,128)(2,1)S(1)}, u32[]{:S(2)}, u32[]{:S(2)}) async-start(bf16[8,128,128]{2,1,0:T(8,128)(2,1)} %get-tuple-element.85), calls=%async_computation | async-start | bytes 524288 | tf_op jit(solution)/shard_map/all_to_all | solution.py:679
  11.9 0.3 collective-permute-start.1
  12.2 1.0 collective-permute-done.1
  13.2 0.7 pad_add_fusion
  13.9 10.4 %all-to-all-done = bf16[8,128,128]{2,1,0:T(8,128)(2,1)S(1)} async-done(((bf16[8,128,128]{2,1,0:T(8,128)(2,1)}), bf16[8,128,128]{2,1,0:T(8,128)(2,1)S(1)}, u32[]{:S(2)}, u32[]{:S(2)}) %all-to-all-start) | async-done | bytes 262176 | tf_op jit(solution)/shard_map/all_to_all | solution.py:679
  24.4 2.6 %collective-permute-start.11 = (bf16[464,128]{1,0:T(8,128)(2,1)S(1)}, bf16[464,128]{1,0:T(8,128)(2,1)S(1)}, u32[]{:S(2)}, u32[]{:S(2)}) collective-permute-start(bf16[464,128]{1,0:T(8,128)(2,1)S(1)} %pad_maximum_fusion.3.refs_0_), channel_id=1, source_target_pairs={{0,3},{1,0},{2,1},{3,2},{4,7},{5,4},{6,5},{7,6},{8,11},{9,8},{10,9... | collective-permute-start | bytes 356360 | tf_op jit(solution)/shard_map/ppermute | solution.py:24
  26.9 0.5 collective-permute-start.10
  27.4 0.6 collective-permute-start.9
  28.1 2.8 %collective-permute-start.4 = (bf16[576,128]{1,0:T(8,128)(2,1)S(1)}, bf16[576,128]{1,0:T(8,128)(2,1)S(1)}, u32[]{:S(2)}, u32[]{:S(2)}) collective-permute-start(bf16[576,128]{1,0:T(8,128)(2,1)S(1)} %pad_maximum_fusion.2.refs_4_), channel_id=1, source_target_pairs={{0,12},{4,0},{8,4},{12,8},{1,13},{5,1},{9,5},{13,9},{2,14},{6,2},{... | collective-permute-start | bytes 442376 | tf_op jit(solution)/shard_map/ppermute | solution.py:24
  30.9 0.3 collective-permute-start.3
  31.2 0.7 collective-permute-start.2
  31.9 0.5 collective-permute-done.10.refs_2_
  32.4 3.6 %collective-permute-done.9.refs_1_ = bf16[464,128]{1,0:T(8,128)(2,1)S(1)} collective-permute-done((bf16[464,128]{1,0:T(8,128)(2,1)S(1)}, bf16[464,128]{1,0:T(8,128)(2,1)S(1)}, u32[]{:S(2)}, u32[]{:S(2)}) %collective-permute-start.9) | collective-permute-done | bytes 118816 | tf_op jit(solution)/shard_map/ppermute | solution.py:24
  36.1 2.8 %collective-permute-start.13 = (bf16[1792,128]{1,0:T(8,128)(2,1)S(1)}, bf16[1792,128]{1,0:T(8,128)(2,1)S(1)}, u32[]{:S(2)}, u32[]{:S(2)}) collective-permute-start(bf16[1792,128]{1,0:T(8,128)(2,1)S(1)} %pad_maximum_fusion.1.refs_5_), channel_id=1, source_target_pairs={{0,12},{4,0},{8,4},{12,8},{1,13},{5,1},{9,5},{13,9},{2,14},{6,2},{... | collective-permute-start | bytes 1376264 | tf_op jit(solution)/shard_map/ppermute | solution.py:24
  38.9 1.7 %collective-permute-done.2.refs_5_ = bf16[576,128]{1,0:T(8,128)(2,1)S(1)} collective-permute-done((bf16[576,128]{1,0:T(8,128)(2,1)S(1)}, bf16[576,128]{1,0:T(8,128)(2,1)S(1)}, u32[]{:S(2)}, u32[]{:S(2)}) %collective-permute-start.2) | collective-permute-done | bytes 147488 | tf_op jit(solution)/shard_map/ppermute | solution.py:24
  40.7 2.6 %collective-permute-start.6 = (bf16[1792,128]{1,0:T(8,128)(2,1)S(1)}, bf16[1792,128]{1,0:T(8,128)(2,1)S(1)}, u32[]{:S(2)}, u32[]{:S(2)}) collective-permute-start(bf16[1792,128]{1,0:T(8,128)(2,1)S(1)} %pad_maximum_fusion.refs_0_), channel_id=1, source_target_pairs={{0,3},{1,0},{2,1},{3,2},{4,7},{5,4},{6,5},{7,6},{8,11},{9,8},{10,9... | collective-permute-start | bytes 1376264 | tf_op jit(solution)/shard_map/ppermute | solution.py:24
  43.3 4.8 %collective-permute-done.13.refs_7_ = bf16[1792,128]{1,0:T(8,128)(2,1)S(1)} collective-permute-done((bf16[1792,128]{1,0:T(8,128)(2,1)S(1)}, bf16[1792,128]{1,0:T(8,128)(2,1)S(1)}, u32[]{:S(2)}, u32[]{:S(2)}) %collective-permute-start.13) | collective-permute-done | bytes 458784 | tf_op jit(solution)/shard_map/ppermute | solution.py:24
  48.2 0.7 slice.61
  48.9 3.4 %collective-permute-start.15 = (bf16[896,128]{1,0:T(8,128)(2,1)}, bf16[896,128]{1,0:T(8,128)(2,1)}, u32[]{:S(2)}, u32[]{:S(2)}) collective-permute-start(bf16[896,128]{1,0:T(8,128)(2,1)} %slice.61), channel_id=1, source_target_pairs={{0,12},{4,0},{8,4},{12,8},{1,13},{5,1},{9,5},{13,9},{2,14},{6,2},{... | collective-permute-start | bytes 688136 | tf_op jit(solution)/shard_map/ppermute | solution.py:24
  52.3 0.7 slice.60
  53.0 0.7 slice.56
  53.7 2.1 %collective-permute-start.8 = (bf16[896,128]{1,0:T(8,128)(2,1)}, bf16[896,128]{1,0:T(8,128)(2,1)}, u32[]{:S(2)}, u32[]{:S(2)}) collective-permute-start(bf16[896,128]{1,0:T(8,128)(2,1)} %slice.56), channel_id=1, source_target_pairs={{0,3},{1,0},{2,1},{3,2},{4,7},{5,4},{6,5},{7,6},{8,11},{9,8},{10,9... | collective-permute-start | bytes 688136 | tf_op jit(solution)/shard_map/ppermute | solution.py:24
  55.8 0.7 slice.55
  56.5 0.8 copy-done.2
  57.3 0.1 pad_add_fusion.1.place_ref.y_ref
  57.4 2.2 %copy-done = bf16[512,4096]{1,0:T(8,128)(2,1)S(1)} copy-done((bf16[512,4096]{1,0:T(8,128)(2,1)S(1)}, bf16[512,4096]{1,0:T(8,128)(2,1)}, u32[]{:S(2)}) %copy-start) | copy-done | bytes 4194328
  59.6 0.1 read_meta.1
  59.6 0.2 collective-permute-done.14.refs_8_
  59.9 3.8 %collective-permute-done.7.refs_3_ = bf16[896,128]{1,0:T(8,128)(2,1)} collective-permute-done((bf16[896,128]{1,0:T(8,128)(2,1)}, bf16[896,128]{1,0:T(8,128)(2,1)}, u32[]{:S(2)}, u32[]{:S(2)}) %collective-permute-start.7) | collective-permute-done | bytes 229408 | tf_op jit(solution)/shard_map/ppermute | solution.py:24
  63.7 8.4 %forward.1 = (bf16[448,4608]{1,0:T(8,128)(2,1)S(1)}, f32[112,1]{1,0:T(8,128)S(1)}, f32[448,1024]{1,0:T(8,128)S(1)}, f32[128,4,128]{2,1,0:T(4,128)S(1)}) custom-call(s32[4]{0:T(128)S(1)} %pad_add_fusion.1.place_ref.y_ref, bf16[512,4096]{1,0:T(8,128)(2,1)S(1)} %copy-done.1, bf16[512,4096]{1,0:T(8,128)(2,1)} %collective-permute-done.w1_ref, ...), custom_call_target="tpu_custom_call" | custom-call | flops 3758096384 | bytes 8388608 | tf_op jit(solution)/shard_map/forward/pallas_call | solution.py:152
  72.1 18.1 %all_to_all.15.every_ref = f32[128,4,128]{2,1,0:T(4,128)S(1)} all-to-all(f32[128,4,128]{2,1,0:T(4,128)S(1)} %get-tuple-element.105), channel_id=1, replica_groups=mesh['c'=2,'z'=8,'y'=4,'x'=4] {'z','y','x'}, dimensions={0} | all-to-all | bytes 524288 | tf_op jit(solution)/shard_map/all_to_all | solution.py:700
  90.2 4.0 %soft_rows.1 = (bf16[448,1024]{1,0:T(8,128)(2,1)S(1)}, bf16[448,4608]{1,0:T(8,128)(2,1)S(1)}, bf16[4,16,128]{2,1,0:T(8,128)(2,1)S(1)}, f32[1,128]{1,0:T(1,128)S(...) custom-call(s32[4]{0:T(128)S(1)} %pad_add_fusion.1.place_ref.y_ref, ...), custom_call_target="tpu_custom_call", output_to_operand_aliasing={{1}: (5, {})} | custom-call | tf_op jit(solution)/shard_map/soft_rows/pallas_call | solution.py:279
  94.2 0.0 copy-start.5
  94.2 0.4 collective-permute-start.16
  94.6 2.4 %collective-permute-start.17 = (bf16[896,128]{1,0:T(8,128)(2,1)S(1)}, bf16[896,128]{1,0:T(8,128)(2,1)S(1)}, u32[]{:S(2)}, u32[]{:S(2)}) collective-permute-start(bf16[896,128]{1,0:T(8,128)(2,1)S(1)} %get-tuple-element.123), channel_id=1, source_target_pairs={{0,3},{1,0},{2,1},{3,2},{4,7},{5,4},{6,5},{7,6},{8,11},{9,8},{10,9... | collective-permute-start | bytes 688136 | tf_op jit(solution)/shard_map/ppermute | solution.py:24
  97.0 0.3 collective-permute-start.18
  97.3 2.4 %collective-permute-start.19 = (bf16[896,128]{1,0:T(8,128)(2,1)S(1)}, bf16[896,128]{1,0:T(8,128)(2,1)S(1)}, u32[]{:S(2)}, u32[]{:S(2)}) collective-permute-start(bf16[896,128]{1,0:T(8,128)(2,1)S(1)} %get-tuple-element.125), channel_id=1, source_target_pairs={{0,12},{4,0},{8,4},{12,8},{1,13},{5,1},{9,5},{13,9},{2,14},{6,2},{... | collective-permute-start | bytes 688136 | tf_op jit(solution)/shard_map/ppermute | solution.py:24
  99.7 6.9 %near_rows.1 = (bf16[1792,128]{1,0:T(8,128)(2,1)S(1)}, bf16[1808,128]{1,0:T(8,128)(2,1)S(1)}, bf16[1808,128]{1,0:T(8,128)(2,1)S(1)}, bf16[1792,128]{1,0:T(8,128)...) custom-call(s32[4]{0:T(128)S(1)} %pad_add_fusion.1.place_ref.y_ref, ...), custom_call_target="tpu_custom_call" | custom-call | tf_op jit(solution)/shard_map/near_rows/pallas_call | solution.py:355
  106.6 6.3 %collective-permute-start.25 = (bf16[448,4608]{1,0:T(8,128)(2,1)S(1)}, bf16[448,4608]{1,0:T(8,128)(2,1)S(1)}, u32[]{:S(2)}, u32[]{:S(2)}) collective-permute-start(bf16[448,4608]{1,0:T(8,128)(2,1)S(1)} %get-tuple-element.143.n_ref), channel_id=1, source_target_pairs={{0,128},{128,0},{1,129},{129,1},{2,130},{130,2},{3,131},{131,3},{4... | collective-permute-start | bytes 12386312 | tf_op jit(solution)/shard_map/ppermute | solution.py:24
  112.9 0.1 relay.2
  113.1 0.1 collective-permute-start.21
  113.2 2.7 %collective-permute-start.22 = (bf16[1872,128]{1,0:T(8,128)(2,1)S(1)}, bf16[1872,128]{1,0:T(8,128)(2,1)S(1)}, u32[]{:S(2)}, u32[]{:S(2)}) collective-permute-start(bf16[1872,128]{1,0:T(8,128)(2,1)S(1)} %get-tuple-element.135), channel_id=1, source_target_pairs={{0,3},{1,0},{2,1},{3,2},{4,7},{5,4},{6,5},{7,6},{8,11},{9,8},{10,9... | collective-permute-start | bytes 1437704 | tf_op jit(solution)/shard_map/ppermute | solution.py:24
  115.8 0.1 relay.3
  116.0 0.1 collective-permute-start.23
  116.1 2.7 %collective-permute-start.24 = (bf16[1792,128]{1,0:T(8,128)(2,1)S(1)}, bf16[1792,128]{1,0:T(8,128)(2,1)S(1)}, u32[]{:S(2)}, u32[]{:S(2)}) collective-permute-start(bf16[1792,128]{1,0:T(8,128)(2,1)S(1)} %get-tuple-element.141), channel_id=1, source_target_pairs={{0,12},{4,0},{8,4},{12,8},{1,13},{5,1},{9,5},{13,9},{2,14},{6,2},{... | collective-permute-start | bytes 1376264 | tf_op jit(solution)/shard_map/ppermute | solution.py:24
  118.7 0.9 collective-permute-done.25.h_ref.m_ref
  119.6 7.5 %outer.1 = bf16[512,4096]{1,0:T(8,128)(2,1)} custom-call(bf16[448,1024]{1,0:T(8,128)(2,1)S(1)} %get-tuple-element.142.g_ref, bf16[448,4608]{1,0:T(8,128)(2,1)S(1)} %collective-permute-done.25.h_ref.m_ref, bf16[448,4608]{1,0:T(8,128)(2,1)S(1)} %get-tuple-element.143.n_ref, bf16[448,4608]{1,0:T(8,128)(2,1)S(1)} %collective-permute-done.25.h_ref.m_ref), custom_call_target="tpu_custom_call" | custom-call | flops 3758096384 | bytes 16777216 | tf_op jit(solution)/shard_map/outer/pallas_call | solution.py:603
  127.1 1.6 %collective-permute-done.23.b1 = bf16[1792,128]{1,0:T(8,128)(2,1)S(1)} collective-permute-done((bf16[1792,128]{1,0:T(8,128)(2,1)S(1)}, bf16[1792,128]{1,0:T(8,128)(2,1)S(1)}, u32[]{:S(2)}, u32[]{:S(2)}) %collective-permute-start.23) | collective-permute-done | bytes 458784 | tf_op jit(solution)/shard_map/ppermute | solution.py:24
  128.8 0.9 turn_rows.1
  129.7 1.0 collective-permute-start.29
  130.7 3.0 %collective-permute-start.27 = (bf16[480,128]{1,0:T(8,128)(2,1)S(1)}, bf16[480,128]{1,0:T(8,128)(2,1)S(1)}, u32[]{:S(2)}, u32[]{:S(2)}) collective-permute-start(bf16[480,128]{1,0:T(8,128)(2,1)S(1)} %get-tuple-element.153), channel_id=1, source_target_pairs={{0,8},{4,12},{8,0},{12,4},{1,9},{5,13},{9,1},{13,5},{2,10},{6,14},... | collective-permute-start | bytes 368648 | tf_op jit(solution)/shard_map/ppermute | solution.py:24
  133.7 0.7 collective-permute-start.30
  134.3 0.6 collective-permute-start.31
  134.9 4.2 %collective-permute-done.30.refs_6_ = bf16[448,128]{1,0:T(8,128)(2,1)S(1)} collective-permute-done((bf16[448,128]{1,0:T(8,128)(2,1)S(1)}, bf16[448,128]{1,0:T(8,128)(2,1)S(1)}, u32[]{:S(2)}, u32[]{:S(2)}) %collective-permute-start.30) | collective-permute-done | bytes 114720 | tf_op jit(solution)/shard_map/ppermute | solution.py:24
  139.1 1.1 collective-permute-done.31.refs_7_
  140.2 0.2 gather_rows.1
  140.4 12.6 %all_to_all.16.total_ref = bf16[8,128,128]{2,1,0:T(8,128)(2,1)} all-to-all(bf16[8,128,128]{2,1,0:T(8,128)(2,1)S(1)} %gather_rows.1), channel_id=1, replica_groups=mesh['c'=2,'z'=8,'y'=4,'x'=4] {'z'}, dimensions={0} | all-to-all | bytes 524288 | tf_op jit(solution)/shard_map/all_to_all | solution.py:724
  153.0 1.8 %finish.1 = (bf16[128,128]{1,0:T(8,128)(2,1)}, f32[2,128]{1,0:T(2,128)}) custom-call(f32[1,128]{1,0:T(1,128)} %copy-done.5, bf16[8,128,128]{2,1,0:T(8,128)(2,1)} %all_to_all.16.total_ref, bf16[128,128]{1,0:T(8,128)(2,1)} %hidden_ref.3, f32[1,128]{1,0:T(1,128)} %bitcast.21, f32[112,1]{1,0:T(8,128)} %copy-done.4), custom_call_target="tpu_custom_call" | custom-call | tf_op jit(solution)/shard_map/finish/pallas_call | solution.py:656
  154.7 4.5 %collective-permute-start.32 = (f32[2,128]{1,0:T(2,128)}, f32[2,128]{1,0:T(2,128)S(1)}, u32[]{:S(2)}, u32[]{:S(2)}) collective-permute-start(f32[2,128]{1,0:T(2,128)} %get-tuple-element.161.sums_ref), channel_id=1, source_target_pairs={{0,128},{128,0},{1,129},{129,1},{2,130},{130,2},{3,131},{131,3},{4... | collective-permute-start | bytes 3080 | tf_op jit(solution)/shard_map/ppermute | solution.py:24
  159.2 1.0 collective-permute-done.32.came_ref
  160.2 0.6 copy-done.7
  160.8 1.2 last.1
  (53 shorter events, 0.3 us)
Async XLA Ops:
  0.6 23.7 %collective-permute-start = (bf16[512,4096]{1,0:T(8,128)(2,1)}, bf16[512,4096]{1,0:T(8,128)(2,1)}, u32[]{:S(2)}, u32[]{:S(2)}) collective-permute-start(bf16[512,4096]{1,0:T(8,128)(2,1)} %w0_ref.5), channel_id=1, source_target_pairs={{0,128},{128,0},{1,129},{129,1},{2,130},{130,2},{3,131},{131,3},{4... | collective-permute-start | bytes 12582920 | tf_op jit(solution)/shard_map/ppermute | solution.py:24
  5.5 18.8 %all-to-all-start = ((bf16[8,128,128]{2,1,0:T(8,128)(2,1)}), bf16[8,128,128]{2,1,0:T(8,128)(2,1)S(1)}, u32[]{:S(2)}, u32[]{:S(2)}) async-start(bf16[8,128,128]{2,1,0:T(8,128)(2,1)} %get-tuple-element.85), calls=%async_computation | async-start | bytes 524288 | tf_op jit(solution)/shard_map/all_to_all | solution.py:679
  11.9 1.3 collective-permute-start.1
  24.4 6.9 %collective-permute-start.11 = (bf16[464,128]{1,0:T(8,128)(2,1)S(1)}, bf16[464,128]{1,0:T(8,128)(2,1)S(1)}, u32[]{:S(2)}, u32[]{:S(2)}) collective-permute-start(bf16[464,128]{1,0:T(8,128)(2,1)S(1)} %pad_maximum_fusion.3.refs_0_), channel_id=1, source_target_pairs={{0,3},{1,0},{2,1},{3,2},{4,7},{5,4},{6,5},{7,6},{8,11},{9,8},{10,9... | collective-permute-start | bytes 356360 | tf_op jit(solution)/shard_map/ppermute | solution.py:24
  26.9 5.5 %collective-permute-start.10 = (bf16[464,128]{1,0:T(8,128)(2,1)S(1)}, bf16[464,128]{1,0:T(8,128)(2,1)S(1)}, u32[]{:S(2)}, u32[]{:S(2)}) collective-permute-start(bf16[464,128]{1,0:T(8,128)(2,1)S(1)} %pad_maximum_fusion.3.refs_0_), channel_id=1, source_target_pairs={{0,2},{1,3},{2,0},{3,1},{4,6},{5,7},{6,4},{7,5},{8,10},{9,11},{10,... | collective-permute-start | bytes 356360 | tf_op jit(solution)/shard_map/ppermute | solution.py:24
  27.4 8.6 %collective-permute-start.9 = (bf16[464,128]{1,0:T(8,128)(2,1)S(1)}, bf16[464,128]{1,0:T(8,128)(2,1)S(1)}, u32[]{:S(2)}, u32[]{:S(2)}) collective-permute-start(bf16[464,128]{1,0:T(8,128)(2,1)S(1)} %pad_maximum_fusion.3.refs_0_), channel_id=1, source_target_pairs={{0,1},{1,2},{2,3},{3,0},{4,5},{5,6},{6,7},{7,4},{8,9},{9,10},{10,1... | collective-permute-start | bytes 356360 | tf_op jit(solution)/shard_map/ppermute | solution.py:24
  28.1 10.8 %collective-permute-start.4 = (bf16[576,128]{1,0:T(8,128)(2,1)S(1)}, bf16[576,128]{1,0:T(8,128)(2,1)S(1)}, u32[]{:S(2)}, u32[]{:S(2)}) collective-permute-start(bf16[576,128]{1,0:T(8,128)(2,1)S(1)} %pad_maximum_fusion.2.refs_4_), channel_id=1, source_target_pairs={{0,12},{4,0},{8,4},{12,8},{1,13},{5,1},{9,5},{13,9},{2,14},{6,2},{... | collective-permute-start | bytes 442376 | tf_op jit(solution)/shard_map/ppermute | solution.py:24
  30.9 8.0 %collective-permute-start.3 = (bf16[576,128]{1,0:T(8,128)(2,1)S(1)}, bf16[576,128]{1,0:T(8,128)(2,1)S(1)}, u32[]{:S(2)}, u32[]{:S(2)}) collective-permute-start(bf16[576,128]{1,0:T(8,128)(2,1)S(1)} %pad_maximum_fusion.2.refs_4_), channel_id=1, source_target_pairs={{0,8},{4,12},{8,0},{12,4},{1,9},{5,13},{9,1},{13,5},{2,10},{6,14},... | collective-permute-start | bytes 442376 | tf_op jit(solution)/shard_map/ppermute | solution.py:24
  31.2 9.4 %collective-permute-start.2 = (bf16[576,128]{1,0:T(8,128)(2,1)S(1)}, bf16[576,128]{1,0:T(8,128)(2,1)S(1)}, u32[]{:S(2)}, u32[]{:S(2)}) collective-permute-start(bf16[576,128]{1,0:T(8,128)(2,1)S(1)} %pad_maximum_fusion.2.refs_4_), channel_id=1, source_target_pairs={{0,4},{4,8},{8,12},{12,0},{1,5},{5,9},{9,13},{13,1},{2,6},{6,10},{... | collective-permute-start | bytes 442376 | tf_op jit(solution)/shard_map/ppermute | solution.py:24
  36.1 12.1 %collective-permute-start.13 = (bf16[1792,128]{1,0:T(8,128)(2,1)S(1)}, bf16[1792,128]{1,0:T(8,128)(2,1)S(1)}, u32[]{:S(2)}, u32[]{:S(2)}) collective-permute-start(bf16[1792,128]{1,0:T(8,128)(2,1)S(1)} %pad_maximum_fusion.1.refs_5_), channel_id=1, source_target_pairs={{0,12},{4,0},{8,4},{12,8},{1,13},{5,1},{9,5},{13,9},{2,14},{6,2},{... | collective-permute-start | bytes 1376264 | tf_op jit(solution)/shard_map/ppermute | solution.py:24
  38.9 13.4 %collective-permute-start.12 = (bf16[1792,128]{1,0:T(8,128)(2,1)S(1)}, bf16[1792,128]{1,0:T(8,128)(2,1)S(1)}, u32[]{:S(2)}, u32[]{:S(2)}) collective-permute-start(bf16[1792,128]{1,0:T(8,128)(2,1)S(1)} %pad_maximum_fusion.1.refs_5_), channel_id=1, source_target_pairs={{0,4},{4,8},{8,12},{12,0},{1,5},{5,9},{9,13},{13,1},{2,6},{6,10},{... | collective-permute-start | bytes 1376264 | tf_op jit(solution)/shard_map/ppermute | solution.py:24
  40.7 12.3 %collective-permute-start.6 = (bf16[1792,128]{1,0:T(8,128)(2,1)S(1)}, bf16[1792,128]{1,0:T(8,128)(2,1)S(1)}, u32[]{:S(2)}, u32[]{:S(2)}) collective-permute-start(bf16[1792,128]{1,0:T(8,128)(2,1)S(1)} %pad_maximum_fusion.refs_0_), channel_id=1, source_target_pairs={{0,3},{1,0},{2,1},{3,2},{4,7},{5,4},{6,5},{7,6},{8,11},{9,8},{10,9... | collective-permute-start | bytes 1376264 | tf_op jit(solution)/shard_map/ppermute | solution.py:24
  43.3 12.5 %collective-permute-start.5 = (bf16[1792,128]{1,0:T(8,128)(2,1)S(1)}, bf16[1792,128]{1,0:T(8,128)(2,1)S(1)}, u32[]{:S(2)}, u32[]{:S(2)}) collective-permute-start(bf16[1792,128]{1,0:T(8,128)(2,1)S(1)} %pad_maximum_fusion.refs_0_), channel_id=1, source_target_pairs={{0,1},{1,2},{2,3},{3,0},{4,5},{5,6},{6,7},{7,4},{8,9},{9,10},{10,1... | collective-permute-start | bytes 1376264 | tf_op jit(solution)/shard_map/ppermute | solution.py:24
  48.9 10.8 %collective-permute-start.15 = (bf16[896,128]{1,0:T(8,128)(2,1)}, bf16[896,128]{1,0:T(8,128)(2,1)}, u32[]{:S(2)}, u32[]{:S(2)}) collective-permute-start(bf16[896,128]{1,0:T(8,128)(2,1)} %slice.61), channel_id=1, source_target_pairs={{0,12},{4,0},{8,4},{12,8},{1,13},{5,1},{9,5},{13,9},{2,14},{6,2},{... | collective-permute-start | bytes 688136 | tf_op jit(solution)/shard_map/ppermute | solution.py:24
  53.0 6.9 %collective-permute-start.14 = (bf16[896,128]{1,0:T(8,128)(2,1)}, bf16[896,128]{1,0:T(8,128)(2,1)}, u32[]{:S(2)}, u32[]{:S(2)}) collective-permute-start(bf16[896,128]{1,0:T(8,128)(2,1)} %slice.60), channel_id=1, source_target_pairs={{0,4},{4,8},{8,12},{12,0},{1,5},{5,9},{9,13},{13,1},{2,6},{6,10},{... | collective-permute-start | bytes 688136 | tf_op jit(solution)/shard_map/ppermute | solution.py:24
  53.7 6.2 %collective-permute-start.8 = (bf16[896,128]{1,0:T(8,128)(2,1)}, bf16[896,128]{1,0:T(8,128)(2,1)}, u32[]{:S(2)}, u32[]{:S(2)}) collective-permute-start(bf16[896,128]{1,0:T(8,128)(2,1)} %slice.56), channel_id=1, source_target_pairs={{0,3},{1,0},{2,1},{3,2},{4,7},{5,4},{6,5},{7,6},{8,11},{9,8},{10,9... | collective-permute-start | bytes 688136 | tf_op jit(solution)/shard_map/ppermute | solution.py:24
  56.5 0.8 copy-start.2
  57.3 6.4 %collective-permute-start.7 = (bf16[896,128]{1,0:T(8,128)(2,1)}, bf16[896,128]{1,0:T(8,128)(2,1)}, u32[]{:S(2)}, u32[]{:S(2)}) collective-permute-start(bf16[896,128]{1,0:T(8,128)(2,1)} %slice.55), channel_id=1, source_target_pairs={{0,1},{1,2},{2,3},{3,0},{4,5},{5,6},{6,7},{7,4},{8,9},{9,10},{10,1... | collective-permute-start | bytes 688136 | tf_op jit(solution)/shard_map/ppermute | solution.py:24
  57.4 2.2 %copy-start = (bf16[512,4096]{1,0:T(8,128)(2,1)S(1)}, bf16[512,4096]{1,0:T(8,128)(2,1)}, u32[]{:S(2)}) copy-start(bf16[512,4096]{1,0:T(8,128)(2,1)} %w0_ref.5) | copy-start | bytes 12582916
  59.5 4.1 %copy-start.1 = (bf16[512,4096]{1,0:T(8,128)(2,1)S(1)}, bf16[512,4096]{1,0:T(8,128)(2,1)}, u32[]{:S(2)}) copy-start(bf16[512,4096]{1,0:T(8,128)(2,1)} %w0_ref.5) | copy-start | bytes 12582916
  59.5 4.1 %copy-start.3 = (bf16[1792,128]{1,0:T(8,128)(2,1)S(1)}, bf16[1792,128]{1,0:T(8,128)(2,1)}, u32[]{:S(2)}) copy-start(bf16[1792,128]{1,0:T(8,128)(2,1)} %copy-done.2) | copy-start | bytes 1376260
  59.6 12.4 %copy-start.6 = (f32[1,128]{1,0:T(1,128)}, f32[1,128]{1,0:T(1,128)S(1)}, u32[]{:S(2)}) copy-start(f32[1,128]{1,0:T(1,128)S(1)} %get-tuple-element.162.total_ref) | copy-start | bytes 1540
  72.1 22.2 %copy-start.4 = (f32[112,1]{1,0:T(8,128)}, f32[112,1]{1,0:T(8,128)S(1)}, u32[]{:S(2)}) copy-start(f32[112,1]{1,0:T(8,128)S(1)} %get-tuple-element.159.inv_ref) | copy-start | bytes 1348
  94.2 12.3 %copy-start.5 = (f32[1,128]{1,0:T(1,128)}, f32[1,128]{1,0:T(1,128)S(1)}, u32[]{:S(2)}) copy-start(f32[1,128]{1,0:T(1,128)S(1)} %get-tuple-element.111.loss_ref) | copy-start | bytes 1540
  94.2 12.3 %collective-permute-start.16 = (bf16[912,128]{1,0:T(8,128)(2,1)S(1)}, bf16[912,128]{1,0:T(8,128)(2,1)S(1)}, u32[]{:S(2)}, u32[]{:S(2)}) collective-permute-start(bf16[912,128]{1,0:T(8,128)(2,1)S(1)} %get-tuple-element.122), channel_id=1, source_target_pairs={{0,1},{1,2},{2,3},{3,0},{4,5},{5,6},{6,7},{7,4},{8,9},{9,10},{10,1... | collective-permute-start | bytes 700424 | tf_op jit(solution)/shard_map/ppermute | solution.py:24
  94.6 12.0 %collective-permute-start.17 = (bf16[896,128]{1,0:T(8,128)(2,1)S(1)}, bf16[896,128]{1,0:T(8,128)(2,1)S(1)}, u32[]{:S(2)}, u32[]{:S(2)}) collective-permute-start(bf16[896,128]{1,0:T(8,128)(2,1)S(1)} %get-tuple-element.123), channel_id=1, source_target_pairs={{0,3},{1,0},{2,1},{3,2},{4,7},{5,4},{6,5},{7,6},{8,11},{9,8},{10,9... | collective-permute-start | bytes 688136 | tf_op jit(solution)/shard_map/ppermute | solution.py:24
  97.0 9.6 %collective-permute-start.18 = (bf16[896,128]{1,0:T(8,128)(2,1)S(1)}, bf16[896,128]{1,0:T(8,128)(2,1)S(1)}, u32[]{:S(2)}, u32[]{:S(2)}) collective-permute-start(bf16[896,128]{1,0:T(8,128)(2,1)S(1)} %get-tuple-element.124), channel_id=1, source_target_pairs={{0,4},{4,8},{8,12},{12,0},{1,5},{5,9},{9,13},{13,1},{2,6},{6,10},{... | collective-permute-start | bytes 688136 | tf_op jit(solution)/shard_map/ppermute | solution.py:24
  97.3 9.3 %collective-permute-start.19 = (bf16[896,128]{1,0:T(8,128)(2,1)S(1)}, bf16[896,128]{1,0:T(8,128)(2,1)S(1)}, u32[]{:S(2)}, u32[]{:S(2)}) collective-permute-start(bf16[896,128]{1,0:T(8,128)(2,1)S(1)} %get-tuple-element.125), channel_id=1, source_target_pairs={{0,12},{4,0},{8,4},{12,8},{1,13},{5,1},{9,5},{13,9},{2,14},{6,2},{... | collective-permute-start | bytes 688136 | tf_op jit(solution)/shard_map/ppermute | solution.py:24
  106.6 13.0 %collective-permute-start.25 = (bf16[448,4608]{1,0:T(8,128)(2,1)S(1)}, bf16[448,4608]{1,0:T(8,128)(2,1)S(1)}, u32[]{:S(2)}, u32[]{:S(2)}) collective-permute-start(bf16[448,4608]{1,0:T(8,128)(2,1)S(1)} %get-tuple-element.143.n_ref), channel_id=1, source_target_pairs={{0,128},{128,0},{1,129},{129,1},{2,130},{130,2},{3,131},{131,3},{4... | collective-permute-start | bytes 12386312 | tf_op jit(solution)/shard_map/ppermute | solution.py:24
  113.1 15.7 %collective-permute-start.21 = (bf16[1872,128]{1,0:T(8,128)(2,1)S(1)}, bf16[1872,128]{1,0:T(8,128)(2,1)S(1)}, u32[]{:S(2)}, u32[]{:S(2)}) collective-permute-start(bf16[1872,128]{1,0:T(8,128)(2,1)S(1)} %get-tuple-element.134), channel_id=1, source_target_pairs={{0,1},{1,2},{2,3},{3,0},{4,5},{5,6},{6,7},{7,4},{8,9},{9,10},{10,1... | collective-permute-start | bytes 1437704 | tf_op jit(solution)/shard_map/ppermute | solution.py:24
  113.2 15.6 %collective-permute-start.22 = (bf16[1872,128]{1,0:T(8,128)(2,1)S(1)}, bf16[1872,128]{1,0:T(8,128)(2,1)S(1)}, u32[]{:S(2)}, u32[]{:S(2)}) collective-permute-start(bf16[1872,128]{1,0:T(8,128)(2,1)S(1)} %get-tuple-element.135), channel_id=1, source_target_pairs={{0,3},{1,0},{2,1},{3,2},{4,7},{5,4},{6,5},{7,6},{8,11},{9,8},{10,9... | collective-permute-start | bytes 1437704 | tf_op jit(solution)/shard_map/ppermute | solution.py:24
  116.0 12.8 %collective-permute-start.23 = (bf16[1792,128]{1,0:T(8,128)(2,1)S(1)}, bf16[1792,128]{1,0:T(8,128)(2,1)S(1)}, u32[]{:S(2)}, u32[]{:S(2)}) collective-permute-start(bf16[1792,128]{1,0:T(8,128)(2,1)S(1)} %get-tuple-element.140), channel_id=1, source_target_pairs={{0,4},{4,8},{8,12},{12,0},{1,5},{5,9},{9,13},{13,1},{2,6},{6,10},{... | collective-permute-start | bytes 1376264 | tf_op jit(solution)/shard_map/ppermute | solution.py:24
  116.1 12.7 %collective-permute-start.24 = (bf16[1792,128]{1,0:T(8,128)(2,1)S(1)}, bf16[1792,128]{1,0:T(8,128)(2,1)S(1)}, u32[]{:S(2)}, u32[]{:S(2)}) collective-permute-start(bf16[1792,128]{1,0:T(8,128)(2,1)S(1)} %get-tuple-element.141), channel_id=1, source_target_pairs={{0,12},{4,0},{8,4},{12,8},{1,13},{5,1},{9,5},{13,9},{2,14},{6,2},{... | collective-permute-start | bytes 1376264 | tf_op jit(solution)/shard_map/ppermute | solution.py:24
  119.6 9.1 %collective-permute-start.20 = (f32[32,128]{1,0:T(8,128)S(1)}, f32[32,128]{1,0:T(8,128)S(1)}, u32[]{:S(2)}, u32[]{:S(2)}) collective-permute-start(f32[32,128]{1,0:T(8,128)S(1)} %get-tuple-element.132.mine), channel_id=1, source_target_pairs={{0,2},{1,3},{2,0},{3,1},{4,6},{5,7},{6,4},{7,5},{8,10},{9,11},{10,... | collective-permute-start | bytes 49160 | tf_op jit(solution)/shard_map/ppermute | solution.py:24
  129.7 4.6 %collective-permute-start.29 = (bf16[448,128]{1,0:T(8,128)(2,1)S(1)}, bf16[448,128]{1,0:T(8,128)(2,1)S(1)}, u32[]{:S(2)}, u32[]{:S(2)}) collective-permute-start(bf16[448,128]{1,0:T(8,128)(2,1)S(1)} %get-tuple-element.156), channel_id=1, source_target_pairs={{0,3},{1,0},{2,1},{3,2},{4,7},{5,4},{6,5},{7,6},{8,11},{9,8},{10,9... | collective-permute-start | bytes 344072 | tf_op jit(solution)/shard_map/ppermute | solution.py:24
  130.7 9.5 %collective-permute-start.26 = (bf16[480,128]{1,0:T(8,128)(2,1)S(1)}, bf16[480,128]{1,0:T(8,128)(2,1)S(1)}, u32[]{:S(2)}, u32[]{:S(2)}) collective-permute-start(bf16[480,128]{1,0:T(8,128)(2,1)S(1)} %get-tuple-element.152), channel_id=1, source_target_pairs={{0,4},{4,8},{8,12},{12,0},{1,5},{5,9},{9,13},{13,1},{2,6},{6,10},{... | collective-permute-start | bytes 368648 | tf_op jit(solution)/shard_map/ppermute | solution.py:24
  130.7 9.5 %collective-permute-start.27 = (bf16[480,128]{1,0:T(8,128)(2,1)S(1)}, bf16[480,128]{1,0:T(8,128)(2,1)S(1)}, u32[]{:S(2)}, u32[]{:S(2)}) collective-permute-start(bf16[480,128]{1,0:T(8,128)(2,1)S(1)} %get-tuple-element.153), channel_id=1, source_target_pairs={{0,8},{4,12},{8,0},{12,4},{1,9},{5,13},{9,1},{13,5},{2,10},{6,14},... | collective-permute-start | bytes 368648 | tf_op jit(solution)/shard_map/ppermute | solution.py:24
  133.7 6.5 %collective-permute-start.28 = (bf16[480,128]{1,0:T(8,128)(2,1)S(1)}, bf16[480,128]{1,0:T(8,128)(2,1)S(1)}, u32[]{:S(2)}, u32[]{:S(2)}) collective-permute-start(bf16[480,128]{1,0:T(8,128)(2,1)S(1)} %get-tuple-element.154), channel_id=1, source_target_pairs={{0,12},{4,0},{8,4},{12,8},{1,13},{5,1},{9,5},{13,9},{2,14},{6,2},{... | collective-permute-start | bytes 368648 | tf_op jit(solution)/shard_map/ppermute | solution.py:24
  133.7 5.4 %collective-permute-start.30 = (bf16[448,128]{1,0:T(8,128)(2,1)S(1)}, bf16[448,128]{1,0:T(8,128)(2,1)S(1)}, u32[]{:S(2)}, u32[]{:S(2)}) collective-permute-start(bf16[448,128]{1,0:T(8,128)(2,1)S(1)} %get-tuple-element.157), channel_id=1, source_target_pairs={{0,2},{1,3},{2,0},{3,1},{4,6},{5,7},{6,4},{7,5},{8,10},{9,11},{10,... | collective-permute-start | bytes 344072 | tf_op jit(solution)/shard_map/ppermute | solution.py:24
  134.3 5.8 %collective-permute-start.31 = (bf16[448,128]{1,0:T(8,128)(2,1)S(1)}, bf16[448,128]{1,0:T(8,128)(2,1)S(1)}, u32[]{:S(2)}, u32[]{:S(2)}) collective-permute-start(bf16[448,128]{1,0:T(8,128)(2,1)S(1)} %get-tuple-element.158), channel_id=1, source_target_pairs={{0,1},{1,2},{2,3},{3,0},{4,5},{5,6},{6,7},{7,4},{8,9},{9,10},{10,1... | collective-permute-start | bytes 344072 | tf_op jit(solution)/shard_map/ppermute | solution.py:24
  154.7 5.5 %collective-permute-start.32 = (f32[2,128]{1,0:T(2,128)}, f32[2,128]{1,0:T(2,128)S(1)}, u32[]{:S(2)}, u32[]{:S(2)}) collective-permute-start(f32[2,128]{1,0:T(2,128)} %get-tuple-element.161.sums_ref), channel_id=1, source_target_pairs={{0,128},{128,0},{1,129},{129,1},{2,130},{130,2},{3,131},{131,3},{4... | collective-permute-start | bytes 3080 | tf_op jit(solution)/shard_map/ppermute | solution.py:24
  160.2 0.6 copy-start.7

commit v2 on v1

--- a/solution.py
+++ b/solution.py
@@ -25,13 +25,11 @@
 
 
 def ring_gather(block, axis):
-    half = block.shape[0] // 2
-    one, three = shift(block, axis, 1), shift(block, axis, -1)
-    two = shift(one[:half], axis, 1), shift(three[half:], axis, -1)
-    return block, one, three, *two
-
-
-PARTS = ((0, 0, 4), (1, 0, 4), (3, 0, 4), (2, 0, 2), (2, 2, 4))
+    one = shift(block, axis, 1)
+    return block, one, shift(block, axis, -1), shift(one, axis, 1)
+
+
+PARTS = ((0, 0, 4), (1, 0, 4), (3, 0, 4), (2, 0, 4))
 
 
 def spot_of(j):
@@ -57,8 +55,8 @@
 
 
 def forward_kernel(Zh, place_ref, w0_ref, w1_ref, gain_ref, *refs):
-    a_refs, b_refs = refs[:5], refs[5:10]
-    n_ref, inv_ref, l_ref, share_ref, w_ref, total_ref, w_sems = refs[10:]
+    a_refs, b_refs = refs[:R], refs[R : 2 * R]
+    n_ref, inv_ref, l_ref, share_ref, w_ref, total_ref, w_sems = refs[2 * R :]
     Z = 2 * Zh
     V = w0_ref.shape[0]
     copies = [
@@ -157,7 +155,7 @@
             jax.ShapeDtypeStruct((rows, 2 * V), f32),
             jax.ShapeDtypeStruct((2 * Zh * R * R, R, 128), f32),
         ),
-        in_specs=[SMEM, HBM, HBM] + [VMEM] * 11,
+        in_specs=[SMEM, HBM, HBM] + [VMEM] * (1 + 2 * R),
         out_specs=(VMEM,) * 4,
         scratch_shapes=[
             pltpu.VMEM((2, V, D), bf16),
@@ -293,59 +291,48 @@
 
 
 def near_kernel(Zh, place_ref, w0_ref, w1_ref, side_ref, g_ref, n_ref, *refs):
-    a0, a1, a3, b0, b1, b3, gain_ref, w_ref, scratch, sems = refs
+    a_refs, b_refs, (gain_ref, wa_ref, wb_ref, sems) = refs[:3], refs[3:6], refs[6:]
     V = w0_ref.shape[0]
-    copies = []
-    wide = 2 * R * 128
-    for q in range(4):
-        for i, w in enumerate((w0_ref, w1_ref)):
-            copies.append(
+    wide = Zh * R * 128
+    towards = [lax.rem(place_ref[0] + k, R) for k in (0, 1, 3)]
+    first, second = [], []
+    for i, w in enumerate((w0_ref, w1_ref)):
+        rows = pl.ds(i * V, V)
+        first.append(pltpu.make_async_copy(w.at[:, pl.ds(0, wide)], wa_ref.at[rows], sems.at[0, i]))
+        for n in range(3 * Zh):
+            column = pl.multiple_of(((Zh + n // 3) * R + towards[n % 3]) * 128, 128)
+            second.append(
                 pltpu.make_async_copy(
-                    w.at[:, pl.ds(q * wide, wide)], w_ref.at[q, pl.ds(i * V, V)], sems.at[q, i]
+                    w.at[:, pl.ds(column, 128)],
+                    wb_ref.at[rows, pl.ds(n * 128, 128)],
+                    sems.at[1 + n, i],
                 )
             )
-    for copy in copies:
+    for copy in first + second:
         copy.start()
-
-    def arrived(q):
-        for i in range(2):
-            pltpu.make_async_copy(
-                w0_ref.at[:, pl.ds(0, wide)], w_ref.at[q, pl.ds(i * V, V)], sems.at[q, i]
-            ).wait()
-        return w_ref[q]
-
     gain_ref[...] = jnp.zeros_like(gain_ref)
-
-    def first(q, _):
-        part = jnp.dot(g_ref[0 : 3 * LIVE, :], arrived(q), preferred_element_type=f32)
-        gain = n_ref[0 : 3 * LIVE, pl.ds(pl.multiple_of(q * wide, 128), wide)].astype(f32)
-        gain = jnp.sum(part * gain, axis=0, keepdims=True)
-        for t in range(2 * R):
-            at = pl.multiple_of((q * 2 * R + t) * LIVE, 16)
-            gain_ref[pl.ds(q * 2 * R + t, 1), :] = gain[:, t * 128 : (t + 1) * 128]
-            for p, ref in enumerate((a0, a1, a3)):
-                ref[pl.ds(at, LIVE), :] = part[
-                    p * LIVE : (p + 1) * LIVE, t * 128 : (t + 1) * 128
-                ].astype(ref.dtype)
-        return 0
-
-    def second(q, _):
-        scratch[...] = jnp.dot(g_ref[...], arrived(2 + q), preferred_element_type=f32)
-        for z in range(2):
-            at = pl.multiple_of((q * 2 + z) * (R * LIVE), 16)
-            for k, ref in ((0, b0), (1, b1), (3, b3)):
-                t = z * R + lax.rem(place_ref[0] + k, R)
-                part = scratch[:, pl.ds(pl.multiple_of(t * 128, 128), 128)]
-                ref[pl.ds(at, R * LIVE), :] = part.astype(ref.dtype)
-                t = (Zh + q * 2) * R + t
-                gain = n_ref[:, pl.ds(pl.multiple_of(t * 128, 128), 128)].astype(f32)
-                gain_ref[pl.ds(t, 1), :] = jnp.sum(part * gain, axis=0, keepdims=True)
-        return 0
-
-    lax.fori_loop(0, 2, first, 0)
-    lax.fori_loop(0, 2, second, 0)
-    a1[Zh * R * LIVE :, :] = side_ref[1]
-    a3[Zh * R * LIVE :, :] = side_ref[2]
+    for copy in first:
+        copy.wait()
+    part = jnp.dot(g_ref[0 : 3 * LIVE, :], wa_ref[...], preferred_element_type=f32)
+    gain = part * n_ref[0 : 3 * LIVE, 0:wide].astype(f32)
+    gain = jnp.sum(gain, axis=0, keepdims=True)
+    for t in range(Zh * R):
+        lanes = slice(t * 128, (t + 1) * 128)
+        gain_ref[t : t + 1, :] = gain[:, lanes]
+        for p, ref in enumerate(a_refs):
+            ref[t * LIVE : (t + 1) * LIVE, :] = part[p * LIVE : (p + 1) * LIVE, lanes].astype(bf16)
+    for p, ref in enumerate(a_refs[1:]):
+        ref[Zh * R * LIVE :, :] = side_ref[p + 1]
+    for copy in second:
+        copy.wait()
+    part = jnp.dot(g_ref[...], wb_ref[...], preferred_element_type=f32)
+    for n in range(3 * Zh):
+        z = n // 3
+        t = (Zh + z) * R + towards[n % 3]
+        block = part[:, n * 128 : (n + 1) * 128]
+        b_refs[n % 3][z * R * LIVE : (z + 1) * R * LIVE, :] = block.astype(bf16)
+        gain = block * n_ref[:, pl.ds(pl.multiple_of(t * 128, 128), 128)].astype(f32)
+        gain_ref[pl.ds(t, 1), :] = jnp.sum(gain, axis=0, keepdims=True)
 
 
 def near_rows(place, Zh, w0, w1, side, g, normed):
@@ -361,11 +348,11 @@
         in_specs=[SMEM, HBM, HBM, VMEM, VMEM, VMEM],
         out_specs=(VMEM,) * 7,
         scratch_shapes=[
-            pltpu.VMEM((4, 2 * V, 2 * R * 128), bf16),
-            pltpu.VMEM((rows, 2 * R * 128), f32),
-            pltpu.SemaphoreType.DMA((4, 2)),
+            pltpu.VMEM((2 * V, Zh * R * 128), bf16),
+            pltpu.VMEM((2 * V, 3 * Zh * 128), bf16),
+            pltpu.SemaphoreType.DMA((1 + 3 * Zh, 2)),
         ],
-        compiler_params=pltpu.CompilerParams(vmem_limit_bytes=28 << 20),
+        compiler_params=pltpu.CompilerParams(vmem_limit_bytes=24 << 20),
         name="near_rows",
     )(place, w0, w1, side, g, normed)
 
@@ -636,30 +623,46 @@
     )(sums, came, total)
 
 
-def finish_kernel(D, loss_ref, total_ref, hidden_ref, gain_ref, inv_ref, out_ref, sums_ref):
+def sums_kernel(loss_ref, total_ref, gain_ref, sums_ref):
+    tile = total_ref[0, LIVE:128, :].astype(f32)
+    for z in range(1, total_ref.shape[0]):
+        tile = tile + total_ref[z, LIVE:128, :].astype(f32)
+    _, target, gain = read_tile(tile, 3)
+    sums_ref[0:1, :] = gain / gain_ref[...]
+    sums_ref[1:2, :] = loss_ref[...] - target
+
+
+def last_sums(loss, total, norm_gain):
+    return pl.pallas_call(
+        sums_kernel,
+        out_shape=jax.ShapeDtypeStruct((2, 128), f32),
+        in_specs=[VMEM] * 3,
+        out_specs=VMEM,
+        name="last_sums",
+    )(loss, total, norm_gain.reshape(1, 128))
+
+
+def finish_kernel(D, total_ref, hidden_ref, gain_ref, inv_ref, out_ref):
     total = total_ref[0].astype(f32)
     for z in range(1, total_ref.shape[0]):
         total = total + total_ref[z].astype(f32)
-    inner, target, gain = read_tile(total[LIVE:128], 3)
+    inner = to_column(read_tile(total[LIVE:128], 1)[0])
     total = total[0:LIVE]
-    inner = to_column(inner)
     inv = inv_ref[...]
     activation = hidden_ref[0:LIVE, :].astype(f32)
     grad = inv * (total * gain_ref[...]) - activation * (inv * inv * (inner / D))
     out_ref[0:LIVE, :] = grad.astype(bf16)
     out_ref[LIVE:128, :] = jnp.zeros((128 - LIVE, 128), bf16)
-    sums_ref[0:1, :] = gain / gain_ref[...]
-    sums_ref[1:2, :] = loss_ref[...] - target
-
-
-def finish(D, loss, total, hidden, norm_gain, inv_rms):
+
+
+def finish(D, total, hidden, norm_gain, inv_rms):
     return pl.pallas_call(
         functools.partial(finish_kernel, D),
-        out_shape=(jax.ShapeDtypeStruct((128, 128), bf16), jax.ShapeDtypeStruct((2, 128), f32)),
-        in_specs=[VMEM] * 5,
-        out_specs=(VMEM, VMEM),
+        out_shape=jax.ShapeDtypeStruct((128, 128), bf16),
+        in_specs=[VMEM] * 4,
+        out_specs=VMEM,
         name="finish",
-    )(loss, total, hidden, norm_gain.reshape(1, 128), inv_rms)
+    )(total, hidden, norm_gain.reshape(1, 128), inv_rms)
 
 
 def body(hidden, norm_gain, head_weight, targets, span_starts, live_rows):
@@ -722,9 +725,11 @@
     b_sums = [outs[R]] + [shift(outs[R + k], "x", -k) for k in range(1, R)]
     total = gather_rows(Zh, outs[2 * R], outs[2 * R + 1], a_sums, b_sums)
     total = lax.all_to_all(total, "z", 0, 0)
-    hidden_grad, sums = finish(D, loss, total, hidden, norm_gain, inv_rms)
-
-    gain_grad, mean_loss = last(sums, shift(sums, "c", 1), live_total)
+    sums = last_sums(loss, total, norm_gain)
+    came = shift(sums, "c", 1)
+    hidden_grad = finish(D, total, hidden, norm_gain, inv_rms)
+    came, hidden_grad = lax.optimization_barrier((came, hidden_grad))
+    gain_grad, mean_loss = last(sums, came, live_total)
     gain_grad, mean_loss = gain_grad.reshape(128), mean_loss.reshape(())
     return (hidden_grad, gain_grad, weight_grad, mean_loss)
 

time: 162 us -> 161 us (level)
  starting transfers between devices: 55.5 us -> 47.5 us
  waiting for transfers between devices: 34.9 us -> 42.9 us
  local copies, waits for them, and re-layouts: 6.45 us -> 2.86 us
    ppermute x33 -> x31, starting transfers between devices: 49 us -> 41.1 us  [shift(): return lax.ppermute(x, axis, [(i, (i + k) % n) for i in range(n)])]
    ppermute x33 -> x31, waiting for transfers between devices: 24.5 us -> 32.5 us  [shift(): return lax.ppermute(x, axis, [(i, (i + k) % n) for i in range(n)])]
    slice x4 -> x0, local copies, waits for them, and re-layouts: 2.82 us -> none  [ring_gather(): two = (shift(one[:half], axis, 1), shift(three[half:], axis, -1))]
    pallas_call x1 -> x2, Pallas kernels: 1.75 us -> 3.33 us  [the longest x1 1.77 us: finish(): pl.pallas_call(functools.partial(finish_kernel, D), out_shape=jax.ShapeDt...]
    unnamed x16 -> x12, local copies, waits for them, and re-layouts: 3.55 us -> 2.78 us
  transfers between devices with their start and end apart: 34 -> 32, of which waited for: 13 -> 12; matrix products, arithmetic and copies ran while one was open for 2% -> 1% of each run, Pallas kernels for 10% -> 11%
where the time goes in v2:
time: 161 us
  starting transfers between devices  47.5 us (30%)
  waiting for transfers between devices  42.9 us (27%)
  Pallas kernels  33.3 us (21%)
  blocking collectives  32.3 us (20%)
  local copies, waits for them, and re-layouts  2.86 us (2%)
    ppermute x31, starting transfers between devices, shift(): return lax.ppermute(x, axis, [(i, (i + k) % n) for i in range(n)])  41.1 us
    ppermute x31, waiting for transfers between devices, shift(): return lax.ppermute(x, axis, [(i, (i + k) % n) for i in range(n)])  32.5 us
    all_to_all x1, blocking collectives, body(): every = lax.all_to_all(share, ('z', 'y', 'x'), 0, 0)  19.7 us
    all_to_all x1, blocking collectives, body(): total = lax.all_to_all(total, 'z', 0, 0)  12.6 us
    all_to_all x1, waiting for transfers between devices, body(): block = lax.all_to_all(block, 'z', 0, 0)  10.4 us
    pallas_call x1, Pallas kernels, forward(): pl.pallas_call(functools.partial(forward_kernel, Zh), out_shape=(jax.Shap...  8.37 us
    pallas_call x1, Pallas kernels, outer(): pl.pallas_call(outer_kernel, grid=(D // V,), out_shape=jax.ShapeDtypeStru...  7.49 us
    all_to_all x1, starting transfers between devices, body(): block = lax.all_to_all(block, 'z', 0, 0)  6.45 us
  transfers between devices with their start and end apart: 32, of which 12 were waited for; matrix products, arithmetic and copies ran while one was open for 1% of the time, Pallas kernels for 11%

profile of v2, /device:TPU:1, one launch (start us, length us, event | category | flops | bytes accessed | tf_op | source)
XLA Modules:
  0.0 160.6 jit_solution(15163797839424124406)
XLA Ops:
  0.6 3.3 %collective-permute-start = (bf16[512,4096]{1,0:T(8,128)(2,1)}, bf16[512,4096]{1,0:T(8,128)(2,1)}, u32[]{:S(2)}, u32[]{:S(2)}) collective-permute-start(bf16[512,4096]{1,0:T(8,128)(2,1)} %w0_ref.5), channel_id=1, source_target_pairs={{0,128},{128,0},{1,129},{129,1},{2,130},{130,2},{3,131},{131,3},{4... | collective-permute-start | bytes 12582920 | tf_op jit(solution)/shard_map/ppermute | solution.py:24
  4.0 1.5 prepare.1
  5.5 6.5 %all-to-all-start = ((bf16[8,128,128]{2,1,0:T(8,128)(2,1)}), bf16[8,128,128]{2,1,0:T(8,128)(2,1)S(1)}, u32[]{:S(2)}, u32[]{:S(2)}) async-start(bf16[8,128,128]{2,1,0:T(8,128)(2,1)} %get-tuple-element.83), calls=%async_computation | async-start | bytes 524288 | tf_op jit(solution)/shard_map/all_to_all | solution.py:682
  11.9 0.3 collective-permute-start.1
  12.2 1.0 collective-permute-done.1
  13.2 0.7 pad_add_fusion
  13.9 10.4 %all-to-all-done = bf16[8,128,128]{2,1,0:T(8,128)(2,1)S(1)} async-done(((bf16[8,128,128]{2,1,0:T(8,128)(2,1)}), bf16[8,128,128]{2,1,0:T(8,128)(2,1)S(1)}, u32[]{:S(2)}, u32[]{:S(2)}) %all-to-all-start) | async-done | bytes 262176 | tf_op jit(solution)/shard_map/all_to_all | solution.py:682
  24.3 0.0 collective-permute-done.w1_ref
  24.4 2.6 %collective-permute-start.10 = (bf16[464,128]{1,0:T(8,128)(2,1)S(1)}, bf16[464,128]{1,0:T(8,128)(2,1)S(1)}, u32[]{:S(2)}, u32[]{:S(2)}) collective-permute-start(bf16[464,128]{1,0:T(8,128)(2,1)S(1)} %pad_maximum_fusion.3.refs_0_), channel_id=1, source_target_pairs={{0,3},{1,0},{2,1},{3,2},{4,7},{5,4},{6,5},{7,6},{8,11},{9,8},{10,9... | collective-permute-start | bytes 356360 | tf_op jit(solution)/shard_map/ppermute | solution.py:24
  26.9 0.5 collective-permute-start.9
  27.4 0.6 collective-permute-start.8
  28.1 2.8 %collective-permute-start.4 = (bf16[576,128]{1,0:T(8,128)(2,1)S(1)}, bf16[576,128]{1,0:T(8,128)(2,1)S(1)}, u32[]{:S(2)}, u32[]{:S(2)}) collective-permute-start(bf16[576,128]{1,0:T(8,128)(2,1)S(1)} %pad_maximum_fusion.2.refs_4_), channel_id=1, source_target_pairs={{0,12},{4,0},{8,4},{12,8},{1,13},{5,1},{9,5},{13,9},{2,14},{6,2},{... | collective-permute-start | bytes 442376 | tf_op jit(solution)/shard_map/ppermute | solution.py:24
  30.9 0.3 collective-permute-start.3
  31.2 0.0 collective-permute-done.10.refs_3_
  31.2 0.7 collective-permute-start.2
  31.9 0.5 collective-permute-done.9.refs_2_
  32.4 3.6 %collective-permute-done.8.refs_1_ = bf16[464,128]{1,0:T(8,128)(2,1)S(1)} collective-permute-done((bf16[464,128]{1,0:T(8,128)(2,1)S(1)}, bf16[464,128]{1,0:T(8,128)(2,1)S(1)}, u32[]{:S(2)}, u32[]{:S(2)}) %collective-permute-start.8) | collective-permute-done | bytes 118816 | tf_op jit(solution)/shard_map/ppermute | solution.py:24
  36.1 1.4 collective-permute-start.11
  37.4 0.0 collective-permute-done.4.refs_7_
  37.5 0.0 collective-permute-done.3.refs_6_
  37.5 3.2 %collective-permute-done.2.refs_5_ = bf16[576,128]{1,0:T(8,128)(2,1)S(1)} collective-permute-done((bf16[576,128]{1,0:T(8,128)(2,1)S(1)}, bf16[576,128]{1,0:T(8,128)(2,1)S(1)}, u32[]{:S(2)}, u32[]{:S(2)}) %collective-permute-start.2) | collective-permute-done | bytes 147488 | tf_op jit(solution)/shard_map/ppermute | solution.py:24
  40.7 1.6 collective-permute-start.5
  42.3 1.2 collective-permute-start.6
  43.5 7.0 %collective-permute-done.11.refs_5_ = bf16[1792,128]{1,0:T(8,128)(2,1)S(1)} collective-permute-done((bf16[1792,128]{1,0:T(8,128)(2,1)S(1)}, bf16[1792,128]{1,0:T(8,128)(2,1)S(1)}, u32[]{:S(2)}, u32[]{:S(2)}) %collective-permute-start.11) | collective-permute-done | bytes 458784 | tf_op jit(solution)/shard_map/ppermute | solution.py:24
  50.5 1.7 %collective-permute-done.5.refs_1_ = bf16[1792,128]{1,0:T(8,128)(2,1)S(1)} collective-permute-done((bf16[1792,128]{1,0:T(8,128)(2,1)S(1)}, bf16[1792,128]{1,0:T(8,128)(2,1)S(1)}, u32[]{:S(2)}, u32[]{:S(2)}) %collective-permute-start.5) | collective-permute-done | bytes 458784 | tf_op jit(solution)/shard_map/ppermute | solution.py:24
  52.2 0.4 collective-permute-start.7
  52.6 0.1 pad_add_fusion.1.place_ref.y_ref
  52.7 2.2 %copy-done = bf16[512,4096]{1,0:T(8,128)(2,1)S(1)} copy-done((bf16[512,4096]{1,0:T(8,128)(2,1)S(1)}, bf16[512,4096]{1,0:T(8,128)(2,1)}, u32[]{:S(2)}) %copy-start) | copy-done | bytes 4194328
  54.8 0.1 read_meta.1
  55.0 7.7 %collective-permute-done.13.refs_7_ = bf16[1792,128]{1,0:T(8,128)(2,1)} collective-permute-done((bf16[1792,128]{1,0:T(8,128)(2,1)S(1)}, bf16[1792,128]{1,0:T(8,128)(2,1)}, u32[]{:S(2)}, u32[]{:S(2)}) %collective-permute-start.13) | collective-permute-done | bytes 458784 | tf_op jit(solution)/shard_map/ppermute | solution.py:24
  62.7 0.0 collective-permute-done.7.refs_3_
  62.7 8.4 %forward.1 = (bf16[448,4608]{1,0:T(8,128)(2,1)S(1)}, f32[112,1]{1,0:T(8,128)S(1)}, f32[448,1024]{1,0:T(8,128)S(1)}, f32[128,4,128]{2,1,0:T(4,128)S(1)}) custom-call(s32[4]{0:T(128)S(1)} %pad_add_fusion.1.place_ref.y_ref, bf16[512,4096]{1,0:T(8,128)(2,1)S(1)} %copy-done.1, bf16[512,4096]{1,0:T(8,128)(2,1)} %collective-permute-done.w1_ref, ...), custom_call_target="tpu_custom_call" | custom-call | flops 3758096384 | bytes 8388608 | tf_op jit(solution)/shard_map/forward/pallas_call | solution.py:150
  71.1 19.7 %all_to_all.15.every_ref = f32[128,4,128]{2,1,0:T(4,128)S(1)} all-to-all(f32[128,4,128]{2,1,0:T(4,128)S(1)} %get-tuple-element.101), channel_id=1, replica_groups=mesh['c'=2,'z'=8,'y'=4,'x'=4] {'z','y','x'}, dimensions={0} | all-to-all | bytes 524288 | tf_op jit(solution)/shard_map/all_to_all | solution.py:703
  90.8 4.0 %soft_rows.1 = (bf16[448,1024]{1,0:T(8,128)(2,1)S(1)}, bf16[448,4608]{1,0:T(8,128)(2,1)S(1)}, bf16[4,16,128]{2,1,0:T(8,128)(2,1)S(1)}, f32[1,128]{1,0:T(1,128)S(...) custom-call(s32[4]{0:T(128)S(1)} %pad_add_fusion.1.place_ref.y_ref, ...), custom_call_target="tpu_custom_call", output_to_operand_aliasing={{1}: (5, {})} | custom-call | tf_op jit(solution)/shard_map/soft_rows/pallas_call | solution.py:277
  94.9 0.0 copy-start.3
  94.9 0.3 collective-permute-start.14
  95.2 2.4 %collective-permute-start.15 = (bf16[896,128]{1,0:T(8,128)(2,1)S(1)}, bf16[896,128]{1,0:T(8,128)(2,1)S(1)}, u32[]{:S(2)}, u32[]{:S(2)}) collective-permute-start(bf16[896,128]{1,0:T(8,128)(2,1)S(1)} %get-tuple-element.119), channel_id=1, source_target_pairs={{0,3},{1,0},{2,1},{3,2},{4,7},{5,4},{6,5},{7,6},{8,11},{9,8},{10,9... | collective-permute-start | bytes 688136 | tf_op jit(solution)/shard_map/ppermute | solution.py:24
  97.6 0.4 collective-permute-start.16
  98.0 2.3 %collective-permute-start.17 = (bf16[896,128]{1,0:T(8,128)(2,1)S(1)}, bf16[896,128]{1,0:T(8,128)(2,1)S(1)}, u32[]{:S(2)}, u32[]{:S(2)}) collective-permute-start(bf16[896,128]{1,0:T(8,128)(2,1)S(1)} %get-tuple-element.121), channel_id=1, source_target_pairs={{0,12},{4,0},{8,4},{12,8},{1,13},{5,1},{9,5},{13,9},{2,14},{6,2},{... | collective-permute-start | bytes 688136 | tf_op jit(solution)/shard_map/ppermute | solution.py:24
  100.3 5.9 %near_rows.1 = (bf16[1792,128]{1,0:T(8,128)(2,1)S(1)}, bf16[1808,128]{1,0:T(8,128)(2,1)S(1)}, bf16[1808,128]{1,0:T(8,128)(2,1)S(1)}, bf16[1792,128]{1,0:T(8,128)...) custom-call(s32[4]{0:T(128)S(1)} %pad_add_fusion.1.place_ref.y_ref, ...), custom_call_target="tpu_custom_call" | custom-call | tf_op jit(solution)/shard_map/near_rows/pallas_call | solution.py:342
  106.3 4.7 %collective-permute-start.23 = (bf16[448,4608]{1,0:T(8,128)(2,1)S(1)}, bf16[448,4608]{1,0:T(8,128)(2,1)S(1)}, u32[]{:S(2)}, u32[]{:S(2)}) collective-permute-start(bf16[448,4608]{1,0:T(8,128)(2,1)S(1)} %get-tuple-element.139.n_ref), channel_id=1, source_target_pairs={{0,128},{128,0},{1,129},{129,1},{2,130},{130,2},{3,131},{131,3},{4... | collective-permute-start | bytes 12386312 | tf_op jit(solution)/shard_map/ppermute | solution.py:24
  111.0 0.1 relay.2
  111.2 0.1 collective-permute-start.19
  111.2 2.7 %collective-permute-start.20 = (bf16[1872,128]{1,0:T(8,128)(2,1)S(1)}, bf16[1872,128]{1,0:T(8,128)(2,1)S(1)}, u32[]{:S(2)}, u32[]{:S(2)}) collective-permute-start(bf16[1872,128]{1,0:T(8,128)(2,1)S(1)} %get-tuple-element.131), channel_id=1, source_target_pairs={{0,3},{1,0},{2,1},{3,2},{4,7},{5,4},{6,5},{7,6},{8,11},{9,8},{10,9... | collective-permute-start | bytes 1437704 | tf_op jit(solution)/shard_map/ppermute | solution.py:24
  113.9 0.1 relay.3
  114.0 0.1 collective-permute-start.21
  114.1 2.7 %collective-permute-start.22 = (bf16[1792,128]{1,0:T(8,128)(2,1)S(1)}, bf16[1792,128]{1,0:T(8,128)(2,1)S(1)}, u32[]{:S(2)}, u32[]{:S(2)}) collective-permute-start(bf16[1792,128]{1,0:T(8,128)(2,1)S(1)} %get-tuple-element.137), channel_id=1, source_target_pairs={{0,12},{4,0},{8,4},{12,8},{1,13},{5,1},{9,5},{13,9},{2,14},{6,2},{... | collective-permute-start | bytes 1376264 | tf_op jit(solution)/shard_map/ppermute | solution.py:24
  116.8 0.9 collective-permute-done.23.h_ref.m_ref
  117.7 7.5 %outer.1 = bf16[512,4096]{1,0:T(8,128)(2,1)} custom-call(bf16[448,1024]{1,0:T(8,128)(2,1)S(1)} %get-tuple-element.138.g_ref, bf16[448,4608]{1,0:T(8,128)(2,1)S(1)} %collective-permute-done.23.h_ref.m_ref, bf16[448,4608]{1,0:T(8,128)(2,1)S(1)} %get-tuple-element.139.n_ref, bf16[448,4608]{1,0:T(8,128)(2,1)S(1)} %collective-permute-done.23.h_ref.m_ref), custom_call_target="tpu_custom_call" | custom-call | flops 3758096384 | bytes 16777216 | tf_op jit(solution)/shard_map/outer/pallas_call | solution.py:590
  125.2 1.6 %collective-permute-done.21.b1 = bf16[1792,128]{1,0:T(8,128)(2,1)S(1)} collective-permute-done((bf16[1792,128]{1,0:T(8,128)(2,1)S(1)}, bf16[1792,128]{1,0:T(8,128)(2,1)S(1)}, u32[]{:S(2)}, u32[]{:S(2)}) %collective-permute-start.21) | collective-permute-done | bytes 458784 | tf_op jit(solution)/shard_map/ppermute | solution.py:24
  126.8 0.9 turn_rows.1
  127.8 1.0 collective-permute-start.27
  128.8 3.0 %collective-permute-start.25 = (bf16[480,128]{1,0:T(8,128)(2,1)S(1)}, bf16[480,128]{1,0:T(8,128)(2,1)S(1)}, u32[]{:S(2)}, u32[]{:S(2)}) collective-permute-start(bf16[480,128]{1,0:T(8,128)(2,1)S(1)} %get-tuple-element.149), channel_id=1, source_target_pairs={{0,8},{4,12},{8,0},{12,4},{1,9},{5,13},{9,1},{13,5},{2,10},{6,14},... | collective-permute-start | bytes 368648 | tf_op jit(solution)/shard_map/ppermute | solution.py:24
  131.7 0.7 collective-permute-start.28
  132.4 0.6 collective-permute-start.29
  133.0 4.2 %collective-permute-done.28.refs_6_ = bf16[448,128]{1,0:T(8,128)(2,1)S(1)} collective-permute-done((bf16[448,128]{1,0:T(8,128)(2,1)S(1)}, bf16[448,128]{1,0:T(8,128)(2,1)S(1)}, u32[]{:S(2)}, u32[]{:S(2)}) %collective-permute-start.28) | collective-permute-done | bytes 114720 | tf_op jit(solution)/shard_map/ppermute | solution.py:24
  137.2 1.1 collective-permute-done.29.refs_7_
  138.2 0.2 gather_rows.1
  138.4 12.6 %all_to_all.16.total_ref = bf16[8,128,128]{2,1,0:T(8,128)(2,1)} all-to-all(bf16[8,128,128]{2,1,0:T(8,128)(2,1)S(1)} %gather_rows.1), channel_id=1, replica_groups=mesh['c'=2,'z'=8,'y'=4,'x'=4] {'z'}, dimensions={0} | all-to-all | bytes 524288 | tf_op jit(solution)/shard_map/all_to_all | solution.py:727
  151.0 1.6 last_sums.1.sums_ref
  152.6 4.5 %collective-permute-start.30 = (f32[2,128]{1,0:T(2,128)}, f32[2,128]{1,0:T(2,128)S(1)}, u32[]{:S(2)}, u32[]{:S(2)}) collective-permute-start(f32[2,128]{1,0:T(2,128)} %last_sums.1.sums_ref), channel_id=1, source_target_pairs={{0,128},{128,0},{1,129},{129,1},{2,130},{130,2},{3,131},{131,3},{4... | collective-permute-start | bytes 3080 | tf_op jit(solution)/shard_map/ppermute | solution.py:24
  157.1 1.8 %finish.1 = bf16[128,128]{1,0:T(8,128)(2,1)} custom-call(bf16[8,128,128]{2,1,0:T(8,128)(2,1)} %all_to_all.16.total_ref, bf16[128,128]{1,0:T(8,128)(2,1)} %hidden_ref.3, f32[1,128]{1,0:T(1,128)} %bitcast.22, f32[112,1]{1,0:T(8,128)} %copy-done.2), custom_call_target="tpu_custom_call" | custom-call | tf_op jit(solution)/shard_map/finish/pallas_call | solution.py:659
  158.8 0.6 copy-done.5
  159.4 1.2 last.1
  (42 shorter events, 0.2 us)
Async XLA Ops:
  0.6 23.7 %collective-permute-start = (bf16[512,4096]{1,0:T(8,128)(2,1)}, bf16[512,4096]{1,0:T(8,128)(2,1)}, u32[]{:S(2)}, u32[]{:S(2)}) collective-permute-start(bf16[512,4096]{1,0:T(8,128)(2,1)} %w0_ref.5), channel_id=1, source_target_pairs={{0,128},{128,0},{1,129},{129,1},{2,130},{130,2},{3,131},{131,3},{4... | collective-permute-start | bytes 12582920 | tf_op jit(solution)/shard_map/ppermute | solution.py:24
  5.5 18.8 %all-to-all-start = ((bf16[8,128,128]{2,1,0:T(8,128)(2,1)}), bf16[8,128,128]{2,1,0:T(8,128)(2,1)S(1)}, u32[]{:S(2)}, u32[]{:S(2)}) async-start(bf16[8,128,128]{2,1,0:T(8,128)(2,1)} %get-tuple-element.83), calls=%async_computation | async-start | bytes 524288 | tf_op jit(solution)/shard_map/all_to_all | solution.py:682
  11.9 1.3 collective-permute-start.1
  24.4 6.9 %collective-permute-start.10 = (bf16[464,128]{1,0:T(8,128)(2,1)S(1)}, bf16[464,128]{1,0:T(8,128)(2,1)S(1)}, u32[]{:S(2)}, u32[]{:S(2)}) collective-permute-start(bf16[464,128]{1,0:T(8,128)(2,1)S(1)} %pad_maximum_fusion.3.refs_0_), channel_id=1, source_target_pairs={{0,3},{1,0},{2,1},{3,2},{4,7},{5,4},{6,5},{7,6},{8,11},{9,8},{10,9... | collective-permute-start | bytes 356360 | tf_op jit(solution)/shard_map/ppermute | solution.py:24
  26.9 5.5 %collective-permute-start.9 = (bf16[464,128]{1,0:T(8,128)(2,1)S(1)}, bf16[464,128]{1,0:T(8,128)(2,1)S(1)}, u32[]{:S(2)}, u32[]{:S(2)}) collective-permute-start(bf16[464,128]{1,0:T(8,128)(2,1)S(1)} %pad_maximum_fusion.3.refs_0_), channel_id=1, source_target_pairs={{0,2},{1,3},{2,0},{3,1},{4,6},{5,7},{6,4},{7,5},{8,10},{9,11},{10,... | collective-permute-start | bytes 356360 | tf_op jit(solution)/shard_map/ppermute | solution.py:24
  27.4 8.6 %collective-permute-start.8 = (bf16[464,128]{1,0:T(8,128)(2,1)S(1)}, bf16[464,128]{1,0:T(8,128)(2,1)S(1)}, u32[]{:S(2)}, u32[]{:S(2)}) collective-permute-start(bf16[464,128]{1,0:T(8,128)(2,1)S(1)} %pad_maximum_fusion.3.refs_0_), channel_id=1, source_target_pairs={{0,1},{1,2},{2,3},{3,0},{4,5},{5,6},{6,7},{7,4},{8,9},{9,10},{10,1... | collective-permute-start | bytes 356360 | tf_op jit(solution)/shard_map/ppermute | solution.py:24
  28.1 9.4 %collective-permute-start.4 = (bf16[576,128]{1,0:T(8,128)(2,1)S(1)}, bf16[576,128]{1,0:T(8,128)(2,1)S(1)}, u32[]{:S(2)}, u32[]{:S(2)}) collective-permute-start(bf16[576,128]{1,0:T(8,128)(2,1)S(1)} %pad_maximum_fusion.2.refs_4_), channel_id=1, source_target_pairs={{0,12},{4,0},{8,4},{12,8},{1,13},{5,1},{9,5},{13,9},{2,14},{6,2},{... | collective-permute-start | bytes 442376 | tf_op jit(solution)/shard_map/ppermute | solution.py:24
  30.9 6.6 %collective-permute-start.3 = (bf16[576,128]{1,0:T(8,128)(2,1)S(1)}, bf16[576,128]{1,0:T(8,128)(2,1)S(1)}, u32[]{:S(2)}, u32[]{:S(2)}) collective-permute-start(bf16[576,128]{1,0:T(8,128)(2,1)S(1)} %pad_maximum_fusion.2.refs_4_), channel_id=1, source_target_pairs={{0,8},{4,12},{8,0},{12,4},{1,9},{5,13},{9,1},{13,5},{2,10},{6,14},... | collective-permute-start | bytes 442376 | tf_op jit(solution)/shard_map/ppermute | solution.py:24
  31.2 9.4 %collective-permute-start.2 = (bf16[576,128]{1,0:T(8,128)(2,1)S(1)}, bf16[576,128]{1,0:T(8,128)(2,1)S(1)}, u32[]{:S(2)}, u32[]{:S(2)}) collective-permute-start(bf16[576,128]{1,0:T(8,128)(2,1)S(1)} %pad_maximum_fusion.2.refs_4_), channel_id=1, source_target_pairs={{0,4},{4,8},{8,12},{12,0},{1,5},{5,9},{9,13},{13,1},{2,6},{6,10},{... | collective-permute-start | bytes 442376 | tf_op jit(solution)/shard_map/ppermute | solution.py:24
  36.1 14.4 %collective-permute-start.11 = (bf16[1792,128]{1,0:T(8,128)(2,1)S(1)}, bf16[1792,128]{1,0:T(8,128)(2,1)S(1)}, u32[]{:S(2)}, u32[]{:S(2)}) collective-permute-start(bf16[1792,128]{1,0:T(8,128)(2,1)S(1)} %pad_maximum_fusion.1.refs_4_), channel_id=1, source_target_pairs={{0,4},{4,8},{8,12},{12,0},{1,5},{5,9},{9,13},{13,1},{2,6},{6,10},{... | collective-permute-start | bytes 1376264 | tf_op jit(solution)/shard_map/ppermute | solution.py:24
  40.7 11.4 %collective-permute-start.5 = (bf16[1792,128]{1,0:T(8,128)(2,1)S(1)}, bf16[1792,128]{1,0:T(8,128)(2,1)S(1)}, u32[]{:S(2)}, u32[]{:S(2)}) collective-permute-start(bf16[1792,128]{1,0:T(8,128)(2,1)S(1)} %pad_maximum_fusion.refs_0_), channel_id=1, source_target_pairs={{0,1},{1,2},{2,3},{3,0},{4,5},{5,6},{6,7},{7,4},{8,9},{9,10},{10,1... | collective-permute-start | bytes 1376264 | tf_op jit(solution)/shard_map/ppermute | solution.py:24
  42.3 12.6 %collective-permute-start.12 = (bf16[1792,128]{1,0:T(8,128)(2,1)S(1)}, bf16[1792,128]{1,0:T(8,128)(2,1)S(1)}, u32[]{:S(2)}, u32[]{:S(2)}) collective-permute-start(bf16[1792,128]{1,0:T(8,128)(2,1)S(1)} %pad_maximum_fusion.1.refs_4_), channel_id=1, source_target_pairs={{0,12},{4,0},{8,4},{12,8},{1,13},{5,1},{9,5},{13,9},{2,14},{6,2},{... | collective-permute-start | bytes 1376264 | tf_op jit(solution)/shard_map/ppermute | solution.py:24
  42.3 12.6 %collective-permute-start.6 = (bf16[1792,128]{1,0:T(8,128)(2,1)S(1)}, bf16[1792,128]{1,0:T(8,128)(2,1)}, u32[]{:S(2)}, u32[]{:S(2)}) collective-permute-start(bf16[1792,128]{1,0:T(8,128)(2,1)S(1)} %pad_maximum_fusion.refs_0_), channel_id=1, source_target_pairs={{0,3},{1,0},{2,1},{3,2},{4,7},{5,4},{6,5},{7,6},{8,11},{9,8},{10,9... | collective-permute-start | bytes 1376264 | tf_op jit(solution)/shard_map/ppermute | solution.py:24
  50.5 12.2 %collective-permute-start.13 = (bf16[1792,128]{1,0:T(8,128)(2,1)S(1)}, bf16[1792,128]{1,0:T(8,128)(2,1)}, u32[]{:S(2)}, u32[]{:S(2)}) collective-permute-start(bf16[1792,128]{1,0:T(8,128)(2,1)S(1)} %collective-permute-done.11.refs_5_), channel_id=1, source_target_pairs={{0,4},{4,8},{8,12},{12,0},{1,5},{5,9},{9,13},{13,1},{2,6},{6,10},{... | collective-permute-start | bytes 1376264 | tf_op jit(solution)/shard_map/ppermute | solution.py:24
  52.2 10.5 %collective-permute-start.7 = (bf16[1792,128]{1,0:T(8,128)(2,1)S(1)}, bf16[1792,128]{1,0:T(8,128)(2,1)}, u32[]{:S(2)}, u32[]{:S(2)}) collective-permute-start(bf16[1792,128]{1,0:T(8,128)(2,1)S(1)} %collective-permute-done.5.refs_1_), channel_id=1, source_target_pairs={{0,1},{1,2},{2,3},{3,0},{4,5},{5,6},{6,7},{7,4},{8,9},{9,10},{10,1... | collective-permute-start | bytes 1376264 | tf_op jit(solution)/shard_map/ppermute | solution.py:24
  52.7 2.2 %copy-start = (bf16[512,4096]{1,0:T(8,128)(2,1)S(1)}, bf16[512,4096]{1,0:T(8,128)(2,1)}, u32[]{:S(2)}) copy-start(bf16[512,4096]{1,0:T(8,128)(2,1)} %w0_ref.5) | copy-start | bytes 12582916
  54.8 7.9 %copy-start.1 = (bf16[512,4096]{1,0:T(8,128)(2,1)S(1)}, bf16[512,4096]{1,0:T(8,128)(2,1)}, u32[]{:S(2)}) copy-start(bf16[512,4096]{1,0:T(8,128)(2,1)} %w0_ref.5) | copy-start | bytes 12582916
  54.9 7.8 %copy-start.4 = (f32[1,128]{1,0:T(1,128)}, f32[1,128]{1,0:T(1,128)S(1)}, u32[]{:S(2)}) copy-start(f32[1,128]{1,0:T(1,128)S(1)} %get-tuple-element.158.total_ref) | copy-start | bytes 1540
  71.1 23.8 %copy-start.2 = (f32[112,1]{1,0:T(8,128)}, f32[112,1]{1,0:T(8,128)S(1)}, u32[]{:S(2)}) copy-start(f32[112,1]{1,0:T(8,128)S(1)} %get-tuple-element.155.inv_ref) | copy-start | bytes 1348
  94.9 11.4 %copy-start.3 = (f32[1,128]{1,0:T(1,128)}, f32[1,128]{1,0:T(1,128)S(1)}, u32[]{:S(2)}) copy-start(f32[1,128]{1,0:T(1,128)S(1)} %get-tuple-element.107.loss_ref) | copy-start | bytes 1540
  94.9 11.4 %collective-permute-start.14 = (bf16[912,128]{1,0:T(8,128)(2,1)S(1)}, bf16[912,128]{1,0:T(8,128)(2,1)S(1)}, u32[]{:S(2)}, u32[]{:S(2)}) collective-permute-start(bf16[912,128]{1,0:T(8,128)(2,1)S(1)} %get-tuple-element.118), channel_id=1, source_target_pairs={{0,1},{1,2},{2,3},{3,0},{4,5},{5,6},{6,7},{7,4},{8,9},{9,10},{10,1... | collective-permute-start | bytes 700424 | tf_op jit(solution)/shard_map/ppermute | solution.py:24
  95.2 11.0 %collective-permute-start.15 = (bf16[896,128]{1,0:T(8,128)(2,1)S(1)}, bf16[896,128]{1,0:T(8,128)(2,1)S(1)}, u32[]{:S(2)}, u32[]{:S(2)}) collective-permute-start(bf16[896,128]{1,0:T(8,128)(2,1)S(1)} %get-tuple-element.119), channel_id=1, source_target_pairs={{0,3},{1,0},{2,1},{3,2},{4,7},{5,4},{6,5},{7,6},{8,11},{9,8},{10,9... | collective-permute-start | bytes 688136 | tf_op jit(solution)/shard_map/ppermute | solution.py:24
  97.6 8.6 %collective-permute-start.16 = (bf16[896,128]{1,0:T(8,128)(2,1)S(1)}, bf16[896,128]{1,0:T(8,128)(2,1)S(1)}, u32[]{:S(2)}, u32[]{:S(2)}) collective-permute-start(bf16[896,128]{1,0:T(8,128)(2,1)S(1)} %get-tuple-element.120), channel_id=1, source_target_pairs={{0,4},{4,8},{8,12},{12,0},{1,5},{5,9},{9,13},{13,1},{2,6},{6,10},{... | collective-permute-start | bytes 688136 | tf_op jit(solution)/shard_map/ppermute | solution.py:24
  98.0 8.2 %collective-permute-start.17 = (bf16[896,128]{1,0:T(8,128)(2,1)S(1)}, bf16[896,128]{1,0:T(8,128)(2,1)S(1)}, u32[]{:S(2)}, u32[]{:S(2)}) collective-permute-start(bf16[896,128]{1,0:T(8,128)(2,1)S(1)} %get-tuple-element.121), channel_id=1, source_target_pairs={{0,12},{4,0},{8,4},{12,8},{1,13},{5,1},{9,5},{13,9},{2,14},{6,2},{... | collective-permute-start | bytes 688136 | tf_op jit(solution)/shard_map/ppermute | solution.py:24
  106.3 11.4 %collective-permute-start.23 = (bf16[448,4608]{1,0:T(8,128)(2,1)S(1)}, bf16[448,4608]{1,0:T(8,128)(2,1)S(1)}, u32[]{:S(2)}, u32[]{:S(2)}) collective-permute-start(bf16[448,4608]{1,0:T(8,128)(2,1)S(1)} %get-tuple-element.139.n_ref), channel_id=1, source_target_pairs={{0,128},{128,0},{1,129},{129,1},{2,130},{130,2},{3,131},{131,3},{4... | collective-permute-start | bytes 12386312 | tf_op jit(solution)/shard_map/ppermute | solution.py:24
  111.2 15.7 %collective-permute-start.19 = (bf16[1872,128]{1,0:T(8,128)(2,1)S(1)}, bf16[1872,128]{1,0:T(8,128)(2,1)S(1)}, u32[]{:S(2)}, u32[]{:S(2)}) collective-permute-start(bf16[1872,128]{1,0:T(8,128)(2,1)S(1)} %get-tuple-element.130), channel_id=1, source_target_pairs={{0,1},{1,2},{2,3},{3,0},{4,5},{5,6},{6,7},{7,4},{8,9},{9,10},{10,1... | collective-permute-start | bytes 1437704 | tf_op jit(solution)/shard_map/ppermute | solution.py:24
  111.2 15.6 %collective-permute-start.20 = (bf16[1872,128]{1,0:T(8,128)(2,1)S(1)}, bf16[1872,128]{1,0:T(8,128)(2,1)S(1)}, u32[]{:S(2)}, u32[]{:S(2)}) collective-permute-start(bf16[1872,128]{1,0:T(8,128)(2,1)S(1)} %get-tuple-element.131), channel_id=1, source_target_pairs={{0,3},{1,0},{2,1},{3,2},{4,7},{5,4},{6,5},{7,6},{8,11},{9,8},{10,9... | collective-permute-start | bytes 1437704 | tf_op jit(solution)/shard_map/ppermute | solution.py:24
  114.0 12.8 %collective-permute-start.21 = (bf16[1792,128]{1,0:T(8,128)(2,1)S(1)}, bf16[1792,128]{1,0:T(8,128)(2,1)S(1)}, u32[]{:S(2)}, u32[]{:S(2)}) collective-permute-start(bf16[1792,128]{1,0:T(8,128)(2,1)S(1)} %get-tuple-element.136), channel_id=1, source_target_pairs={{0,4},{4,8},{8,12},{12,0},{1,5},{5,9},{9,13},{13,1},{2,6},{6,10},{... | collective-permute-start | bytes 1376264 | tf_op jit(solution)/shard_map/ppermute | solution.py:24
  114.1 12.7 %collective-permute-start.22 = (bf16[1792,128]{1,0:T(8,128)(2,1)S(1)}, bf16[1792,128]{1,0:T(8,128)(2,1)S(1)}, u32[]{:S(2)}, u32[]{:S(2)}) collective-permute-start(bf16[1792,128]{1,0:T(8,128)(2,1)S(1)} %get-tuple-element.137), channel_id=1, source_target_pairs={{0,12},{4,0},{8,4},{12,8},{1,13},{5,1},{9,5},{13,9},{2,14},{6,2},{... | collective-permute-start | bytes 1376264 | tf_op jit(solution)/shard_map/ppermute | solution.py:24
  117.7 9.1 %collective-permute-start.18 = (f32[32,128]{1,0:T(8,128)S(1)}, f32[32,128]{1,0:T(8,128)S(1)}, u32[]{:S(2)}, u32[]{:S(2)}) collective-permute-start(f32[32,128]{1,0:T(8,128)S(1)} %get-tuple-element.128.mine), channel_id=1, source_target_pairs={{0,2},{1,3},{2,0},{3,1},{4,6},{5,7},{6,4},{7,5},{8,10},{9,11},{10,... | collective-permute-start | bytes 49160 | tf_op jit(solution)/shard_map/ppermute | solution.py:24
  127.8 4.6 %collective-permute-start.27 = (bf16[448,128]{1,0:T(8,128)(2,1)S(1)}, bf16[448,128]{1,0:T(8,128)(2,1)S(1)}, u32[]{:S(2)}, u32[]{:S(2)}) collective-permute-start(bf16[448,128]{1,0:T(8,128)(2,1)S(1)} %get-tuple-element.152), channel_id=1, source_target_pairs={{0,3},{1,0},{2,1},{3,2},{4,7},{5,4},{6,5},{7,6},{8,11},{9,8},{10,9... | collective-permute-start | bytes 344072 | tf_op jit(solution)/shard_map/ppermute | solution.py:24
  128.7 9.5 %collective-permute-start.24 = (bf16[480,128]{1,0:T(8,128)(2,1)S(1)}, bf16[480,128]{1,0:T(8,128)(2,1)S(1)}, u32[]{:S(2)}, u32[]{:S(2)}) collective-permute-start(bf16[480,128]{1,0:T(8,128)(2,1)S(1)} %get-tuple-element.148), channel_id=1, source_target_pairs={{0,4},{4,8},{8,12},{12,0},{1,5},{5,9},{9,13},{13,1},{2,6},{6,10},{... | collective-permute-start | bytes 368648 | tf_op jit(solution)/shard_map/ppermute | solution.py:24
  128.8 9.5 %collective-permute-start.25 = (bf16[480,128]{1,0:T(8,128)(2,1)S(1)}, bf16[480,128]{1,0:T(8,128)(2,1)S(1)}, u32[]{:S(2)}, u32[]{:S(2)}) collective-permute-start(bf16[480,128]{1,0:T(8,128)(2,1)S(1)} %get-tuple-element.149), channel_id=1, source_target_pairs={{0,8},{4,12},{8,0},{12,4},{1,9},{5,13},{9,1},{13,5},{2,10},{6,14},... | collective-permute-start | bytes 368648 | tf_op jit(solution)/shard_map/ppermute | solution.py:24
  131.7 6.5 %collective-permute-start.26 = (bf16[480,128]{1,0:T(8,128)(2,1)S(1)}, bf16[480,128]{1,0:T(8,128)(2,1)S(1)}, u32[]{:S(2)}, u32[]{:S(2)}) collective-permute-start(bf16[480,128]{1,0:T(8,128)(2,1)S(1)} %get-tuple-element.150), channel_id=1, source_target_pairs={{0,12},{4,0},{8,4},{12,8},{1,13},{5,1},{9,5},{13,9},{2,14},{6,2},{... | collective-permute-start | bytes 368648 | tf_op jit(solution)/shard_map/ppermute | solution.py:24
  131.7 5.4 %collective-permute-start.28 = (bf16[448,128]{1,0:T(8,128)(2,1)S(1)}, bf16[448,128]{1,0:T(8,128)(2,1)S(1)}, u32[]{:S(2)}, u32[]{:S(2)}) collective-permute-start(bf16[448,128]{1,0:T(8,128)(2,1)S(1)} %get-tuple-element.153), channel_id=1, source_target_pairs={{0,2},{1,3},{2,0},{3,1},{4,6},{5,7},{6,4},{7,5},{8,10},{9,11},{10,... | collective-permute-start | bytes 344072 | tf_op jit(solution)/shard_map/ppermute | solution.py:24
  132.4 5.8 %collective-permute-start.29 = (bf16[448,128]{1,0:T(8,128)(2,1)S(1)}, bf16[448,128]{1,0:T(8,128)(2,1)S(1)}, u32[]{:S(2)}, u32[]{:S(2)}) collective-permute-start(bf16[448,128]{1,0:T(8,128)(2,1)S(1)} %get-tuple-element.154), channel_id=1, source_target_pairs={{0,1},{1,2},{2,3},{3,0},{4,5},{5,6},{6,7},{7,4},{8,9},{9,10},{10,1... | collective-permute-start | bytes 344072 | tf_op jit(solution)/shard_map/ppermute | solution.py:24
  152.6 6.3 %collective-permute-start.30 = (f32[2,128]{1,0:T(2,128)}, f32[2,128]{1,0:T(2,128)S(1)}, u32[]{:S(2)}, u32[]{:S(2)}) collective-permute-start(f32[2,128]{1,0:T(2,128)} %last_sums.1.sums_ref), channel_id=1, source_target_pairs={{0,128},{128,0},{1,129},{129,1},{2,130},{130,2},{3,131},{131,3},{4... | collective-permute-start | bytes 3080 | tf_op jit(solution)/shard_map/ppermute | solution.py:24
  158.8 0.6 copy-start.5

commit v3 on v2

--- a/solution.py
+++ b/solution.py
@@ -24,9 +24,15 @@
     return lax.ppermute(x, axis, [(i, (i + k) % n) for i in range(n)])
 
 
+def around(x, axis, k):
+    n = lax.axis_size(axis)
+    pairs = [(c * n + i, c * n + (i + (k, -k)[c]) % n) for c in range(2) for i in range(n)]
+    return lax.ppermute(x, ("c", axis), pairs)
+
+
 def ring_gather(block, axis):
-    one = shift(block, axis, 1)
-    return block, one, shift(block, axis, -1), shift(one, axis, 1)
+    one = around(block, axis, 1)
+    return block, one, around(block, axis, -1), around(one, axis, 1)
 
 
 PARTS = ((0, 0, 4), (1, 0, 4), (3, 0, 4), (2, 0, 4))
@@ -50,8 +56,8 @@
     return jnp.sum(jnp.where(same(), row, 0.0), axis=1, keepdims=True)
 
 
-def place_of(x, p):
-    return lax.rem(x - ORDER[p] + R, R)
+def place_of(place_ref, p):
+    return lax.rem(place_ref[1] - place_ref[4] * ORDER[p] + R, R)
 
 
 def forward_kernel(Zh, place_ref, w0_ref, w1_ref, gain_ref, *refs):
@@ -98,7 +104,7 @@
 
     def scale(ref, i, k, p, half):
         inv = total_ref[p]
-        y = lax.rem(place_ref[0] - k + R, R)
+        y = lax.rem(place_ref[0] - place_ref[4] * k + R, R)
         rows = pl.ds(pl.multiple_of(p * LIVE, 16), LIVE)
 
         def one(z, _):
@@ -140,7 +146,7 @@
         logits = l_ref[p * LIVE : (p + 1) * LIVE, :]
         top = jnp.max(logits, axis=1, keepdims=True)
         here = top + jnp.log(jnp.sum(jnp.exp(logits - top), axis=1, keepdims=True))
-        share = jnp.where(place == place_of(place_ref[1], p), to_row(here), share)
+        share = jnp.where(place == place_of(place_ref, p), to_row(here), share)
     share_ref[...] = jnp.broadcast_to(share[None], share_ref.shape)
 
 
@@ -220,7 +226,7 @@
         inner, target, loss = sums
         rows = pl.ds(pl.multiple_of(p * LIVE, 16), LIVE)
         distance = jnp.where(p < 2, p, 5 - p)
-        here = lax.rem(place_ref[1] - distance + R, R)
+        here = lax.rem(place_ref[1] - place_ref[4] * distance + R, R)
         total = jnp.sum(jnp.where(place == here, log_total, 0.0), axis=0, keepdims=True)
         pick_row = lambda ref: jnp.sum(jnp.where(place == p, ref[...], 0.0), axis=0, keepdims=True)
         live = pick_row(live_ref)
@@ -294,7 +300,7 @@
     a_refs, b_refs, (gain_ref, wa_ref, wb_ref, sems) = refs[:3], refs[3:6], refs[6:]
     V = w0_ref.shape[0]
     wide = Zh * R * 128
-    towards = [lax.rem(place_ref[0] + k, R) for k in (0, 1, 3)]
+    towards = [lax.rem(place_ref[0] + place_ref[4] * k + R, R) for k in (0, 1, 3)]
     first, second = [], []
     for i, w in enumerate((w0_ref, w1_ref)):
         rows = pl.ds(i * V, V)
@@ -403,7 +409,7 @@
     def one(z, _):
         to = pl.ds(pl.multiple_of(z * LIVE, 16), LIVE)
         for k in range(R):
-            row = pl.multiple_of((z * R + lax.rem(y_ref[0] + k, R)) * LIVE, 16)
+            row = pl.multiple_of((z * R + lax.rem(y_ref[0] + y_ref[4] * k + R, R)) * LIVE, 16)
             rows = pl.ds(row, LIVE)
             total = a0[rows, :].astype(f32) + a1[rows, :].astype(f32) + a2[rows, :].astype(f32)
             outs[k][to, :] = total.astype(outs[k].dtype)
@@ -429,7 +435,7 @@
     for k in range(R):
         gain = jnp.zeros((Z, 128), f32)
         for z in range(Z):
-            line = gain_ref[pl.ds(z * R + lax.rem(y_ref[0] + k, R), 1), :]
+            line = gain_ref[pl.ds(z * R + lax.rem(y_ref[0] + y_ref[4] * k + R, R), 1), :]
             gain = jnp.where(place == z, line, gain)
         if k == 0:
             outs[2 * R + 1][...] = gain
@@ -536,9 +542,10 @@
     label_ref, live_ref, factor_ref, total_ref, gain_ref = refs[2 * R :]
     Z = gain_ref.shape[0] // R
     for k, ref in enumerate(a_refs):
+        pieces = ref[at:, :].astype(f32)
         for z in range(Z):
-            pieces = ref[at + z * 16 : at + (z + 1) * 16, :].astype(f32)
-            gain_ref[k * Z + z : k * Z + z + 1, :] = pieces[0:1] + pieces[1:2] + pieces[2:3]
+            three = [pieces[3 * z + i : 3 * z + i + 1] for i in range(3)]
+            gain_ref[k * Z + z : k * Z + z + 1, :] = three[0] + three[1] + three[2]
     place = lax.broadcasted_iota(jnp.int32, (R, 128), 0)
     labels, live, total = jnp.zeros((R, 128), f32), jnp.zeros((R, 128), f32), jnp.zeros((1, 1), f32)
     for p, j in enumerate(ORDER):
@@ -673,7 +680,7 @@
     c, z, y, x = (lax.axis_index(a) for a in "czyx")
     spot = (z * Y + y) * X + x
     first, second = (c * (Z * Y * X) + spot) * V, ((1 - c) * (Z * Y * X) + spot) * V
-    place = jnp.stack([y, x, first, second]).astype(jnp.int32)
+    place = jnp.stack([y, x, first, second, 1 - 2 * c]).astype(jnp.int32)
 
     live_other = shift(live_rows, "c", 1)
     weight_other = shift(head_weight, "c", 1)
@@ -683,12 +690,13 @@
     meta = meta + jnp.pad(live_other[None].astype(bf16), ((4, 11), (0, 0)))
     block, weight_other, meta = lax.optimization_barrier((block, weight_other, meta))
 
+    pieces = block[:, LIVE : LIVE + 3].reshape(3 * Z, 128)
     a_block = jnp.concatenate(
-        [block[:Zh, :LIVE].reshape(-1, 128), block[:, LIVE:].reshape(-1, 128)]
+        [block[:Zh, :LIVE].reshape(-1, 128), jnp.pad(pieces, ((0, -3 * Z % 16), (0, 0)))]
     )
     b_block = jnp.concatenate([block[Zh:, :LIVE].reshape(-1, 128), meta])
-    a_blocks = [a_block] + [shift(a_block, "y", k) for k in range(1, R)]
-    b_blocks = [b_block] + [shift(b_block, "x", k) for k in range(1, R)]
+    a_blocks = [a_block] + [around(a_block, "y", k) for k in range(1, R)]
+    b_blocks = [b_block] + [around(b_block, "x", k) for k in range(1, R)]
     a_all = ring_gather(jnp.concatenate([a[: Zh * LIVE] for a in a_blocks]), "x")
     b_all = ring_gather(jnp.concatenate([b[: Zh * LIVE] for b in b_blocks]), "y")
     labels, live, factor, live_total, gain = read_meta(
@@ -705,8 +713,8 @@
         place, Zh, *weights, every, logits, normed, labels, live, factor
     )
 
-    a_low, a_high = shift(a_low, "x", 1), shift(a_high, "x", -1)
-    b_low, b_high = shift(b_low, "y", 1), shift(b_high, "y", -1)
+    a_low, a_high = around(a_low, "x", 1), around(a_high, "x", -1)
+    b_low, b_high = around(b_low, "y", 1), around(b_high, "y", -1)
     near = near_rows(place, Zh, *weights, side, g, normed)
     near, a_low, a_high, b_low, b_high, g, normed = lax.optimization_barrier(
         (near, a_low, a_high, b_low, b_high, g, normed)
@@ -715,14 +723,14 @@
     a0, a1, a3, b0, b1, b3, gain_near = near
     a_up, a_down, gain = relay(a3, a1, a_low, a_high, gain_far, gain_near)
     b_up, b_down = relay(b1, b3, b_low, b_high)
-    a_in = shift(a_up, "x", 1), shift(a_down, "x", -1)
-    b_in = shift(b_up, "y", 1), shift(b_down, "y", -1)
-    gain_in = shift(gain, "x", 2)
+    a_in = around(a_up, "x", 1), around(a_down, "x", -1)
+    b_in = around(b_up, "y", 1), around(b_down, "y", -1)
+    gain_in = around(gain, "x", 2)
     weight_grad = outer(g, normed, theirs, D)
     a_in, b_in, weight_grad = lax.optimization_barrier((a_in, b_in, weight_grad))
     outs = turn_rows(place, Zh, side, gain, gain_in, (a0, *a_in), (b0, *b_in))
-    a_sums = [outs[0]] + [shift(outs[k], "y", k) for k in range(1, R)]
-    b_sums = [outs[R]] + [shift(outs[R + k], "x", -k) for k in range(1, R)]
+    a_sums = [outs[0]] + [around(outs[k], "y", k) for k in range(1, R)]
+    b_sums = [outs[R]] + [around(outs[R + k], "x", -k) for k in range(1, R)]
     total = gather_rows(Zh, outs[2 * R], outs[2 * R + 1], a_sums, b_sums)
     total = lax.all_to_all(total, "z", 0, 0)
     sums = last_sums(loss, total, norm_gain)

time: 161 us -> 159 us (0.988)
  waiting for transfers between devices: 42.9 us -> 28.5 us
  starting transfers between devices: 47.5 us -> 58.5 us
    ppermute x0 -> x27, starting transfers between devices: none -> 32.2 us  [around(): return lax.ppermute(x, ('c', axis), pairs)]
    ppermute x31 -> x4, waiting for transfers between devices: 32.5 us -> 4.26 us  [shift(): return lax.ppermute(x, axis, [(i, (i + k) % n) for i in range(n)])]
    ppermute x31 -> x4, starting transfers between devices: 41.1 us -> 19.9 us  [shift(): return lax.ppermute(x, axis, [(i, (i + k) % n) for i in range(n)])]
    ppermute x0 -> x27, waiting for transfers between devices: none -> 13.9 us  [around(): return lax.ppermute(x, ('c', axis), pairs)]
where the time goes in v3:
time: 159 us; the launch traced here: 158 us
  starting transfers between devices  58.5 us (37%)
  Pallas kernels  33.7 us (21%)
  blocking collectives  32.6 us (21%)
  waiting for transfers between devices  28.5 us (18%)
  local copies, waits for them, and re-layouts  2.96 us (2%)
    ppermute x27, starting transfers between devices, around(): return lax.ppermute(x, ('c', axis), pairs)  32.2 us
    all_to_all x1, blocking collectives, body(): every = lax.all_to_all(share, ('z', 'y', 'x'), 0, 0)  20.1 us
    ppermute x4, starting transfers between devices, shift(): return lax.ppermute(x, axis, [(i, (i + k) % n) for i in range(n)])  19.9 us
    ppermute x27, waiting for transfers between devices, around(): return lax.ppermute(x, ('c', axis), pairs)  13.9 us
    all_to_all x1, blocking collectives, body(): total = lax.all_to_all(total, 'z', 0, 0)  12.5 us
    all_to_all x1, waiting for transfers between devices, body(): block = lax.all_to_all(block, 'z', 0, 0)  10.4 us
    pallas_call x1, Pallas kernels, forward(): pl.pallas_call(functools.partial(forward_kernel, Zh), out_shape=(jax.Shap...  8.32 us
    pallas_call x1, Pallas kernels, outer(): pl.pallas_call(outer_kernel, grid=(D // V,), out_shape=jax.ShapeDtypeStru...  7.47 us
  transfers between devices with their start and end apart: 32, of which 12 were waited for; matrix products, arithmetic and copies ran while one was open for 1% of the time, Pallas kernels for 11%

profile of v3, /device:TPU:1, one launch (start us, length us, event | category | flops | bytes accessed | tf_op | source)
XLA Modules:
  0.0 158.0 jit_solution(6770464940214729053)
XLA Ops:
  0.6 3.3 %collective-permute-start = (bf16[512,4096]{1,0:T(8,128)(2,1)}, bf16[512,4096]{1,0:T(8,128)(2,1)}, u32[]{:S(2)}, u32[]{:S(2)}) collective-permute-start(bf16[512,4096]{1,0:T(8,128)(2,1)} %w0_ref.5), channel_id=1, source_target_pairs={{0,128},{128,0},{1,129},{129,1},{2,130},{130,2},{3,131},{131,3},{4... | collective-permute-start | bytes 12582920 | tf_op jit(solution)/shard_map/ppermute | solution.py:24
  4.0 1.5 prepare.1
  5.5 6.5 %all-to-all-start = ((bf16[8,128,128]{2,1,0:T(8,128)(2,1)}), bf16[8,128,128]{2,1,0:T(8,128)(2,1)S(1)}, u32[]{:S(2)}, u32[]{:S(2)}) async-start(bf16[8,128,128]{2,1,0:T(8,128)(2,1)} %get-tuple-element.83), calls=%async_computation | async-start | bytes 524288 | tf_op jit(solution)/shard_map/all_to_all | solution.py:689
  11.9 0.3 collective-permute-start.1
  12.2 1.0 collective-permute-done.1
  13.2 0.7 pad_add_fusion
  13.9 10.4 %all-to-all-done = bf16[8,128,128]{2,1,0:T(8,128)(2,1)S(1)} async-done(((bf16[8,128,128]{2,1,0:T(8,128)(2,1)}), bf16[8,128,128]{2,1,0:T(8,128)(2,1)S(1)}, u32[]{:S(2)}, u32[]{:S(2)}) %all-to-all-start) | async-done | bytes 262176 | tf_op jit(solution)/shard_map/all_to_all | solution.py:689
  24.4 1.3 collective-permute-start.10
  25.6 2.5 %collective-permute-start.9 = (bf16[464,128]{1,0:T(8,128)(2,1)S(1)}, bf16[464,128]{1,0:T(8,128)(2,1)S(1)}, u32[]{:S(2)}, u32[]{:S(2)}) collective-permute-start(bf16[464,128]{1,0:T(8,128)(2,1)S(1)} %pad_maximum_fusion.2.refs_0_), channel_id=1, source_target_pairs={{0,2},{1,3},{2,0},{3,1},{128,130},{129,131},{130,128},{131,129},{4... | collective-permute-start | bytes 356360 | tf_op jit(solution)/shard_map/ppermute | solution.py:30
  28.1 1.1 collective-permute-start.8
  29.3 1.4 collective-permute-start.4
  30.7 2.6 %collective-permute-start.3 = (bf16[480,128]{1,0:T(8,128)(2,1)S(1)}, bf16[480,128]{1,0:T(8,128)(2,1)S(1)}, u32[]{:S(2)}, u32[]{:S(2)}) collective-permute-start(bf16[480,128]{1,0:T(8,128)(2,1)S(1)} %fusion.1.refs_4_), channel_id=1, source_target_pairs={{0,8},{4,12},{8,0},{12,4},{128,136},{132,140},{136,128},{140,132},... | collective-permute-start | bytes 368648 | tf_op jit(solution)/shard_map/ppermute | solution.py:30
  33.3 0.0 collective-permute-done.10.refs_3_
  33.3 1.1 collective-permute-start.2
  34.4 0.0 collective-permute-done.8.refs_1_
  34.5 1.6 %collective-permute-start.11 = (bf16[1792,128]{1,0:T(8,128)(2,1)S(1)}, bf16[1792,128]{1,0:T(8,128)(2,1)S(1)}, u32[]{:S(2)}, u32[]{:S(2)}) collective-permute-start(bf16[1792,128]{1,0:T(8,128)(2,1)S(1)} %pad_maximum_fusion.1.refs_4_), channel_id=1, source_target_pairs={{0,4},{4,8},{8,12},{12,0},{128,140},{132,128},{136,132},{140,136},... | collective-permute-start | bytes 1376264 | tf_op jit(solution)/shard_map/ppermute | solution.py:30
  36.1 0.8 collective-permute-done.3.refs_6_
  36.9 1.5 collective-permute-done.2.refs_5_
  38.4 1.3 collective-permute-start.5
  39.7 0.0 collective-permute-start.12
  39.7 1.4 collective-permute-start.6
  41.0 2.1 %collective-permute-done.11.refs_5_ = bf16[1792,128]{1,0:T(8,128)(2,1)S(1)} collective-permute-done((bf16[1792,128]{1,0:T(8,128)(2,1)S(1)}, bf16[1792,128]{1,0:T(8,128)(2,1)S(1)}, u32[]{:S(2)}, u32[]{:S(2)}) %collective-permute-start.11) | collective-permute-done | bytes 458784 | tf_op jit(solution)/shard_map/ppermute | solution.py:30
  43.2 3.4 %collective-permute-start.13 = (bf16[1792,128]{1,0:T(8,128)(2,1)S(1)}, bf16[1792,128]{1,0:T(8,128)(2,1)}, u32[]{:S(2)}, u32[]{:S(2)}) collective-permute-start(bf16[1792,128]{1,0:T(8,128)(2,1)S(1)} %collective-permute-done.11.refs_5_), channel_id=1, source_target_pairs={{0,4},{4,8},{8,12},{12,0},{128,140},{132,128},{136,132},{140,136},... | collective-permute-start | bytes 1376264 | tf_op jit(solution)/shard_map/ppermute | solution.py:30
  46.6 1.9 %collective-permute-start.7 = (bf16[1792,128]{1,0:T(8,128)(2,1)S(1)}, bf16[1792,128]{1,0:T(8,128)(2,1)}, u32[]{:S(2)}, u32[]{:S(2)}) collective-permute-start(bf16[1792,128]{1,0:T(8,128)(2,1)S(1)} %collective-permute-done.5.refs_1_), channel_id=1, source_target_pairs={{0,1},{1,2},{2,3},{3,0},{128,131},{129,128},{130,129},{131,130},{4... | collective-permute-start | bytes 1376264 | tf_op jit(solution)/shard_map/ppermute | solution.py:30
  48.5 0.1 stack.23.place_ref.y_ref
  48.6 2.2 %copy-done = bf16[512,4096]{1,0:T(8,128)(2,1)S(1)} copy-done((bf16[512,4096]{1,0:T(8,128)(2,1)S(1)}, bf16[512,4096]{1,0:T(8,128)(2,1)}, u32[]{:S(2)}) %copy-start) | copy-done | bytes 4194328
  50.8 0.1 read_meta.1
  50.9 1.5 collective-permute-done.6.refs_2_
  52.4 2.8 %collective-permute-done.13.refs_7_ = bf16[1792,128]{1,0:T(8,128)(2,1)} collective-permute-done((bf16[1792,128]{1,0:T(8,128)(2,1)S(1)}, bf16[1792,128]{1,0:T(8,128)(2,1)}, u32[]{:S(2)}, u32[]{:S(2)}) %collective-permute-start.13) | collective-permute-done | bytes 458784 | tf_op jit(solution)/shard_map/ppermute | solution.py:30
  55.2 1.2 collective-permute-done.7.refs_3_
  56.4 8.3 %forward.1 = (bf16[448,4608]{1,0:T(8,128)(2,1)S(1)}, f32[112,1]{1,0:T(8,128)S(1)}, f32[448,1024]{1,0:T(8,128)S(1)}, f32[128,4,128]{2,1,0:T(4,128)S(1)}) custom-call(s32[5]{0:T(128)S(1)} %stack.23.place_ref.y_ref, bf16[512,4096]{1,0:T(8,128)(2,1)S(1)} %copy-done.1, bf16[512,4096]{1,0:T(8,128)(2,1)} %collective-permute-done.w1_ref, ...), custom_call_target="tpu_custom_call" | custom-call | flops 3758096384 | bytes 8388608 | tf_op jit(solution)/shard_map/forward/pallas_call | solution.py:156
  64.7 20.1 %all_to_all.15.every_ref = f32[128,4,128]{2,1,0:T(4,128)S(1)} all-to-all(f32[128,4,128]{2,1,0:T(4,128)S(1)} %get-tuple-element.101), channel_id=1, replica_groups=mesh['c'=2,'z'=8,'y'=4,'x'=4] {'z','y','x'}, dimensions={0} | all-to-all | bytes 524288 | tf_op jit(solution)/shard_map/all_to_all | solution.py:711
  84.9 4.2 %soft_rows.1 = (bf16[448,1024]{1,0:T(8,128)(2,1)S(1)}, bf16[448,4608]{1,0:T(8,128)(2,1)S(1)}, bf16[4,16,128]{2,1,0:T(8,128)(2,1)S(1)}, f32[1,128]{1,0:T(1,128)S(...) custom-call(s32[5]{0:T(128)S(1)} %stack.23.place_ref.y_ref, ...), custom_call_target="tpu_custom_call", output_to_operand_aliasing={{1}: (5, {})} | custom-call | tf_op jit(solution)/shard_map/soft_rows/pallas_call | solution.py:283
  89.1 0.0 copy-start.3
  89.1 0.7 collective-permute-start.14
  89.8 0.8 collective-permute-start.15
  90.7 0.2 collective-permute-start.16
  90.9 1.2 collective-permute-start.17
  92.1 6.1 %near_rows.1 = (bf16[1792,128]{1,0:T(8,128)(2,1)S(1)}, bf16[1808,128]{1,0:T(8,128)(2,1)S(1)}, bf16[1808,128]{1,0:T(8,128)(2,1)S(1)}, bf16[1792,128]{1,0:T(8,128)...) custom-call(s32[5]{0:T(128)S(1)} %stack.23.place_ref.y_ref, ...), custom_call_target="tpu_custom_call" | custom-call | tf_op jit(solution)/shard_map/near_rows/pallas_call | solution.py:348
  98.3 10.7 %collective-permute-start.23 = (bf16[448,4608]{1,0:T(8,128)(2,1)S(1)}, bf16[448,4608]{1,0:T(8,128)(2,1)S(1)}, u32[]{:S(2)}, u32[]{:S(2)}) collective-permute-start(bf16[448,4608]{1,0:T(8,128)(2,1)S(1)} %get-tuple-element.139.n_ref), channel_id=1, source_target_pairs={{0,128},{128,0},{1,129},{129,1},{2,130},{130,2},{3,131},{131,3},{4... | collective-permute-start | bytes 12386312 | tf_op jit(solution)/shard_map/ppermute | solution.py:24
  109.0 0.1 relay.2
  109.2 0.1 collective-permute-start.19
  109.3 1.5 collective-permute-start.20
  110.8 0.1 relay.3
  110.9 0.8 collective-permute-start.21
  111.6 0.8 collective-permute-start.22
  112.4 3.3 %collective-permute-done.23.h_ref.m_ref = bf16[448,4608]{1,0:T(8,128)(2,1)S(1)} collective-permute-done((bf16[448,4608]{1,0:T(8,128)(2,1)S(1)}, bf16[448,4608]{1,0:T(8,128)(2,1)S(1)}, u32[]{:S(2)}, u32[]{:S(2)}) %collective-permute-start.23) | collective-permute-done | bytes 4128800 | tf_op jit(solution)/shard_map/ppermute | solution.py:24
  115.7 7.5 %outer.1 = bf16[512,4096]{1,0:T(8,128)(2,1)} custom-call(bf16[448,1024]{1,0:T(8,128)(2,1)S(1)} %get-tuple-element.138.g_ref, bf16[448,4608]{1,0:T(8,128)(2,1)S(1)} %collective-permute-done.23.h_ref.m_ref, bf16[448,4608]{1,0:T(8,128)(2,1)S(1)} %get-tuple-element.139.n_ref, bf16[448,4608]{1,0:T(8,128)(2,1)S(1)} %collective-permute-done.23.h_ref.m_ref), custom_call_target="tpu_custom_call" | custom-call | flops 3758096384 | bytes 16777216 | tf_op jit(solution)/shard_map/outer/pallas_call | solution.py:597
  123.2 0.6 collective-permute-done.22.b2
  123.8 0.9 turn_rows.1
  124.7 1.6 collective-permute-start.27
  126.3 1.2 collective-permute-start.25
  127.5 0.3 collective-permute-start.26
  127.8 2.6 %collective-permute-start.28 = (bf16[448,128]{1,0:T(8,128)(2,1)S(1)}, bf16[448,128]{1,0:T(8,128)(2,1)S(1)}, u32[]{:S(2)}, u32[]{:S(2)}) collective-permute-start(bf16[448,128]{1,0:T(8,128)(2,1)S(1)} %get-tuple-element.153), channel_id=1, source_target_pairs={{0,2},{1,3},{2,0},{3,1},{128,130},{129,131},{130,128},{131,129},{4... | collective-permute-start | bytes 344072 | tf_op jit(solution)/shard_map/ppermute | solution.py:30
  130.3 1.0 collective-permute-start.29
  131.3 1.6 %collective-permute-done.28.refs_6_ = bf16[448,128]{1,0:T(8,128)(2,1)S(1)} collective-permute-done((bf16[448,128]{1,0:T(8,128)(2,1)S(1)}, bf16[448,128]{1,0:T(8,128)(2,1)S(1)}, u32[]{:S(2)}, u32[]{:S(2)}) %collective-permute-start.28) | collective-permute-done | bytes 114720 | tf_op jit(solution)/shard_map/ppermute | solution.py:30
  132.9 1.7 %collective-permute-done.29.refs_7_ = bf16[448,128]{1,0:T(8,128)(2,1)S(1)} collective-permute-done((bf16[448,128]{1,0:T(8,128)(2,1)S(1)}, bf16[448,128]{1,0:T(8,128)(2,1)S(1)}, u32[]{:S(2)}, u32[]{:S(2)}) %collective-permute-start.29) | collective-permute-done | bytes 114720 | tf_op jit(solution)/shard_map/ppermute | solution.py:30
  134.7 0.2 gather_rows.1
  134.9 12.5 %all_to_all.16.total_ref = bf16[8,128,128]{2,1,0:T(8,128)(2,1)} all-to-all(bf16[8,128,128]{2,1,0:T(8,128)(2,1)S(1)} %gather_rows.1), channel_id=1, replica_groups=mesh['c'=2,'z'=8,'y'=4,'x'=4] {'z'}, dimensions={0} | all-to-all | bytes 524288 | tf_op jit(solution)/shard_map/all_to_all | solution.py:735
  147.4 1.6 last_sums.1.sums_ref
  148.9 5.5 %collective-permute-start.30 = (f32[2,128]{1,0:T(2,128)}, f32[2,128]{1,0:T(2,128)S(1)}, u32[]{:S(2)}, u32[]{:S(2)}) collective-permute-start(f32[2,128]{1,0:T(2,128)} %last_sums.1.sums_ref), channel_id=1, source_target_pairs={{0,128},{128,0},{1,129},{129,1},{2,130},{130,2},{3,131},{131,3},{4... | collective-permute-start | bytes 3080 | tf_op jit(solution)/shard_map/ppermute | solution.py:24
  154.4 1.8 %finish.1 = bf16[128,128]{1,0:T(8,128)(2,1)} custom-call(bf16[8,128,128]{2,1,0:T(8,128)(2,1)} %all_to_all.16.total_ref, bf16[128,128]{1,0:T(8,128)(2,1)} %hidden_ref.3, f32[1,128]{1,0:T(1,128)} %bitcast.21, f32[112,1]{1,0:T(8,128)} %copy-done.2), custom_call_target="tpu_custom_call" | custom-call | tf_op jit(solution)/shard_map/finish/pallas_call | solution.py:666
  156.2 0.6 copy-done.5
  156.8 1.2 last.1
  (43 shorter events, 0.3 us)
Async XLA Ops:
  0.6 23.7 %collective-permute-start = (bf16[512,4096]{1,0:T(8,128)(2,1)}, bf16[512,4096]{1,0:T(8,128)(2,1)}, u32[]{:S(2)}, u32[]{:S(2)}) collective-permute-start(bf16[512,4096]{1,0:T(8,128)(2,1)} %w0_ref.5), channel_id=1, source_target_pairs={{0,128},{128,0},{1,129},{129,1},{2,130},{130,2},{3,131},{131,3},{4... | collective-permute-start | bytes 12582920 | tf_op jit(solution)/shard_map/ppermute | solution.py:24
  5.5 18.8 %all-to-all-start = ((bf16[8,128,128]{2,1,0:T(8,128)(2,1)}), bf16[8,128,128]{2,1,0:T(8,128)(2,1)S(1)}, u32[]{:S(2)}, u32[]{:S(2)}) async-start(bf16[8,128,128]{2,1,0:T(8,128)(2,1)} %get-tuple-element.83), calls=%async_computation | async-start | bytes 524288 | tf_op jit(solution)/shard_map/all_to_all | solution.py:689
  11.9 1.3 collective-permute-start.1
  24.4 8.9 %collective-permute-start.10 = (bf16[464,128]{1,0:T(8,128)(2,1)S(1)}, bf16[464,128]{1,0:T(8,128)(2,1)S(1)}, u32[]{:S(2)}, u32[]{:S(2)}) collective-permute-start(bf16[464,128]{1,0:T(8,128)(2,1)S(1)} %pad_maximum_fusion.2.refs_0_), channel_id=1, source_target_pairs={{0,3},{1,0},{2,1},{3,2},{128,129},{129,130},{130,131},{131,128},{4... | collective-permute-start | bytes 356360 | tf_op jit(solution)/shard_map/ppermute | solution.py:30
  25.6 8.7 %collective-permute-start.9 = (bf16[464,128]{1,0:T(8,128)(2,1)S(1)}, bf16[464,128]{1,0:T(8,128)(2,1)S(1)}, u32[]{:S(2)}, u32[]{:S(2)}) collective-permute-start(bf16[464,128]{1,0:T(8,128)(2,1)S(1)} %pad_maximum_fusion.2.refs_0_), channel_id=1, source_target_pairs={{0,2},{1,3},{2,0},{3,1},{128,130},{129,131},{130,128},{131,129},{4... | collective-permute-start | bytes 356360 | tf_op jit(solution)/shard_map/ppermute | solution.py:30
  28.1 6.3 %collective-permute-start.8 = (bf16[464,128]{1,0:T(8,128)(2,1)S(1)}, bf16[464,128]{1,0:T(8,128)(2,1)S(1)}, u32[]{:S(2)}, u32[]{:S(2)}) collective-permute-start(bf16[464,128]{1,0:T(8,128)(2,1)S(1)} %pad_maximum_fusion.2.refs_0_), channel_id=1, source_target_pairs={{0,1},{1,2},{2,3},{3,0},{128,131},{129,128},{130,129},{131,130},{4... | collective-permute-start | bytes 356360 | tf_op jit(solution)/shard_map/ppermute | solution.py:30
  29.3 6.8 %collective-permute-start.4 = (bf16[480,128]{1,0:T(8,128)(2,1)S(1)}, bf16[480,128]{1,0:T(8,128)(2,1)S(1)}, u32[]{:S(2)}, u32[]{:S(2)}) collective-permute-start(bf16[480,128]{1,0:T(8,128)(2,1)S(1)} %fusion.1.refs_4_), channel_id=1, source_target_pairs={{0,12},{4,0},{8,4},{12,8},{128,132},{132,136},{136,140},{140,128},... | collective-permute-start | bytes 368648 | tf_op jit(solution)/shard_map/ppermute | solution.py:30
  30.7 6.2 %collective-permute-start.3 = (bf16[480,128]{1,0:T(8,128)(2,1)S(1)}, bf16[480,128]{1,0:T(8,128)(2,1)S(1)}, u32[]{:S(2)}, u32[]{:S(2)}) collective-permute-start(bf16[480,128]{1,0:T(8,128)(2,1)S(1)} %fusion.1.refs_4_), channel_id=1, source_target_pairs={{0,8},{4,12},{8,0},{12,4},{128,136},{132,140},{136,128},{140,132},... | collective-permute-start | bytes 368648 | tf_op jit(solution)/shard_map/ppermute | solution.py:30
  33.3 5.1 %collective-permute-start.2 = (bf16[480,128]{1,0:T(8,128)(2,1)S(1)}, bf16[480,128]{1,0:T(8,128)(2,1)S(1)}, u32[]{:S(2)}, u32[]{:S(2)}) collective-permute-start(bf16[480,128]{1,0:T(8,128)(2,1)S(1)} %fusion.1.refs_4_), channel_id=1, source_target_pairs={{0,4},{4,8},{8,12},{12,0},{128,140},{132,128},{136,132},{140,136},... | collective-permute-start | bytes 368648 | tf_op jit(solution)/shard_map/ppermute | solution.py:30
  34.5 8.7 %collective-permute-start.11 = (bf16[1792,128]{1,0:T(8,128)(2,1)S(1)}, bf16[1792,128]{1,0:T(8,128)(2,1)S(1)}, u32[]{:S(2)}, u32[]{:S(2)}) collective-permute-start(bf16[1792,128]{1,0:T(8,128)(2,1)S(1)} %pad_maximum_fusion.1.refs_4_), channel_id=1, source_target_pairs={{0,4},{4,8},{8,12},{12,0},{128,140},{132,128},{136,132},{140,136},... | collective-permute-start | bytes 1376264 | tf_op jit(solution)/shard_map/ppermute | solution.py:30
  38.4 8.2 %collective-permute-start.5 = (bf16[1792,128]{1,0:T(8,128)(2,1)S(1)}, bf16[1792,128]{1,0:T(8,128)(2,1)S(1)}, u32[]{:S(2)}, u32[]{:S(2)}) collective-permute-start(bf16[1792,128]{1,0:T(8,128)(2,1)S(1)} %pad_maximum_fusion.refs_0_), channel_id=1, source_target_pairs={{0,1},{1,2},{2,3},{3,0},{128,131},{129,128},{130,129},{131,130},{4... | collective-permute-start | bytes 1376264 | tf_op jit(solution)/shard_map/ppermute | solution.py:30
  39.7 11.2 %collective-permute-start.12 = (bf16[1792,128]{1,0:T(8,128)(2,1)S(1)}, bf16[1792,128]{1,0:T(8,128)(2,1)S(1)}, u32[]{:S(2)}, u32[]{:S(2)}) collective-permute-start(bf16[1792,128]{1,0:T(8,128)(2,1)S(1)} %pad_maximum_fusion.1.refs_4_), channel_id=1, source_target_pairs={{0,12},{4,0},{8,4},{12,8},{128,132},{132,136},{136,140},{140,128},... | collective-permute-start | bytes 1376264 | tf_op jit(solution)/shard_map/ppermute | solution.py:30
  39.7 12.7 %collective-permute-start.6 = (bf16[1792,128]{1,0:T(8,128)(2,1)S(1)}, bf16[1792,128]{1,0:T(8,128)(2,1)}, u32[]{:S(2)}, u32[]{:S(2)}) collective-permute-start(bf16[1792,128]{1,0:T(8,128)(2,1)S(1)} %pad_maximum_fusion.refs_0_), channel_id=1, source_target_pairs={{0,3},{1,0},{2,1},{3,2},{128,129},{129,130},{130,131},{131,128},{4... | collective-permute-start | bytes 1376264 | tf_op jit(solution)/shard_map/ppermute | solution.py:30
  43.2 12.0 %collective-permute-start.13 = (bf16[1792,128]{1,0:T(8,128)(2,1)S(1)}, bf16[1792,128]{1,0:T(8,128)(2,1)}, u32[]{:S(2)}, u32[]{:S(2)}) collective-permute-start(bf16[1792,128]{1,0:T(8,128)(2,1)S(1)} %collective-permute-done.11.refs_5_), channel_id=1, source_target_pairs={{0,4},{4,8},{8,12},{12,0},{128,140},{132,128},{136,132},{140,136},... | collective-permute-start | bytes 1376264 | tf_op jit(solution)/shard_map/ppermute | solution.py:30
  46.6 9.8 %collective-permute-start.7 = (bf16[1792,128]{1,0:T(8,128)(2,1)S(1)}, bf16[1792,128]{1,0:T(8,128)(2,1)}, u32[]{:S(2)}, u32[]{:S(2)}) collective-permute-start(bf16[1792,128]{1,0:T(8,128)(2,1)S(1)} %collective-permute-done.5.refs_1_), channel_id=1, source_target_pairs={{0,1},{1,2},{2,3},{3,0},{128,131},{129,128},{130,129},{131,130},{4... | collective-permute-start | bytes 1376264 | tf_op jit(solution)/shard_map/ppermute | solution.py:30
  48.6 2.2 %copy-start = (bf16[512,4096]{1,0:T(8,128)(2,1)S(1)}, bf16[512,4096]{1,0:T(8,128)(2,1)}, u32[]{:S(2)}) copy-start(bf16[512,4096]{1,0:T(8,128)(2,1)} %w0_ref.5) | copy-start | bytes 12582916
  50.8 5.6 %copy-start.1 = (bf16[512,4096]{1,0:T(8,128)(2,1)S(1)}, bf16[512,4096]{1,0:T(8,128)(2,1)}, u32[]{:S(2)}) copy-start(bf16[512,4096]{1,0:T(8,128)(2,1)} %w0_ref.5) | copy-start | bytes 12582916
  50.9 5.5 %copy-start.4 = (f32[1,128]{1,0:T(1,128)}, f32[1,128]{1,0:T(1,128)S(1)}, u32[]{:S(2)}) copy-start(f32[1,128]{1,0:T(1,128)S(1)} %get-tuple-element.158.total_ref) | copy-start | bytes 1540
  64.7 24.4 %copy-start.2 = (f32[112,1]{1,0:T(8,128)}, f32[112,1]{1,0:T(8,128)S(1)}, u32[]{:S(2)}) copy-start(f32[112,1]{1,0:T(8,128)S(1)} %get-tuple-element.155.inv_ref) | copy-start | bytes 1348
  89.1 9.2 %copy-start.3 = (f32[1,128]{1,0:T(1,128)}, f32[1,128]{1,0:T(1,128)S(1)}, u32[]{:S(2)}) copy-start(f32[1,128]{1,0:T(1,128)S(1)} %get-tuple-element.107.loss_ref) | copy-start | bytes 1540
  89.1 9.2 %collective-permute-start.14 = (bf16[912,128]{1,0:T(8,128)(2,1)S(1)}, bf16[912,128]{1,0:T(8,128)(2,1)S(1)}, u32[]{:S(2)}, u32[]{:S(2)}) collective-permute-start(bf16[912,128]{1,0:T(8,128)(2,1)S(1)} %get-tuple-element.118), channel_id=1, source_target_pairs={{0,1},{1,2},{2,3},{3,0},{128,131},{129,128},{130,129},{131,130},{4... | collective-permute-start | bytes 700424 | tf_op jit(solution)/shard_map/ppermute | solution.py:30
  89.8 8.4 %collective-permute-start.15 = (bf16[896,128]{1,0:T(8,128)(2,1)S(1)}, bf16[896,128]{1,0:T(8,128)(2,1)S(1)}, u32[]{:S(2)}, u32[]{:S(2)}) collective-permute-start(bf16[896,128]{1,0:T(8,128)(2,1)S(1)} %get-tuple-element.119), channel_id=1, source_target_pairs={{0,3},{1,0},{2,1},{3,2},{128,129},{129,130},{130,131},{131,128},{4... | collective-permute-start | bytes 688136 | tf_op jit(solution)/shard_map/ppermute | solution.py:30
  90.7 7.6 %collective-permute-start.16 = (bf16[896,128]{1,0:T(8,128)(2,1)S(1)}, bf16[896,128]{1,0:T(8,128)(2,1)S(1)}, u32[]{:S(2)}, u32[]{:S(2)}) collective-permute-start(bf16[896,128]{1,0:T(8,128)(2,1)S(1)} %get-tuple-element.120), channel_id=1, source_target_pairs={{0,4},{4,8},{8,12},{12,0},{128,140},{132,128},{136,132},{140,136},... | collective-permute-start | bytes 688136 | tf_op jit(solution)/shard_map/ppermute | solution.py:30
  90.9 7.4 %collective-permute-start.17 = (bf16[896,128]{1,0:T(8,128)(2,1)S(1)}, bf16[896,128]{1,0:T(8,128)(2,1)S(1)}, u32[]{:S(2)}, u32[]{:S(2)}) collective-permute-start(bf16[896,128]{1,0:T(8,128)(2,1)S(1)} %get-tuple-element.121), channel_id=1, source_target_pairs={{0,12},{4,0},{8,4},{12,8},{128,132},{132,136},{136,140},{140,128},... | collective-permute-start | bytes 688136 | tf_op jit(solution)/shard_map/ppermute | solution.py:30
  98.3 17.4 %collective-permute-start.23 = (bf16[448,4608]{1,0:T(8,128)(2,1)S(1)}, bf16[448,4608]{1,0:T(8,128)(2,1)S(1)}, u32[]{:S(2)}, u32[]{:S(2)}) collective-permute-start(bf16[448,4608]{1,0:T(8,128)(2,1)S(1)} %get-tuple-element.139.n_ref), channel_id=1, source_target_pairs={{0,128},{128,0},{1,129},{129,1},{2,130},{130,2},{3,131},{131,3},{4... | collective-permute-start | bytes 12386312 | tf_op jit(solution)/shard_map/ppermute | solution.py:24
  109.2 14.6 %collective-permute-start.19 = (bf16[1872,128]{1,0:T(8,128)(2,1)S(1)}, bf16[1872,128]{1,0:T(8,128)(2,1)S(1)}, u32[]{:S(2)}, u32[]{:S(2)}) collective-permute-start(bf16[1872,128]{1,0:T(8,128)(2,1)S(1)} %get-tuple-element.130), channel_id=1, source_target_pairs={{0,1},{1,2},{2,3},{3,0},{128,131},{129,128},{130,129},{131,130},{4... | collective-permute-start | bytes 1437704 | tf_op jit(solution)/shard_map/ppermute | solution.py:30
  109.3 14.5 %collective-permute-start.20 = (bf16[1872,128]{1,0:T(8,128)(2,1)S(1)}, bf16[1872,128]{1,0:T(8,128)(2,1)S(1)}, u32[]{:S(2)}, u32[]{:S(2)}) collective-permute-start(bf16[1872,128]{1,0:T(8,128)(2,1)S(1)} %get-tuple-element.131), channel_id=1, source_target_pairs={{0,3},{1,0},{2,1},{3,2},{128,129},{129,130},{130,131},{131,128},{4... | collective-permute-start | bytes 1437704 | tf_op jit(solution)/shard_map/ppermute | solution.py:30
  110.9 12.3 %collective-permute-start.21 = (bf16[1792,128]{1,0:T(8,128)(2,1)S(1)}, bf16[1792,128]{1,0:T(8,128)(2,1)S(1)}, u32[]{:S(2)}, u32[]{:S(2)}) collective-permute-start(bf16[1792,128]{1,0:T(8,128)(2,1)S(1)} %get-tuple-element.136), channel_id=1, source_target_pairs={{0,4},{4,8},{8,12},{12,0},{128,140},{132,128},{136,132},{140,136},... | collective-permute-start | bytes 1376264 | tf_op jit(solution)/shard_map/ppermute | solution.py:30
  111.6 12.1 %collective-permute-start.22 = (bf16[1792,128]{1,0:T(8,128)(2,1)S(1)}, bf16[1792,128]{1,0:T(8,128)(2,1)S(1)}, u32[]{:S(2)}, u32[]{:S(2)}) collective-permute-start(bf16[1792,128]{1,0:T(8,128)(2,1)S(1)} %get-tuple-element.137), channel_id=1, source_target_pairs={{0,12},{4,0},{8,4},{12,8},{128,132},{132,136},{136,140},{140,128},... | collective-permute-start | bytes 1376264 | tf_op jit(solution)/shard_map/ppermute | solution.py:30
  115.7 8.1 %collective-permute-start.18 = (f32[32,128]{1,0:T(8,128)S(1)}, f32[32,128]{1,0:T(8,128)S(1)}, u32[]{:S(2)}, u32[]{:S(2)}) collective-permute-start(f32[32,128]{1,0:T(8,128)S(1)} %get-tuple-element.128.mine), channel_id=1, source_target_pairs={{0,2},{1,3},{2,0},{3,1},{128,130},{129,131},{130,128},{131,129},{4... | collective-permute-start | bytes 49160 | tf_op jit(solution)/shard_map/ppermute | solution.py:30
  124.7 5.6 %collective-permute-start.27 = (bf16[448,128]{1,0:T(8,128)(2,1)S(1)}, bf16[448,128]{1,0:T(8,128)(2,1)S(1)}, u32[]{:S(2)}, u32[]{:S(2)}) collective-permute-start(bf16[448,128]{1,0:T(8,128)(2,1)S(1)} %get-tuple-element.152), channel_id=1, source_target_pairs={{0,3},{1,0},{2,1},{3,2},{128,129},{129,130},{130,131},{131,128},{4... | collective-permute-start | bytes 344072 | tf_op jit(solution)/shard_map/ppermute | solution.py:30
  126.3 8.4 %collective-permute-start.24 = (bf16[480,128]{1,0:T(8,128)(2,1)S(1)}, bf16[480,128]{1,0:T(8,128)(2,1)S(1)}, u32[]{:S(2)}, u32[]{:S(2)}) collective-permute-start(bf16[480,128]{1,0:T(8,128)(2,1)S(1)} %get-tuple-element.148), channel_id=1, source_target_pairs={{0,4},{4,8},{8,12},{12,0},{128,140},{132,128},{136,132},{140,136},... | collective-permute-start | bytes 368648 | tf_op jit(solution)/shard_map/ppermute | solution.py:30
  126.3 8.4 %collective-permute-start.25 = (bf16[480,128]{1,0:T(8,128)(2,1)S(1)}, bf16[480,128]{1,0:T(8,128)(2,1)S(1)}, u32[]{:S(2)}, u32[]{:S(2)}) collective-permute-start(bf16[480,128]{1,0:T(8,128)(2,1)S(1)} %get-tuple-element.149), channel_id=1, source_target_pairs={{0,8},{4,12},{8,0},{12,4},{128,136},{132,140},{136,128},{140,132},... | collective-permute-start | bytes 368648 | tf_op jit(solution)/shard_map/ppermute | solution.py:30
  127.5 7.2 %collective-permute-start.26 = (bf16[480,128]{1,0:T(8,128)(2,1)S(1)}, bf16[480,128]{1,0:T(8,128)(2,1)S(1)}, u32[]{:S(2)}, u32[]{:S(2)}) collective-permute-start(bf16[480,128]{1,0:T(8,128)(2,1)S(1)} %get-tuple-element.150), channel_id=1, source_target_pairs={{0,12},{4,0},{8,4},{12,8},{128,132},{132,136},{136,140},{140,128},... | collective-permute-start | bytes 368648 | tf_op jit(solution)/shard_map/ppermute | solution.py:30
  127.8 5.1 %collective-permute-start.28 = (bf16[448,128]{1,0:T(8,128)(2,1)S(1)}, bf16[448,128]{1,0:T(8,128)(2,1)S(1)}, u32[]{:S(2)}, u32[]{:S(2)}) collective-permute-start(bf16[448,128]{1,0:T(8,128)(2,1)S(1)} %get-tuple-element.153), channel_id=1, source_target_pairs={{0,2},{1,3},{2,0},{3,1},{128,130},{129,131},{130,128},{131,129},{4... | collective-permute-start | bytes 344072 | tf_op jit(solution)/shard_map/ppermute | solution.py:30
  130.3 4.3 %collective-permute-start.29 = (bf16[448,128]{1,0:T(8,128)(2,1)S(1)}, bf16[448,128]{1,0:T(8,128)(2,1)S(1)}, u32[]{:S(2)}, u32[]{:S(2)}) collective-permute-start(bf16[448,128]{1,0:T(8,128)(2,1)S(1)} %get-tuple-element.154), channel_id=1, source_target_pairs={{0,1},{1,2},{2,3},{3,0},{128,131},{129,128},{130,129},{131,130},{4... | collective-permute-start | bytes 344072 | tf_op jit(solution)/shard_map/ppermute | solution.py:30
  148.9 7.3 %collective-permute-start.30 = (f32[2,128]{1,0:T(2,128)}, f32[2,128]{1,0:T(2,128)S(1)}, u32[]{:S(2)}, u32[]{:S(2)}) collective-permute-start(f32[2,128]{1,0:T(2,128)} %last_sums.1.sums_ref), channel_id=1, source_target_pairs={{0,128},{128,0},{1,129},{129,1},{2,130},{130,2},{3,131},{131,3},{4... | collective-permute-start | bytes 3080 | tf_op jit(solution)/shard_map/ppermute | solution.py:24
  156.2 0.6 copy-start.5

commit v4 on v3

--- a/solution.py
+++ b/solution.py
@@ -193,8 +193,7 @@
 
 
 def soft_kernel(Zh, place_ref, w0_ref, w1_ref, every_ref, l_ref, n_ref, label_ref, live_ref, factor_ref, *refs):
-    g_ref, ng_ref, side_ref, loss_ref, gain_ref, a_low, a_high, b_low, b_high = refs[:9]
-    wa_ref, wb_ref, sems = refs[9:]
+    g_ref, ng_ref, side_ref, loss_ref, gain_ref, a_far, b_far, wa_ref, wb_ref, sems = refs
     V = w0_ref.shape[0]
     far = lax.rem(place_ref[0] + 2, R)
     copies = []
@@ -251,35 +250,31 @@
     for pair in copies:
         for copy in pair:
             copy.wait()
-    half = Zh // 2
     gain_ref[...] = jnp.zeros_like(gain_ref)
     part = jnp.dot(g_ref[(R - 1) * LIVE :, :], wa_ref[...], preferred_element_type=f32)
     gain = part * n_ref[(R - 1) * LIVE :, 0 : Zh * R * 128].astype(f32)
     gain = jnp.sum(gain, axis=0, keepdims=True)
     for t in range(Zh * R):
-        at = t % (half * R) * LIVE
         gain_ref[t : t + 1, :] = gain[:, t * 128 : (t + 1) * 128]
-        (a_low if t < half * R else a_high)[at : at + LIVE, :] = part[
-            :, t * 128 : (t + 1) * 128
-        ].astype(bf16)
+        a_far[t * LIVE : (t + 1) * LIVE, :] = part[:, t * 128 : (t + 1) * 128].astype(bf16)
     part = jnp.dot(g_ref[...], wb_ref[...], preferred_element_type=f32)
     for z in range(Zh):
-        at = z % half * R * LIVE
+        at = z * R * LIVE
         t = (Zh + z) * R + far
         block = part[:, z * 128 : (z + 1) * 128]
-        (b_low if z < half else b_high)[at : at + R * LIVE, :] = block.astype(bf16)
+        b_far[at : at + R * LIVE, :] = block.astype(bf16)
         gain = block * n_ref[:, pl.ds(pl.multiple_of(t * 128, 128), 128)].astype(f32)
         gain_ref[pl.ds(t, 1), :] = jnp.sum(gain, axis=0, keepdims=True)
-    a_low[Zh // 2 * R * LIVE :, :] = side_ref[R - 1]
+    a_far[Zh * R * LIVE :, :] = side_ref[R - 1]
 
 
 def soft_rows(place, Zh, w0, w1, every, logits, normed, labels, live, factor):
     V = w0.shape[0]
     rows = logits.shape[0]
-    half = Zh // 2 * R * LIVE
+    block = Zh * R * LIVE
     shapes = [((rows, 2 * V), bf16), (normed.shape, bf16), ((R, 16, 128), bf16), ((1, 128), f32)]
     shapes += [((2 * Zh * R, 128), f32)]
-    shapes += [((half + 16, 128), bf16)] + [((half, 128), bf16)] * 3
+    shapes += [((block + 16, 128), bf16), ((block, 128), bf16)]
     return pl.pallas_call(
         functools.partial(soft_kernel, Zh),
         out_shape=tuple(jax.ShapeDtypeStruct(*shape) for shape in shapes),
@@ -368,39 +363,35 @@
     return high, (value - high.astype(f32)).astype(bf16)
 
 
-def relay_kernel(up, down, low, high, *refs):
-    half, block = high.shape[0], 2 * high.shape[0]
-    up_out, down_out = refs[-2:] if len(refs) == 2 else refs[2:4]
-    add = lambda a, b: (a.astype(f32) + b.astype(f32)).astype(bf16)
-    up_out[0:half, :] = add(up[0:half, :], low[0:half, :])
-    up_out[half:block, :] = up[half:block, :]
-    down_out[0:half, :] = down[0:half, :]
-    down_out[half:block, :] = add(down[half:block, :], high[...])
-    if len(refs) > 2:
-        mine, came = read_tile(up[block:, :], 2), read_tile(low[half:, :], 2)
-        up_out[block : block + 16, :] = split_tile([a + b for a, b in zip(mine, came)])
-        down_out[block : block + 16, :] = down[block:, :]
-        gain = refs[0][...] + refs[1][...]
-        refs[4][...] = gain
-        lines = gain.shape[0]
-        for i, piece in enumerate(two(gain)):
-            for out in (up_out, down_out):
-                at = block + 16 + i * lines
-                out[at : at + lines, :] = piece
-
-
-def relay(up, down, low, high, *gains):
-    lines = gains[0].shape[0] if gains else 0
-    shape = jax.ShapeDtypeStruct((up.shape[0] + 2 * lines, 128), bf16)
-    shapes = (shape, shape) + ((jax.ShapeDtypeStruct((lines, 128), f32),) if gains else ())
+def relay_kernel(a_up, a_down, a_far, gain_0, gain_1, b_up, b_far, a_out, down_out, b_out, gain_out):
+    block = b_up.shape[0]
+    add = lambda a, b: (a[0:block, :].astype(f32) + b[0:block, :].astype(f32)).astype(bf16)
+    a_out[0:block, :] = add(a_up, a_far)
+    b_out[...] = add(b_up, b_far)
+    mine, came = (read_tile(ref[block:, :], 2) for ref in (a_up, a_far))
+    a_out[block : block + 16, :] = split_tile([a + b for a, b in zip(mine, came)])
+    down_out[0 : block + 16, :] = a_down[...]
+    gain = gain_0[...] + gain_1[...]
+    gain_out[...] = gain
+    lines = gain.shape[0]
+    for i, piece in enumerate(two(gain)):
+        at = block + 16 + i * lines
+        a_out[at : at + lines, :] = piece
+        down_out[at : at + lines, :] = piece
+
+
+def relay(a_up, a_down, a_far, gain_0, gain_1, b_up, b_far):
+    lines = gain_0.shape[0]
+    long = (a_up.shape[0] + 2 * lines, 128)
+    shapes = [(long, bf16), (long, bf16), (b_up.shape, bf16), (gain_0.shape, f32)]
     return pl.pallas_call(
         relay_kernel,
-        out_shape=shapes,
-        in_specs=[VMEM] * (4 + len(gains)),
-        out_specs=(VMEM,) * len(shapes),
+        out_shape=tuple(jax.ShapeDtypeStruct(*shape) for shape in shapes),
+        in_specs=[VMEM] * 7,
+        out_specs=(VMEM,) * 4,
         compiler_params=pltpu.CompilerParams(vmem_limit_bytes=SCOPED),
         name="relay",
-    )(up, down, low, high, *gains)
+    )(a_up, a_down, a_far, gain_0, gain_1, b_up, b_far)
 
 
 def turn_kernel(Zh, y_ref, side_ref, mine, far, a0, a1, a2, b0, b1, b2, *outs):
@@ -709,22 +700,18 @@
     weights = (head_weight, weight_other)
     normed, inv_rms, logits, share = forward(place, Zh, *weights, gain, a_all, b_all)
     every = lax.all_to_all(share, ("z", "y", "x"), 0, 0)
-    g, normed, side, loss, gain_far, a_low, a_high, b_low, b_high = soft_rows(
+    g, normed, side, loss, gain_far, a_far, b_far = soft_rows(
         place, Zh, *weights, every, logits, normed, labels, live, factor
     )
 
-    a_low, a_high = around(a_low, "x", 1), around(a_high, "x", -1)
-    b_low, b_high = around(b_low, "y", 1), around(b_high, "y", -1)
+    a_far, b_far = around(a_far, "x", 1), around(b_far, "y", 1)
     near = near_rows(place, Zh, *weights, side, g, normed)
-    near, a_low, a_high, b_low, b_high, g, normed = lax.optimization_barrier(
-        (near, a_low, a_high, b_low, b_high, g, normed)
-    )
+    near, a_far, b_far, g, normed = lax.optimization_barrier((near, a_far, b_far, g, normed))
     theirs = shift(normed, "c", 1)
     a0, a1, a3, b0, b1, b3, gain_near = near
-    a_up, a_down, gain = relay(a3, a1, a_low, a_high, gain_far, gain_near)
-    b_up, b_down = relay(b1, b3, b_low, b_high)
+    a_up, a_down, b_up, gain = relay(a3, a1, a_far, gain_far, gain_near, b1, b_far)
     a_in = around(a_up, "x", 1), around(a_down, "x", -1)
-    b_in = around(b_up, "y", 1), around(b_down, "y", -1)
+    b_in = around(b_up, "y", 1), around(b3, "y", -1)
     gain_in = around(gain, "x", 2)
     weight_grad = outer(g, normed, theirs, D)
     a_in, b_in, weight_grad = lax.optimization_barrier((a_in, b_in, weight_grad))

time: 159 us -> 157 us (0.987)
    ppermute x27 -> x25, starting transfers between devices: 32.2 us -> 33.1 us  [around(): return lax.ppermute(x, ('c', axis), pairs)]
    ppermute x27 -> x25, waiting for transfers between devices: 13.9 us -> 14.6 us  [around(): return lax.ppermute(x, ('c', axis), pairs)]
  transfers between devices with their start and end apart: 32 -> 30, of which waited for: 12 -> 12; matrix products, arithmetic and copies ran while one was open for 1% -> 1% of each run, Pallas kernels for 11% -> 11%
where the time goes in v4:
time: 157 us
  starting transfers between devices  57.9 us (37%)
  Pallas kernels  33.6 us (21%)
  blocking collectives  32.5 us (21%)
  waiting for transfers between devices  28.2 us (18%)
  local copies, waits for them, and re-layouts  2.96 us (2%)
    ppermute x25, starting transfers between devices, around(): return lax.ppermute(x, ('c', axis), pairs)  33.1 us
    all_to_all x1, blocking collectives, body(): every = lax.all_to_all(share, ('z', 'y', 'x'), 0, 0)  20.1 us
    ppermute x4, starting transfers between devices, shift(): return lax.ppermute(x, axis, [(i, (i + k) % n) for i in range(n)])  18.4 us
    ppermute x25, waiting for transfers between devices, around(): return lax.ppermute(x, ('c', axis), pairs)  14.6 us
    all_to_all x1, blocking collectives, body(): total = lax.all_to_all(total, 'z', 0, 0)  12.4 us
    all_to_all x1, waiting for transfers between devices, body(): block = lax.all_to_all(block, 'z', 0, 0)  10.4 us
    pallas_call x1, Pallas kernels, forward(): pl.pallas_call(functools.partial(forward_kernel, Zh), out_shape=(jax.Shap...  8.32 us
    pallas_call x1, Pallas kernels, outer(): pl.pallas_call(outer_kernel, grid=(D // V,), out_shape=jax.ShapeDtypeStru...  7.48 us
  transfers between devices with their start and end apart: 30, of which 12 were waited for; matrix products, arithmetic and copies ran while one was open for 1% of the time, Pallas kernels for 11%

profile of v4, /device:TPU:1, one launch (start us, length us, event | category | flops | bytes accessed | tf_op | source)
XLA Modules:
  0.0 156.9 jit_solution(8772412494439439596)
XLA Ops:
  0.6 3.3 %collective-permute-start = (bf16[512,4096]{1,0:T(8,128)(2,1)}, bf16[512,4096]{1,0:T(8,128)(2,1)}, u32[]{:S(2)}, u32[]{:S(2)}) collective-permute-start(bf16[512,4096]{1,0:T(8,128)(2,1)} %w0_ref.5), channel_id=1, source_target_pairs={{0,128},{128,0},{1,129},{129,1},{2,130},{130,2},{3,131},{131,3},{4... | collective-permute-start | bytes 12582920 | tf_op jit(solution)/shard_map/ppermute | solution.py:24
  4.0 1.5 prepare.1
  5.5 6.5 %all-to-all-start = ((bf16[8,128,128]{2,1,0:T(8,128)(2,1)}), bf16[8,128,128]{2,1,0:T(8,128)(2,1)S(1)}, u32[]{:S(2)}, u32[]{:S(2)}) async-start(bf16[8,128,128]{2,1,0:T(8,128)(2,1)} %get-tuple-element.78), calls=%async_computation | async-start | bytes 524288 | tf_op jit(solution)/shard_map/all_to_all | solution.py:680
  11.9 0.3 collective-permute-start.1
  12.2 1.0 collective-permute-done.1
  13.2 0.7 pad_add_fusion
  13.9 10.4 %all-to-all-done = bf16[8,128,128]{2,1,0:T(8,128)(2,1)S(1)} async-done(((bf16[8,128,128]{2,1,0:T(8,128)(2,1)}), bf16[8,128,128]{2,1,0:T(8,128)(2,1)S(1)}, u32[]{:S(2)}, u32[]{:S(2)}) %all-to-all-start) | async-done | bytes 262176 | tf_op jit(solution)/shard_map/all_to_all | solution.py:680
  24.3 0.0 collective-permute-done.w1_ref
  24.4 1.3 collective-permute-start.10
  25.6 2.5 %collective-permute-start.9 = (bf16[464,128]{1,0:T(8,128)(2,1)S(1)}, bf16[464,128]{1,0:T(8,128)(2,1)S(1)}, u32[]{:S(2)}, u32[]{:S(2)}) collective-permute-start(bf16[464,128]{1,0:T(8,128)(2,1)S(1)} %pad_maximum_fusion.2.refs_0_), channel_id=1, source_target_pairs={{0,2},{1,3},{2,0},{3,1},{128,130},{129,131},{130,128},{131,129},{4... | collective-permute-start | bytes 356360 | tf_op jit(solution)/shard_map/ppermute | solution.py:30
  28.1 1.1 collective-permute-start.8
  29.3 1.4 collective-permute-start.4
  30.7 2.6 %collective-permute-start.3 = (bf16[480,128]{1,0:T(8,128)(2,1)S(1)}, bf16[480,128]{1,0:T(8,128)(2,1)S(1)}, u32[]{:S(2)}, u32[]{:S(2)}) collective-permute-start(bf16[480,128]{1,0:T(8,128)(2,1)S(1)} %fusion.1.refs_4_), channel_id=1, source_target_pairs={{0,8},{4,12},{8,0},{12,4},{128,136},{132,140},{136,128},{140,132},... | collective-permute-start | bytes 368648 | tf_op jit(solution)/shard_map/ppermute | solution.py:30
  33.3 1.1 collective-permute-start.2
  34.4 0.0 collective-permute-done.9.refs_2_
  34.4 0.0 collective-permute-done.8.refs_1_
  34.5 1.6 %collective-permute-start.11 = (bf16[1792,128]{1,0:T(8,128)(2,1)S(1)}, bf16[1792,128]{1,0:T(8,128)(2,1)S(1)}, u32[]{:S(2)}, u32[]{:S(2)}) collective-permute-start(bf16[1792,128]{1,0:T(8,128)(2,1)S(1)} %pad_maximum_fusion.1.refs_4_), channel_id=1, source_target_pairs={{0,4},{4,8},{8,12},{12,0},{128,140},{132,128},{136,132},{140,136},... | collective-permute-start | bytes 1376264 | tf_op jit(solution)/shard_map/ppermute | solution.py:30
  36.1 0.0 collective-permute-done.4.refs_7_
  36.1 0.8 collective-permute-done.3.refs_6_
  36.9 1.5 collective-permute-done.2.refs_5_
  38.4 1.3 collective-permute-start.5
  39.7 0.0 collective-permute-start.12
  39.7 1.4 collective-permute-start.6
  41.0 2.1 %collective-permute-done.11.refs_5_ = bf16[1792,128]{1,0:T(8,128)(2,1)S(1)} collective-permute-done((bf16[1792,128]{1,0:T(8,128)(2,1)S(1)}, bf16[1792,128]{1,0:T(8,128)(2,1)S(1)}, u32[]{:S(2)}, u32[]{:S(2)}) %collective-permute-start.11) | collective-permute-done | bytes 458784 | tf_op jit(solution)/shard_map/ppermute | solution.py:30
  43.2 3.4 %collective-permute-start.13 = (bf16[1792,128]{1,0:T(8,128)(2,1)S(1)}, bf16[1792,128]{1,0:T(8,128)(2,1)}, u32[]{:S(2)}, u32[]{:S(2)}) collective-permute-start(bf16[1792,128]{1,0:T(8,128)(2,1)S(1)} %collective-permute-done.11.refs_5_), channel_id=1, source_target_pairs={{0,4},{4,8},{8,12},{12,0},{128,140},{132,128},{136,132},{140,136},... | collective-permute-start | bytes 1376264 | tf_op jit(solution)/shard_map/ppermute | solution.py:30
  46.6 0.0 collective-permute-done.5.refs_1_
  46.6 1.9 %collective-permute-start.7 = (bf16[1792,128]{1,0:T(8,128)(2,1)S(1)}, bf16[1792,128]{1,0:T(8,128)(2,1)}, u32[]{:S(2)}, u32[]{:S(2)}) collective-permute-start(bf16[1792,128]{1,0:T(8,128)(2,1)S(1)} %collective-permute-done.5.refs_1_), channel_id=1, source_target_pairs={{0,1},{1,2},{2,3},{3,0},{128,131},{129,128},{130,129},{131,130},{4... | collective-permute-start | bytes 1376264 | tf_op jit(solution)/shard_map/ppermute | solution.py:30
  48.5 0.1 stack.23.place_ref.y_ref
  48.6 2.2 %copy-done = bf16[512,4096]{1,0:T(8,128)(2,1)S(1)} copy-done((bf16[512,4096]{1,0:T(8,128)(2,1)S(1)}, bf16[512,4096]{1,0:T(8,128)(2,1)}, u32[]{:S(2)}) %copy-start) | copy-done | bytes 4194328
  50.8 0.1 read_meta.1
  50.9 1.5 collective-permute-done.6.refs_2_
  52.4 2.8 %collective-permute-done.13.refs_7_ = bf16[1792,128]{1,0:T(8,128)(2,1)} collective-permute-done((bf16[1792,128]{1,0:T(8,128)(2,1)S(1)}, bf16[1792,128]{1,0:T(8,128)(2,1)}, u32[]{:S(2)}, u32[]{:S(2)}) %collective-permute-start.13) | collective-permute-done | bytes 458784 | tf_op jit(solution)/shard_map/ppermute | solution.py:30
  55.2 1.2 collective-permute-done.7.refs_3_
  56.4 8.3 %forward.1 = (bf16[448,4608]{1,0:T(8,128)(2,1)S(1)}, f32[112,1]{1,0:T(8,128)S(1)}, f32[448,1024]{1,0:T(8,128)S(1)}, f32[128,4,128]{2,1,0:T(4,128)S(1)}) custom-call(s32[5]{0:T(128)S(1)} %stack.23.place_ref.y_ref, bf16[512,4096]{1,0:T(8,128)(2,1)S(1)} %copy-done.1, bf16[512,4096]{1,0:T(8,128)(2,1)} %collective-permute-done.w1_ref, ...), custom_call_target="tpu_custom_call" | custom-call | flops 3758096384 | bytes 8388608 | tf_op jit(solution)/shard_map/forward/pallas_call | solution.py:156
  64.7 20.1 %all_to_all.15.every_ref = f32[128,4,128]{2,1,0:T(4,128)S(1)} all-to-all(f32[128,4,128]{2,1,0:T(4,128)S(1)} %get-tuple-element.96), channel_id=1, replica_groups=mesh['c'=2,'z'=8,'y'=4,'x'=4] {'z','y','x'}, dimensions={0} | all-to-all | bytes 524288 | tf_op jit(solution)/shard_map/all_to_all | solution.py:702
  84.9 4.2 %soft_rows.1 = (bf16[448,1024]{1,0:T(8,128)(2,1)S(1)}, bf16[448,4608]{1,0:T(8,128)(2,1)S(1)}, bf16[4,16,128]{2,1,0:T(8,128)(2,1)S(1)}, f32[1,128]{1,0:T(1,128)S(...) custom-call(s32[5]{0:T(128)S(1)} %stack.23.place_ref.y_ref, ...), custom_call_target="tpu_custom_call", output_to_operand_aliasing={{1}: (5, {})} | custom-call | tf_op jit(solution)/shard_map/soft_rows/pallas_call | solution.py:278
  89.1 0.0 copy-start.3
  89.1 0.7 collective-permute-start.14
  89.8 0.2 collective-permute-start.15
  90.0 6.1 %near_rows.1 = (bf16[1792,128]{1,0:T(8,128)(2,1)S(1)}, bf16[1808,128]{1,0:T(8,128)(2,1)S(1)}, bf16[1808,128]{1,0:T(8,128)(2,1)S(1)}, bf16[1792,128]{1,0:T(8,128)...) custom-call(s32[5]{0:T(128)S(1)} %stack.23.place_ref.y_ref, ...), custom_call_target="tpu_custom_call" | custom-call | tf_op jit(solution)/shard_map/near_rows/pallas_call | solution.py:343
  96.1 1.0 collective-permute-done.15.b_far
  97.2 0.0 collective-permute-done.14.a_far
  97.2 9.4 %collective-permute-start.21 = (bf16[448,4608]{1,0:T(8,128)(2,1)S(1)}, bf16[448,4608]{1,0:T(8,128)(2,1)S(1)}, u32[]{:S(2)}, u32[]{:S(2)}) collective-permute-start(bf16[448,4608]{1,0:T(8,128)(2,1)S(1)} %get-tuple-element.129.n_ref), channel_id=1, source_target_pairs={{0,128},{128,0},{1,129},{129,1},{2,130},{130,2},{3,131},{131,3},{4... | collective-permute-start | bytes 12386312 | tf_op jit(solution)/shard_map/ppermute | solution.py:24
  106.5 0.2 relay.1
  106.8 2.7 %collective-permute-start.17 = (bf16[1872,128]{1,0:T(8,128)(2,1)S(1)}, bf16[1872,128]{1,0:T(8,128)(2,1)S(1)}, u32[]{:S(2)}, u32[]{:S(2)}) collective-permute-start(bf16[1872,128]{1,0:T(8,128)(2,1)S(1)} %get-tuple-element.124), channel_id=1, source_target_pairs={{0,1},{1,2},{2,3},{3,0},{128,131},{129,128},{130,129},{131,130},{4... | collective-permute-start | bytes 1437704 | tf_op jit(solution)/shard_map/ppermute | solution.py:30
  109.5 1.5 collective-permute-start.20
  111.0 2.3 %collective-permute-done.21.h_ref.m_ref = bf16[448,4608]{1,0:T(8,128)(2,1)S(1)} collective-permute-done((bf16[448,4608]{1,0:T(8,128)(2,1)S(1)}, bf16[448,4608]{1,0:T(8,128)(2,1)S(1)}, u32[]{:S(2)}, u32[]{:S(2)}) %collective-permute-start.21) | collective-permute-done | bytes 4128800 | tf_op jit(solution)/shard_map/ppermute | solution.py:24
  113.2 1.5 collective-permute-start.16
  114.8 7.5 %outer.1 = bf16[512,4096]{1,0:T(8,128)(2,1)} custom-call(bf16[448,1024]{1,0:T(8,128)(2,1)S(1)} %get-tuple-element.128.g_ref, bf16[448,4608]{1,0:T(8,128)(2,1)S(1)} %collective-permute-done.21.h_ref.m_ref, bf16[448,4608]{1,0:T(8,128)(2,1)S(1)} %get-tuple-element.129.n_ref, bf16[448,4608]{1,0:T(8,128)(2,1)S(1)} %collective-permute-done.21.h_ref.m_ref), custom_call_target="tpu_custom_call" | custom-call | flops 3758096384 | bytes 16777216 | tf_op jit(solution)/shard_map/outer/pallas_call | solution.py:588
  122.3 1.0 turn_rows.1
  123.2 1.5 collective-permute-start.25
  124.8 1.0 collective-permute-start.23
  125.8 0.4 collective-permute-start.24
  126.2 3.0 %collective-permute-start.26 = (bf16[448,128]{1,0:T(8,128)(2,1)S(1)}, bf16[448,128]{1,0:T(8,128)(2,1)S(1)}, u32[]{:S(2)}, u32[]{:S(2)}) collective-permute-start(bf16[448,128]{1,0:T(8,128)(2,1)S(1)} %get-tuple-element.143), channel_id=1, source_target_pairs={{0,2},{1,3},{2,0},{3,1},{128,130},{129,131},{130,128},{131,129},{4... | collective-permute-start | bytes 344072 | tf_op jit(solution)/shard_map/ppermute | solution.py:30
  129.2 1.0 collective-permute-start.27
  130.2 1.2 collective-permute-done.26.refs_6_
  131.4 2.4 %collective-permute-done.27.refs_7_ = bf16[448,128]{1,0:T(8,128)(2,1)S(1)} collective-permute-done((bf16[448,128]{1,0:T(8,128)(2,1)S(1)}, bf16[448,128]{1,0:T(8,128)(2,1)S(1)}, u32[]{:S(2)}, u32[]{:S(2)}) %collective-permute-start.27) | collective-permute-done | bytes 114720 | tf_op jit(solution)/shard_map/ppermute | solution.py:30
  133.8 0.2 gather_rows.1
  134.0 12.4 %all_to_all.16.total_ref = bf16[8,128,128]{2,1,0:T(8,128)(2,1)} all-to-all(bf16[8,128,128]{2,1,0:T(8,128)(2,1)S(1)} %gather_rows.1), channel_id=1, replica_groups=mesh['c'=2,'z'=8,'y'=4,'x'=4] {'z'}, dimensions={0} | all-to-all | bytes 524288 | tf_op jit(solution)/shard_map/all_to_all | solution.py:722
  146.4 1.5 last_sums.1.sums_ref
  147.9 5.4 %collective-permute-start.28 = (f32[2,128]{1,0:T(2,128)}, f32[2,128]{1,0:T(2,128)S(1)}, u32[]{:S(2)}, u32[]{:S(2)}) collective-permute-start(f32[2,128]{1,0:T(2,128)} %last_sums.1.sums_ref), channel_id=1, source_target_pairs={{0,128},{128,0},{1,129},{129,1},{2,130},{130,2},{3,131},{131,3},{4... | collective-permute-start | bytes 3080 | tf_op jit(solution)/shard_map/ppermute | solution.py:24
  153.3 1.8 %finish.1 = bf16[128,128]{1,0:T(8,128)(2,1)} custom-call(bf16[8,128,128]{2,1,0:T(8,128)(2,1)} %all_to_all.16.total_ref, bf16[128,128]{1,0:T(8,128)(2,1)} %hidden_ref.3, f32[1,128]{1,0:T(1,128)} %bitcast.21, f32[112,1]{1,0:T(8,128)} %copy-done.2), custom_call_target="tpu_custom_call" | custom-call | tf_op jit(solution)/shard_map/finish/pallas_call | solution.py:657
  155.1 0.6 copy-done.5
  155.7 1.2 last.1
  (38 shorter events, 0.2 us)
Async XLA Ops:
  0.6 23.7 %collective-permute-start = (bf16[512,4096]{1,0:T(8,128)(2,1)}, bf16[512,4096]{1,0:T(8,128)(2,1)}, u32[]{:S(2)}, u32[]{:S(2)}) collective-permute-start(bf16[512,4096]{1,0:T(8,128)(2,1)} %w0_ref.5), channel_id=1, source_target_pairs={{0,128},{128,0},{1,129},{129,1},{2,130},{130,2},{3,131},{131,3},{4... | collective-permute-start | bytes 12582920 | tf_op jit(solution)/shard_map/ppermute | solution.py:24
  5.5 18.8 %all-to-all-start = ((bf16[8,128,128]{2,1,0:T(8,128)(2,1)}), bf16[8,128,128]{2,1,0:T(8,128)(2,1)S(1)}, u32[]{:S(2)}, u32[]{:S(2)}) async-start(bf16[8,128,128]{2,1,0:T(8,128)(2,1)} %get-tuple-element.78), calls=%async_computation | async-start | bytes 524288 | tf_op jit(solution)/shard_map/all_to_all | solution.py:680
  11.9 1.3 collective-permute-start.1
  24.4 8.9 %collective-permute-start.10 = (bf16[464,128]{1,0:T(8,128)(2,1)S(1)}, bf16[464,128]{1,0:T(8,128)(2,1)S(1)}, u32[]{:S(2)}, u32[]{:S(2)}) collective-permute-start(bf16[464,128]{1,0:T(8,128)(2,1)S(1)} %pad_maximum_fusion.2.refs_0_), channel_id=1, source_target_pairs={{0,3},{1,0},{2,1},{3,2},{128,129},{129,130},{130,131},{131,128},{4... | collective-permute-start | bytes 356360 | tf_op jit(solution)/shard_map/ppermute | solution.py:30
  25.6 8.7 %collective-permute-start.9 = (bf16[464,128]{1,0:T(8,128)(2,1)S(1)}, bf16[464,128]{1,0:T(8,128)(2,1)S(1)}, u32[]{:S(2)}, u32[]{:S(2)}) collective-permute-start(bf16[464,128]{1,0:T(8,128)(2,1)S(1)} %pad_maximum_fusion.2.refs_0_), channel_id=1, source_target_pairs={{0,2},{1,3},{2,0},{3,1},{128,130},{129,131},{130,128},{131,129},{4... | collective-permute-start | bytes 356360 | tf_op jit(solution)/shard_map/ppermute | solution.py:30
  28.1 6.3 %collective-permute-start.8 = (bf16[464,128]{1,0:T(8,128)(2,1)S(1)}, bf16[464,128]{1,0:T(8,128)(2,1)S(1)}, u32[]{:S(2)}, u32[]{:S(2)}) collective-permute-start(bf16[464,128]{1,0:T(8,128)(2,1)S(1)} %pad_maximum_fusion.2.refs_0_), channel_id=1, source_target_pairs={{0,1},{1,2},{2,3},{3,0},{128,131},{129,128},{130,129},{131,130},{4... | collective-permute-start | bytes 356360 | tf_op jit(solution)/shard_map/ppermute | solution.py:30
  29.3 6.8 %collective-permute-start.4 = (bf16[480,128]{1,0:T(8,128)(2,1)S(1)}, bf16[480,128]{1,0:T(8,128)(2,1)S(1)}, u32[]{:S(2)}, u32[]{:S(2)}) collective-permute-start(bf16[480,128]{1,0:T(8,128)(2,1)S(1)} %fusion.1.refs_4_), channel_id=1, source_target_pairs={{0,12},{4,0},{8,4},{12,8},{128,132},{132,136},{136,140},{140,128},... | collective-permute-start | bytes 368648 | tf_op jit(solution)/shard_map/ppermute | solution.py:30
  30.7 6.2 %collective-permute-start.3 = (bf16[480,128]{1,0:T(8,128)(2,1)S(1)}, bf16[480,128]{1,0:T(8,128)(2,1)S(1)}, u32[]{:S(2)}, u32[]{:S(2)}) collective-permute-start(bf16[480,128]{1,0:T(8,128)(2,1)S(1)} %fusion.1.refs_4_), channel_id=1, source_target_pairs={{0,8},{4,12},{8,0},{12,4},{128,136},{132,140},{136,128},{140,132},... | collective-permute-start | bytes 368648 | tf_op jit(solution)/shard_map/ppermute | solution.py:30
  33.3 5.1 %collective-permute-start.2 = (bf16[480,128]{1,0:T(8,128)(2,1)S(1)}, bf16[480,128]{1,0:T(8,128)(2,1)S(1)}, u32[]{:S(2)}, u32[]{:S(2)}) collective-permute-start(bf16[480,128]{1,0:T(8,128)(2,1)S(1)} %fusion.1.refs_4_), channel_id=1, source_target_pairs={{0,4},{4,8},{8,12},{12,0},{128,140},{132,128},{136,132},{140,136},... | collective-permute-start | bytes 368648 | tf_op jit(solution)/shard_map/ppermute | solution.py:30
  34.5 8.7 %collective-permute-start.11 = (bf16[1792,128]{1,0:T(8,128)(2,1)S(1)}, bf16[1792,128]{1,0:T(8,128)(2,1)S(1)}, u32[]{:S(2)}, u32[]{:S(2)}) collective-permute-start(bf16[1792,128]{1,0:T(8,128)(2,1)S(1)} %pad_maximum_fusion.1.refs_4_), channel_id=1, source_target_pairs={{0,4},{4,8},{8,12},{12,0},{128,140},{132,128},{136,132},{140,136},... | collective-permute-start | bytes 1376264 | tf_op jit(solution)/shard_map/ppermute | solution.py:30
  38.4 8.2 %collective-permute-start.5 = (bf16[1792,128]{1,0:T(8,128)(2,1)S(1)}, bf16[1792,128]{1,0:T(8,128)(2,1)S(1)}, u32[]{:S(2)}, u32[]{:S(2)}) collective-permute-start(bf16[1792,128]{1,0:T(8,128)(2,1)S(1)} %pad_maximum_fusion.refs_0_), channel_id=1, source_target_pairs={{0,1},{1,2},{2,3},{3,0},{128,131},{129,128},{130,129},{131,130},{4... | collective-permute-start | bytes 1376264 | tf_op jit(solution)/shard_map/ppermute | solution.py:30
  39.7 11.2 %collective-permute-start.12 = (bf16[1792,128]{1,0:T(8,128)(2,1)S(1)}, bf16[1792,128]{1,0:T(8,128)(2,1)S(1)}, u32[]{:S(2)}, u32[]{:S(2)}) collective-permute-start(bf16[1792,128]{1,0:T(8,128)(2,1)S(1)} %pad_maximum_fusion.1.refs_4_), channel_id=1, source_target_pairs={{0,12},{4,0},{8,4},{12,8},{128,132},{132,136},{136,140},{140,128},... | collective-permute-start | bytes 1376264 | tf_op jit(solution)/shard_map/ppermute | solution.py:30
  39.7 12.7 %collective-permute-start.6 = (bf16[1792,128]{1,0:T(8,128)(2,1)S(1)}, bf16[1792,128]{1,0:T(8,128)(2,1)}, u32[]{:S(2)}, u32[]{:S(2)}) collective-permute-start(bf16[1792,128]{1,0:T(8,128)(2,1)S(1)} %pad_maximum_fusion.refs_0_), channel_id=1, source_target_pairs={{0,3},{1,0},{2,1},{3,2},{128,129},{129,130},{130,131},{131,128},{4... | collective-permute-start | bytes 1376264 | tf_op jit(solution)/shard_map/ppermute | solution.py:30
  43.2 12.0 %collective-permute-start.13 = (bf16[1792,128]{1,0:T(8,128)(2,1)S(1)}, bf16[1792,128]{1,0:T(8,128)(2,1)}, u32[]{:S(2)}, u32[]{:S(2)}) collective-permute-start(bf16[1792,128]{1,0:T(8,128)(2,1)S(1)} %collective-permute-done.11.refs_5_), channel_id=1, source_target_pairs={{0,4},{4,8},{8,12},{12,0},{128,140},{132,128},{136,132},{140,136},... | collective-permute-start | bytes 1376264 | tf_op jit(solution)/shard_map/ppermute | solution.py:30
  46.6 9.8 %collective-permute-start.7 = (bf16[1792,128]{1,0:T(8,128)(2,1)S(1)}, bf16[1792,128]{1,0:T(8,128)(2,1)}, u32[]{:S(2)}, u32[]{:S(2)}) collective-permute-start(bf16[1792,128]{1,0:T(8,128)(2,1)S(1)} %collective-permute-done.5.refs_1_), channel_id=1, source_target_pairs={{0,1},{1,2},{2,3},{3,0},{128,131},{129,128},{130,129},{131,130},{4... | collective-permute-start | bytes 1376264 | tf_op jit(solution)/shard_map/ppermute | solution.py:30
  48.6 2.2 %copy-start = (bf16[512,4096]{1,0:T(8,128)(2,1)S(1)}, bf16[512,4096]{1,0:T(8,128)(2,1)}, u32[]{:S(2)}) copy-start(bf16[512,4096]{1,0:T(8,128)(2,1)} %w0_ref.5) | copy-start | bytes 12582916
  50.8 5.6 %copy-start.1 = (bf16[512,4096]{1,0:T(8,128)(2,1)S(1)}, bf16[512,4096]{1,0:T(8,128)(2,1)}, u32[]{:S(2)}) copy-start(bf16[512,4096]{1,0:T(8,128)(2,1)} %w0_ref.5) | copy-start | bytes 12582916
  50.9 5.5 %copy-start.4 = (f32[1,128]{1,0:T(1,128)}, f32[1,128]{1,0:T(1,128)S(1)}, u32[]{:S(2)}) copy-start(f32[1,128]{1,0:T(1,128)S(1)} %get-tuple-element.148.total_ref) | copy-start | bytes 1540
  64.7 24.4 %copy-start.2 = (f32[112,1]{1,0:T(8,128)}, f32[112,1]{1,0:T(8,128)S(1)}, u32[]{:S(2)}) copy-start(f32[112,1]{1,0:T(8,128)S(1)} %get-tuple-element.145.inv_ref) | copy-start | bytes 1348
  89.1 7.0 %copy-start.3 = (f32[1,128]{1,0:T(1,128)}, f32[1,128]{1,0:T(1,128)S(1)}, u32[]{:S(2)}) copy-start(f32[1,128]{1,0:T(1,128)S(1)} %get-tuple-element.102.loss_ref) | copy-start | bytes 1540
  89.1 8.0 %collective-permute-start.14 = (bf16[1808,128]{1,0:T(8,128)(2,1)S(1)}, bf16[1808,128]{1,0:T(8,128)(2,1)S(1)}, u32[]{:S(2)}, u32[]{:S(2)}) collective-permute-start(bf16[1808,128]{1,0:T(8,128)(2,1)S(1)} %get-tuple-element.113), channel_id=1, source_target_pairs={{0,1},{1,2},{2,3},{3,0},{128,131},{129,128},{130,129},{131,130},{4... | collective-permute-start | bytes 1388552 | tf_op jit(solution)/shard_map/ppermute | solution.py:30
  89.8 7.3 %collective-permute-start.15 = (bf16[1792,128]{1,0:T(8,128)(2,1)S(1)}, bf16[1792,128]{1,0:T(8,128)(2,1)S(1)}, u32[]{:S(2)}, u32[]{:S(2)}) collective-permute-start(bf16[1792,128]{1,0:T(8,128)(2,1)S(1)} %get-tuple-element.114), channel_id=1, source_target_pairs={{0,4},{4,8},{8,12},{12,0},{128,140},{132,128},{136,132},{140,136},... | collective-permute-start | bytes 1376264 | tf_op jit(solution)/shard_map/ppermute | solution.py:30
  97.2 16.1 %collective-permute-start.21 = (bf16[448,4608]{1,0:T(8,128)(2,1)S(1)}, bf16[448,4608]{1,0:T(8,128)(2,1)S(1)}, u32[]{:S(2)}, u32[]{:S(2)}) collective-permute-start(bf16[448,4608]{1,0:T(8,128)(2,1)S(1)} %get-tuple-element.129.n_ref), channel_id=1, source_target_pairs={{0,128},{128,0},{1,129},{129,1},{2,130},{130,2},{3,131},{131,3},{4... | collective-permute-start | bytes 12386312 | tf_op jit(solution)/shard_map/ppermute | solution.py:24
  106.8 15.5 %collective-permute-start.17 = (bf16[1872,128]{1,0:T(8,128)(2,1)S(1)}, bf16[1872,128]{1,0:T(8,128)(2,1)S(1)}, u32[]{:S(2)}, u32[]{:S(2)}) collective-permute-start(bf16[1872,128]{1,0:T(8,128)(2,1)S(1)} %get-tuple-element.124), channel_id=1, source_target_pairs={{0,1},{1,2},{2,3},{3,0},{128,131},{129,128},{130,129},{131,130},{4... | collective-permute-start | bytes 1437704 | tf_op jit(solution)/shard_map/ppermute | solution.py:30
  109.5 12.8 %collective-permute-start.18 = (bf16[1872,128]{1,0:T(8,128)(2,1)S(1)}, bf16[1872,128]{1,0:T(8,128)(2,1)S(1)}, u32[]{:S(2)}, u32[]{:S(2)}) collective-permute-start(bf16[1872,128]{1,0:T(8,128)(2,1)S(1)} %get-tuple-element.125), channel_id=1, source_target_pairs={{0,3},{1,0},{2,1},{3,2},{128,129},{129,130},{130,131},{131,128},{4... | collective-permute-start | bytes 1437704 | tf_op jit(solution)/shard_map/ppermute | solution.py:30
  109.5 12.7 %collective-permute-start.19 = (bf16[1792,128]{1,0:T(8,128)(2,1)S(1)}, bf16[1792,128]{1,0:T(8,128)(2,1)S(1)}, u32[]{:S(2)}, u32[]{:S(2)}) collective-permute-start(bf16[1792,128]{1,0:T(8,128)(2,1)S(1)} %get-tuple-element.126), channel_id=1, source_target_pairs={{0,4},{4,8},{8,12},{12,0},{128,140},{132,128},{136,132},{140,136},... | collective-permute-start | bytes 1376264 | tf_op jit(solution)/shard_map/ppermute | solution.py:30
  109.5 12.7 %collective-permute-start.20 = (bf16[1792,128]{1,0:T(8,128)(2,1)S(1)}, bf16[1792,128]{1,0:T(8,128)(2,1)S(1)}, u32[]{:S(2)}, u32[]{:S(2)}) collective-permute-start(bf16[1792,128]{1,0:T(8,128)(2,1)S(1)} %get-tuple-element.127), channel_id=1, source_target_pairs={{0,12},{4,0},{8,4},{12,8},{128,132},{132,136},{136,140},{140,128},... | collective-permute-start | bytes 1376264 | tf_op jit(solution)/shard_map/ppermute | solution.py:30
  113.2 9.0 %collective-permute-start.16 = (f32[32,128]{1,0:T(8,128)S(1)}, f32[32,128]{1,0:T(8,128)S(1)}, u32[]{:S(2)}, u32[]{:S(2)}) collective-permute-start(f32[32,128]{1,0:T(8,128)S(1)} %get-tuple-element.122.mine), channel_id=1, source_target_pairs={{0,2},{1,3},{2,0},{3,1},{128,130},{129,131},{130,128},{131,129},{4... | collective-permute-start | bytes 49160 | tf_op jit(solution)/shard_map/ppermute | solution.py:30
  123.2 6.0 %collective-permute-start.25 = (bf16[448,128]{1,0:T(8,128)(2,1)S(1)}, bf16[448,128]{1,0:T(8,128)(2,1)S(1)}, u32[]{:S(2)}, u32[]{:S(2)}) collective-permute-start(bf16[448,128]{1,0:T(8,128)(2,1)S(1)} %get-tuple-element.142), channel_id=1, source_target_pairs={{0,3},{1,0},{2,1},{3,2},{128,129},{129,130},{130,131},{131,128},{4... | collective-permute-start | bytes 344072 | tf_op jit(solution)/shard_map/ppermute | solution.py:30
  124.8 9.0 %collective-permute-start.22 = (bf16[480,128]{1,0:T(8,128)(2,1)S(1)}, bf16[480,128]{1,0:T(8,128)(2,1)S(1)}, u32[]{:S(2)}, u32[]{:S(2)}) collective-permute-start(bf16[480,128]{1,0:T(8,128)(2,1)S(1)} %get-tuple-element.138), channel_id=1, source_target_pairs={{0,4},{4,8},{8,12},{12,0},{128,140},{132,128},{136,132},{140,136},... | collective-permute-start | bytes 368648 | tf_op jit(solution)/shard_map/ppermute | solution.py:30
  124.8 9.0 %collective-permute-start.23 = (bf16[480,128]{1,0:T(8,128)(2,1)S(1)}, bf16[480,128]{1,0:T(8,128)(2,1)S(1)}, u32[]{:S(2)}, u32[]{:S(2)}) collective-permute-start(bf16[480,128]{1,0:T(8,128)(2,1)S(1)} %get-tuple-element.139), channel_id=1, source_target_pairs={{0,8},{4,12},{8,0},{12,4},{128,136},{132,140},{136,128},{140,132},... | collective-permute-start | bytes 368648 | tf_op jit(solution)/shard_map/ppermute | solution.py:30
  125.8 8.0 %collective-permute-start.24 = (bf16[480,128]{1,0:T(8,128)(2,1)S(1)}, bf16[480,128]{1,0:T(8,128)(2,1)S(1)}, u32[]{:S(2)}, u32[]{:S(2)}) collective-permute-start(bf16[480,128]{1,0:T(8,128)(2,1)S(1)} %get-tuple-element.140), channel_id=1, source_target_pairs={{0,12},{4,0},{8,4},{12,8},{128,132},{132,136},{136,140},{140,128},... | collective-permute-start | bytes 368648 | tf_op jit(solution)/shard_map/ppermute | solution.py:30
  126.2 5.2 %collective-permute-start.26 = (bf16[448,128]{1,0:T(8,128)(2,1)S(1)}, bf16[448,128]{1,0:T(8,128)(2,1)S(1)}, u32[]{:S(2)}, u32[]{:S(2)}) collective-permute-start(bf16[448,128]{1,0:T(8,128)(2,1)S(1)} %get-tuple-element.143), channel_id=1, source_target_pairs={{0,2},{1,3},{2,0},{3,1},{128,130},{129,131},{130,128},{131,129},{4... | collective-permute-start | bytes 344072 | tf_op jit(solution)/shard_map/ppermute | solution.py:30
  129.2 4.6 %collective-permute-start.27 = (bf16[448,128]{1,0:T(8,128)(2,1)S(1)}, bf16[448,128]{1,0:T(8,128)(2,1)S(1)}, u32[]{:S(2)}, u32[]{:S(2)}) collective-permute-start(bf16[448,128]{1,0:T(8,128)(2,1)S(1)} %get-tuple-element.144), channel_id=1, source_target_pairs={{0,1},{1,2},{2,3},{3,0},{128,131},{129,128},{130,129},{131,130},{4... | collective-permute-start | bytes 344072 | tf_op jit(solution)/shard_map/ppermute | solution.py:30
  147.9 7.2 %collective-permute-start.28 = (f32[2,128]{1,0:T(2,128)}, f32[2,128]{1,0:T(2,128)S(1)}, u32[]{:S(2)}, u32[]{:S(2)}) collective-permute-start(f32[2,128]{1,0:T(2,128)} %last_sums.1.sums_ref), channel_id=1, source_target_pairs={{0,128},{128,0},{1,129},{129,1},{2,130},{130,2},{3,131},{131,3},{4... | collective-permute-start | bytes 3080 | tf_op jit(solution)/shard_map/ppermute | solution.py:24
  155.1 0.6 copy-start.5
